TPU v7x, 512 devices: a whole 4x4x16 slice. The times are simulated.
512 devices in a mesh: gx: 8 (over x, core), gy: 8 (over z_lo), gz: 8 (over z_hi, y).
Axes of the slice: x: 4, y: 4, z: 16 (z_hi: 2, z_lo: 8; z = z_hi * 8 + z_lo), core: 2. Of those that a mesh axis runs over, the one named last changes fastest.
Arguments:
- checkpoint: float32 [2, 7, 32, 128, 1024], P(None, None, 'gx', 'gy', 'gz'), may hold values from 0.02 to 0.3
- cotangent: float32 [2, 7, 32, 128, 1024], P(None, None, 'gx', 'gy', 'gz'), may hold values from -6 to 6
- reaction_rate: float32 [32, 128, 1024], P('gx', 'gy', 'gz'), may hold values from 0.2 to 2
- relax_time: float32 [2, 32, 128, 1024], P(None, 'gx', 'gy', 'gz'), may hold values from 0.6 to 1.8
Outputs:
- adjoint_state: float32 [2, 7, 32, 128, 1024], P(None, None, 'gx', 'gy', 'gz')
- grad_rate: float32 [32, 128, 1024], P('gx', 'gy', 'gz')
- grad_relax: float32 [2, 32, 128, 1024], P(None, 'gx', 'gy', 'gz')
All inputs are finite; a program needn't handle non-finite values.
Results may differ from a plain program's by a relative error of at most 0.00002.
Values sent between devices are 32-bit elements; how exact they have to be, the bound alone decides.
No kernel may reach another device: no remote copies, remote signals or barrier semaphores. Data moves between devices by JAX's collectives and lax.ppermute only.
A program may use at most 64 MiB of HBM per device.

v0:
```python
import jax
import jax.numpy as jnp
from jax import lax
from jax.sharding import PartitionSpec as P

WEIGHTS = (0.25, 0.125, 0.125, 0.125, 0.125, 0.125, 0.125)
OFFSETS = ((0, 0, 0), (1, 0, 0), (-1, 0, 0), (0, 1, 0), (0, -1, 0), (0, 0, 1), (0, 0, -1))


def extended(value, sides, width):
    for axis, dim in sides:
        count, length = (lax.axis_size(axis), value.shape[dim])
        up = [(i, (i + 1) % count) for i in range(count)]
        down = [(j, i) for i, j in up]
        last = lax.slice_in_dim(value, length - width, length, axis=dim)
        initial = lax.slice_in_dim(value, 0, width, axis=dim)
        before = lax.ppermute(last, axis, up)
        after = lax.ppermute(initial, axis, down)
        value = jnp.concatenate([before, value, after], axis=dim)
    return value


def collide(state, reaction_rate, relax_time):
    weight_row = jnp.asarray(WEIGHTS, state.dtype).reshape(1, 7, 1, 1, 1)
    density = jnp.sum(state, axis=1)
    reaction = reaction_rate * density[0] * density[1]
    source = jnp.stack([-reaction, reaction])
    inverse = 1.0 / relax_time
    balance = weight_row * density[:, None]
    return state - (state - balance) * inverse[:, None] + weight_row * source[:, None]


def adjoint_collide(upstream, state, reaction_rate, relax_time):
    weight_row = jnp.asarray(WEIGHTS, state.dtype).reshape(1, 7, 1, 1, 1)
    density = jnp.sum(state, axis=1)
    inverse = 1.0 / relax_time
    moments = jnp.sum(weight_row * upstream, axis=1)
    contrast = moments[1] - moments[0]
    coupling = jnp.stack(
        [reaction_rate * density[1] * contrast, reaction_rate * density[0] * contrast]
    )
    earlier = (1.0 - inverse)[:, None] * upstream + (moments * inverse + coupling)[:, None]
    rate_part = density[0] * density[1] * contrast
    balance = weight_row * density[:, None]
    relax_part = jnp.sum(upstream * (state - balance), axis=1) * inverse * inverse
    return (earlier, rate_part, relax_part)


def stream_rim(stack, directions):
    padded = extended(stack, (("gx", 3), ("gy", 4), ("gz", 5)), 1)
    size_x, size_y, size_z = (stack.shape[3], stack.shape[4], stack.shape[5])
    moved = []
    for index in range(7):
        shift_x = OFFSETS[index][0] * directions[0]
        shift_y = OFFSETS[index][1] * directions[0]
        shift_z = OFFSETS[index][2] * directions[0]
        moved.append(
            padded[
                0,
                :,
                index,
                1 - shift_x : 1 - shift_x + size_x,
                1 - shift_y : 1 - shift_y + size_y,
                1 - shift_z : 1 - shift_z + size_z,
            ]
        )
    results = [jnp.stack(moved, axis=1)]
    return results


def stream_many(stack, directions):
    return stream_rim(stack, directions)


def on_device(checkpoint, cotangent, reaction_rate, relax_time):
    collided = collide(checkpoint, reaction_rate, relax_time)
    middle = stream_many(collided[None], (1,))[0]
    upstream = stream_many(cotangent[None], (-1,))[0]
    later, rate_late, relax_late = adjoint_collide(upstream, middle, reaction_rate, relax_time)
    upstream = stream_many(later[None], (-1,))[0]
    adjoint_state, rate_early, relax_early = adjoint_collide(
        upstream, checkpoint, reaction_rate, relax_time
    )
    return (adjoint_state, rate_late + rate_early, relax_late + relax_early)


def solution(mesh):
    placed = (
        P(None, None, "gx", "gy", "gz"),
        P(None, None, "gx", "gy", "gz"),
        P("gx", "gy", "gz"),
        P(None, "gx", "gy", "gz"),
    )
    return jax.shard_map(
        on_device,
        mesh=mesh,
        in_specs=placed,
        out_specs=(P(None, None, "gx", "gy", "gz"), P("gx", "gy", "gz"), P(None, "gx", "gy", "gz")),
        check_vma=False,
    )
```

profile of v0, /device:TPU:6, one launch (start us, length us, event | category | flops | bytes accessed | tf_op | source)
XLA Modules:
  0.0 152.7 jit_solution(7000950803430103531)
XLA Ops:
  0.6 1.1 reduce_sum.106
  1.8 0.8 copy-done.10
  3.5 1.7 %collective-permute-start.7 = (f32[1,2,7,1,16,128]{5,4,3,2,1,0:T(8,128)S(1)}, f32[1,2,7,1,16,128]{5,4,3,2,1,0:T(8,128)S(1)}, u32[]{:S(2)}, u32[]{:S(2)}) collective-permute-start(f32[1,2,7,1,16,128]{5,4,3,2,1,0:T(8,128)S(1)} %get-tuple-element.60), channel_id=1, source_target_pairs={{64,0},{128,64},{192,128},{256,192},{320,256},{384,320},{448,384},... | collective-permute-start | bytes 344072 | tf_op jit(solution)/shard_map/ppermute | solution.py:18
  5.4 4.2 %collective-permute-start.1 = (f32[1,2,7,1,16,128]{5,4,3,2,1,0:T(8,128)S(1)}, f32[1,2,7,1,16,128]{5,4,3,2,1,0:T(8,128)S(1)}, u32[]{:S(2)}, u32[]{:S(2)}) collective-permute-start(f32[1,2,7,1,16,128]{5,4,3,2,1,0:T(8,128)S(1)} %copy.411), channel_id=1, source_target_pairs={{0,64},{64,128},{128,192},{192,256},{256,320},{320,384},{384,448},... | collective-permute-start | bytes 344072 | tf_op jit(solution)/shard_map/ppermute | solution.py:17
  10.4 1.9 %collective-permute-start.8 = (f32[1,2,7,6,1,128]{5,1,4,3,2,0:T(2,128)S(1)}, f32[1,2,7,6,1,128]{5,1,4,3,2,0:T(2,128)S(1)}, u32[]{:S(2)}, u32[]{:S(2)}) collective-permute-start(f32[1,2,7,6,1,128]{5,1,4,3,2,0:T(2,128)S(1)} %copy.433), channel_id=1, source_target_pairs={{0,8},{8,16},{16,24},{24,32},{32,40},{40,48},{48,56},{56,0},{1,9},... | collective-permute-start | bytes 129032 | tf_op jit(solution)/shard_map/ppermute | solution.py:17
  12.4 10.6 %collective-permute-start.9 = (f32[1,2,7,6,1,128]{5,1,4,3,2,0:T(2,128)S(1)}, f32[1,2,7,6,1,128]{5,1,4,3,2,0:T(2,128)S(1)}, u32[]{:S(2)}, u32[]{:S(2)}) collective-permute-start(f32[1,2,7,6,1,128]{5,1,4,3,2,0:T(2,128)S(1)} %copy.436), channel_id=1, source_target_pairs={{8,0},{16,8},{24,16},{32,24},{40,32},{48,40},{56,48},{0,56},{9,1},... | collective-permute-start | bytes 129032 | tf_op jit(solution)/shard_map/ppermute | solution.py:18
  23.1 3.9 %collective-permute-start.2 = (f32[1,2,7,6,1,128]{5,1,4,3,2,0:T(2,128)S(1)}, f32[1,2,7,6,1,128]{5,1,4,3,2,0:T(2,128)S(1)}, u32[]{:S(2)}, u32[]{:S(2)}) collective-permute-start(f32[1,2,7,6,1,128]{5,1,4,3,2,0:T(2,128)S(1)} %copy.415), channel_id=1, source_target_pairs={{8,0},{16,8},{24,16},{32,24},{40,32},{48,40},{56,48},{0,56},{9,1},... | collective-permute-start | bytes 129032 | tf_op jit(solution)/shard_map/ppermute | solution.py:18
  27.7 1.9 %collective-permute-start.3 = (f32[1,2,7,6,1,128]{5,1,4,3,2,0:T(2,128)}, f32[1,2,7,6,1,128]{5,1,4,3,2,0:T(2,128)}, u32[]{:S(2)}, u32[]{:S(2)}) collective-permute-start(f32[1,2,7,6,1,128]{5,1,4,3,2,0:T(2,128)} %copy.417), channel_id=1, source_target_pairs={{0,8},{8,16},{16,24},{24,32},{32,40},{40,48},{48,56},{56,0},{1,9},... | collective-permute-start | bytes 129032 | tf_op jit(solution)/shard_map/ppermute | solution.py:17
  29.8 0.8 copy-done.5
  30.5 0.8 copy-done.3
  31.6 1.3 fusion.23
  32.9 2.4 %copy.441 = f32[1,2,7,6,18,1]{4,1,5,3,2,0:T(2,128)} copy(f32[1,2,7,6,18,1]{5,4,3,2,1,0:T(8,128)} %get-tuple-element.49) | data formatting | bytes 12096 | tf_op jit(solution)/shard_map/slice | solution.py:15
  35.4 3.5 %collective-permute-start.10 = (f32[1,2,7,6,18,1]{4,1,5,3,2,0:T(2,128)}, f32[1,2,7,6,18,1]{4,1,5,3,2,0:T(2,128)}, u32[]{:S(2)}, u32[]{:S(2)}) collective-permute-start(f32[1,2,7,6,18,1]{4,1,5,3,2,0:T(2,128)} %copy.441), channel_id=1, source_target_pairs={{0,1},{1,2},{2,3},{3,4},{4,5},{5,6},{6,7},{7,0},{8,9},{9,10},{10,1... | collective-permute-start | bytes 18152 | tf_op jit(solution)/shard_map/ppermute | solution.py:17
  38.8 1.2 copy.444
  40.0 14.0 %collective-permute-start.11 = (f32[1,2,7,6,18,1]{4,1,5,3,2,0:T(2,128)}, f32[1,2,7,6,18,1]{4,1,5,3,2,0:T(2,128)}, u32[]{:S(2)}, u32[]{:S(2)}) collective-permute-start(f32[1,2,7,6,18,1]{4,1,5,3,2,0:T(2,128)} %copy.444), channel_id=1, source_target_pairs={{1,0},{2,1},{3,2},{4,3},{5,4},{6,5},{7,6},{0,7},{9,8},{10,9},{11,1... | collective-permute-start | bytes 18152 | tf_op jit(solution)/shard_map/ppermute | solution.py:18
  54.1 0.8 copy.418
  55.1 1.3 fusion.24
  56.4 2.4 %copy.421 = f32[1,2,7,6,18,1]{4,1,5,3,2,0:T(2,128)} copy(f32[1,2,7,6,18,1]{5,4,3,1,2,0:T(8,128)} %get-tuple-element.51) | data formatting | bytes 12096 | tf_op jit(solution)/shard_map/slice | solution.py:16
  58.8 3.9 %collective-permute-start.4 = (f32[1,2,7,6,18,1]{4,1,5,3,2,0:T(2,128)}, f32[1,2,7,6,18,1]{4,1,5,3,2,0:T(2,128)}, u32[]{:S(2)}, u32[]{:S(2)}) collective-permute-start(f32[1,2,7,6,18,1]{4,1,5,3,2,0:T(2,128)} %copy.421), channel_id=1, source_target_pairs={{1,0},{2,1},{3,2},{4,3},{5,4},{6,5},{7,6},{0,7},{9,8},{10,9},{11,1... | collective-permute-start | bytes 18152 | tf_op jit(solution)/shard_map/ppermute | solution.py:18
  62.7 1.2 copy.423
  63.9 1.9 %collective-permute-start.5 = (f32[1,2,7,6,18,1]{4,1,5,3,2,0:T(2,128)}, f32[1,2,7,6,18,1]{4,1,5,3,2,0:T(2,128)}, u32[]{:S(2)}, u32[]{:S(2)}) collective-permute-start(f32[1,2,7,6,18,1]{4,1,5,3,2,0:T(2,128)} %copy.423), channel_id=1, source_target_pairs={{0,1},{1,2},{2,3},{3,4},{4,5},{5,6},{6,7},{7,0},{8,9},{9,10},{10,1... | collective-permute-start | bytes 18152 | tf_op jit(solution)/shard_map/ppermute | solution.py:17
  69.8 2.4 %copy.442 = f32[1,2,7,6,18,1]{5,4,3,1,2,0:T(8,128)} copy(f32[1,2,7,6,18,1]{4,1,5,3,2,0:T(2,128)} %collective-permute-done.10) | data formatting | bytes 12096 | tf_op jit(solution)/shard_map/ppermute | solution.py:17
  72.2 1.4 copy.445
  73.6 1.6 %bitcast_dynamic-update-slice_fusion.4 = (f32[2,7,4,16,128]{4,3,2,0,1:T(8,128)}, f32[1,2,1,4,16,128]{5,4,3,1,2,0:T(8,128)S(1)}) fusion(f32[2,7,4,16,128]{4,3,2,0,1:T(8,128)} %get-tuple-element.26, f32[1,2,7,6,18,1]{5,4,3,1,2,0:T(8,128)} %copy.442, f32[1,2,7,6,1,128]{5,4,3,2,1,0:T(1,128)S(1)} %copy.440, ...), kind=kLoop, calls=%fused_computation.87 | loop fusion | flops 790528 | bytes 1937408
  75.2 0.7 bitcast_dynamic-update-slice_fusion.3
  76.1 2.4 %copy.422 = f32[1,2,7,6,18,1]{5,4,3,1,2,0:T(8,128)} copy(f32[1,2,7,6,18,1]{4,1,5,3,2,0:T(2,128)} %collective-permute-done.4) | data formatting | bytes 12096 | tf_op jit(solution)/shard_map/ppermute | solution.py:18
  78.5 4.3 %collective-permute-done.5 = f32[1,2,7,6,18,1]{4,1,5,3,2,0:T(2,128)} collective-permute-done((f32[1,2,7,6,18,1]{4,1,5,3,2,0:T(2,128)}, f32[1,2,7,6,18,1]{4,1,5,3,2,0:T(2,128)}, u32[]{:S(2)}, u32[]{:S(2)}) %collective-permute-start.5) | collective-permute-done | bytes 6080 | tf_op jit(solution)/shard_map/ppermute | solution.py:17
  82.8 1.4 copy.424
  84.2 1.6 %bitcast_dynamic-update-slice_fusion.8 = (f32[2,7,4,16,128]{4,3,2,0,1:T(8,128)}, f32[1,2,1,4,16,128]{5,4,3,1,2,0:T(8,128)S(1)}) fusion(f32[2,7,4,16,128]{4,3,2,0,1:T(8,128)} %get-tuple-element.38, f32[1,2,7,6,18,1]{5,4,3,1,2,0:T(8,128)} %copy.422, f32[1,2,7,6,1,128]{5,4,3,1,2,0:T(1,128)S(1)} %copy.416, f32[1,2,7,4,16,128]{5,4,3,1,2,0:T(8,128)S(1)} %bitcast.171, ...), kind=kLoop, calls=%fused_computation.91 | loop fusion | flops 81920 | bytes 1937408
  85.9 0.7 bitcast_dynamic-update-slice_fusion.7
  86.9 1.8 %multiply_reduce_fusion.1 = (f32[2,4,16,128]{3,2,1,0:T(8,128)}, f32[2,4,16,128]{3,2,1,0:T(8,128)S(1)}) fusion(f32[2,7,4,16,128]{4,3,2,0,1:T(8,128)} %get-tuple-element.34, f32[2,7,4,16,128]{4,3,2,0,1:T(8,128)S(1)} %copy-done.4, f32[7]{0:T(128)S(1)} %copy-done.16, f32[2,4,16,128]{3,2,1,0:T(8,128)S(1)} %bitcast.173), kind=kLoop, calls=%fused_computation.6 | loop fusion | flops 655360 | bytes 1114140 | tf_op jit(solution)/shard_map/reduce_sum | solution.py:45
  88.8 1.0 copy-done.6
  90.5 2.1 %collective-permute-done.12 = f32[1,2,7,1,16,128]{5,4,3,2,1,0:T(8,128)S(1)} collective-permute-done((f32[1,2,7,1,16,128]{5,4,3,2,1,0:T(8,128)S(1)}, f32[1,2,7,1,16,128]{5,4,3,2,1,0:T(8,128)S(1)}, u32[]{:S(2)}, u32[]{:S(2)}) %collective-permute-start.12) | collective-permute-done | bytes 114720 | tf_op jit(solution)/shard_map/ppermute | solution.py:18
  92.5 1.9 %collective-permute-done.13 = f32[1,2,7,1,16,128]{5,4,3,2,1,0:T(8,128)S(1)} collective-permute-done((f32[1,2,7,1,16,128]{5,4,3,2,1,0:T(8,128)S(1)}, f32[1,2,7,1,16,128]{5,4,3,2,1,0:T(8,128)S(1)}, u32[]{:S(2)}, u32[]{:S(2)}) %collective-permute-start.13) | collective-permute-done | bytes 114720 | tf_op jit(solution)/shard_map/ppermute | solution.py:17
  94.5 6.5 %collective-permute-start.14 = (f32[1,2,7,6,1,128]{5,1,4,3,2,0:T(2,128)S(1)}, f32[1,2,7,6,1,128]{5,1,4,3,2,0:T(2,128)S(1)}, u32[]{:S(2)}, u32[]{:S(2)}) collective-permute-start(f32[1,2,7,6,1,128]{5,1,4,3,2,0:T(2,128)S(1)} %copy.456), channel_id=1, source_target_pairs={{8,0},{16,8},{24,16},{32,24},{40,32},{48,40},{56,48},{0,56},{9,1},... | collective-permute-start | bytes 129032 | tf_op jit(solution)/shard_map/ppermute | solution.py:18
  101.0 1.9 %collective-permute-start.15 = (f32[1,2,7,6,1,128]{5,1,4,3,2,0:T(2,128)S(1)}, f32[1,2,7,6,1,128]{5,1,4,3,2,0:T(2,128)S(1)}, u32[]{:S(2)}, u32[]{:S(2)}) collective-permute-start(f32[1,2,7,6,1,128]{5,1,4,3,2,0:T(2,128)S(1)} %copy.458), channel_id=1, source_target_pairs={{0,8},{8,16},{16,24},{24,32},{32,40},{40,48},{48,56},{56,0},{1,9},... | collective-permute-start | bytes 129032 | tf_op jit(solution)/shard_map/ppermute | solution.py:17
  103.0 10.5 %collective-permute-done.15 = f32[1,2,7,6,1,128]{5,1,4,3,2,0:T(2,128)S(1)} collective-permute-done((f32[1,2,7,6,1,128]{5,1,4,3,2,0:T(2,128)S(1)}, f32[1,2,7,6,1,128]{5,1,4,3,2,0:T(2,128)S(1)}, u32[]{:S(2)}, u32[]{:S(2)}) %collective-permute-start.15) | collective-permute-done | bytes 43040 | tf_op jit(solution)/shard_map/ppermute | solution.py:17
  114.1 1.2 copy.462
  115.3 12.7 %collective-permute-start.16 = (f32[1,2,7,6,18,1]{4,1,5,3,2,0:T(2,128)}, f32[1,2,7,6,18,1]{4,1,5,3,2,0:T(2,128)}, u32[]{:S(2)}, u32[]{:S(2)}) collective-permute-start(f32[1,2,7,6,18,1]{4,1,5,3,2,0:T(2,128)} %copy.462), channel_id=1, source_target_pairs={{1,0},{2,1},{3,2},{4,3},{5,4},{6,5},{7,6},{0,7},{9,8},{10,9},{11,1... | collective-permute-start | bytes 18152 | tf_op jit(solution)/shard_map/ppermute | solution.py:18
  128.0 1.2 copy.464
  129.2 1.9 %collective-permute-start.17 = (f32[1,2,7,6,18,1]{4,1,5,3,2,0:T(2,128)}, f32[1,2,7,6,18,1]{4,1,5,3,2,0:T(2,128)}, u32[]{:S(2)}, u32[]{:S(2)}) collective-permute-start(f32[1,2,7,6,18,1]{4,1,5,3,2,0:T(2,128)} %copy.464), channel_id=1, source_target_pairs={{0,1},{1,2},{2,3},{3,4},{4,5},{5,6},{6,7},{7,0},{8,9},{9,10},{10,1... | collective-permute-start | bytes 18152 | tf_op jit(solution)/shard_map/ppermute | solution.py:17
  132.4 1.4 copy.463
  133.8 12.4 %collective-permute-done.17 = f32[1,2,7,6,18,1]{4,1,5,3,2,0:T(2,128)} collective-permute-done((f32[1,2,7,6,18,1]{4,1,5,3,2,0:T(2,128)}, f32[1,2,7,6,18,1]{4,1,5,3,2,0:T(2,128)}, u32[]{:S(2)}, u32[]{:S(2)}) %collective-permute-start.17) | collective-permute-done | bytes 6080 | tf_op jit(solution)/shard_map/ppermute | solution.py:17
  146.3 1.4 copy.465
  147.7 0.7 fusion.3
  148.4 0.7 fusion.1
  149.1 1.2 multiply_reduce_fusion
  151.9 0.8 multiply_add_fusion
  (107 shorter events, 11.7 us)
Async XLA Ops:
  0.6 2.0 %copy-start = (f32[2,7,4,16,128]{4,3,2,1,0:T(8,128)S(1)}, f32[2,7,4,16,128]{4,3,2,1,0:T(8,128)}, u32[]{:S(2)}) copy-start(f32[2,7,4,16,128]{4,3,2,1,0:T(8,128)} %param.7) | copy-start | bytes 1376260
  0.6 1.1 copy-start.13
  1.8 0.8 copy-start.10
  2.6 0.7 copy-start.16
  3.5 1.8 %copy-start.12 = (f32[2,7,4,16,128]{4,3,2,1,0:T(8,128)S(1)}, f32[2,7,4,16,128]{4,3,2,1,0:T(8,128)}, u32[]{:S(2)}) copy-start(f32[2,7,4,16,128]{4,3,2,1,0:T(8,128)} %param.8) | copy-start | bytes 1376260
  3.5 6.1 %collective-permute-start.6 = (f32[1,2,7,1,16,128]{5,4,3,2,1,0:T(8,128)S(1)}, f32[1,2,7,1,16,128]{5,4,3,2,1,0:T(8,128)S(1)}, u32[]{:S(2)}, u32[]{:S(2)}) collective-permute-start(f32[1,2,7,1,16,128]{5,4,3,2,1,0:T(8,128)S(1)} %get-tuple-element.61), channel_id=1, source_target_pairs={{0,64},{64,128},{128,192},{192,256},{256,320},{320,384},{384,448},... | collective-permute-start | bytes 344072 | tf_op jit(solution)/shard_map/ppermute | solution.py:17
  3.5 6.8 %collective-permute-start.7 = (f32[1,2,7,1,16,128]{5,4,3,2,1,0:T(8,128)S(1)}, f32[1,2,7,1,16,128]{5,4,3,2,1,0:T(8,128)S(1)}, u32[]{:S(2)}, u32[]{:S(2)}) collective-permute-start(f32[1,2,7,1,16,128]{5,4,3,2,1,0:T(8,128)S(1)} %get-tuple-element.60), channel_id=1, source_target_pairs={{64,0},{128,64},{192,128},{256,192},{320,256},{384,320},{448,384},... | collective-permute-start | bytes 344072 | tf_op jit(solution)/shard_map/ppermute | solution.py:18
  5.3 17.7 %collective-permute-start = (f32[1,2,7,1,16,128]{5,4,3,2,1,0:T(8,128)S(1)}, f32[1,2,7,1,16,128]{5,4,3,2,1,0:T(8,128)S(1)}, u32[]{:S(2)}, u32[]{:S(2)}) collective-permute-start(f32[1,2,7,1,16,128]{5,4,3,2,1,0:T(8,128)S(1)} %copy.409), channel_id=1, source_target_pairs={{64,0},{128,64},{192,128},{256,192},{320,256},{384,320},{448,384},... | collective-permute-start | bytes 344072 | tf_op jit(solution)/shard_map/ppermute | solution.py:18
  5.4 17.7 %collective-permute-start.1 = (f32[1,2,7,1,16,128]{5,4,3,2,1,0:T(8,128)S(1)}, f32[1,2,7,1,16,128]{5,4,3,2,1,0:T(8,128)S(1)}, u32[]{:S(2)}, u32[]{:S(2)}) collective-permute-start(f32[1,2,7,1,16,128]{5,4,3,2,1,0:T(8,128)S(1)} %copy.411), channel_id=1, source_target_pairs={{0,64},{64,128},{128,192},{192,256},{256,320},{320,384},{384,448},... | collective-permute-start | bytes 344072 | tf_op jit(solution)/shard_map/ppermute | solution.py:17
  10.4 20.9 %collective-permute-start.8 = (f32[1,2,7,6,1,128]{5,1,4,3,2,0:T(2,128)S(1)}, f32[1,2,7,6,1,128]{5,1,4,3,2,0:T(2,128)S(1)}, u32[]{:S(2)}, u32[]{:S(2)}) collective-permute-start(f32[1,2,7,6,1,128]{5,1,4,3,2,0:T(2,128)S(1)} %copy.433), channel_id=1, source_target_pairs={{0,8},{8,16},{16,24},{24,32},{32,40},{40,48},{48,56},{56,0},{1,9},... | collective-permute-start | bytes 129032 | tf_op jit(solution)/shard_map/ppermute | solution.py:17
  12.4 19.0 %collective-permute-start.9 = (f32[1,2,7,6,1,128]{5,1,4,3,2,0:T(2,128)S(1)}, f32[1,2,7,6,1,128]{5,1,4,3,2,0:T(2,128)S(1)}, u32[]{:S(2)}, u32[]{:S(2)}) collective-permute-start(f32[1,2,7,6,1,128]{5,1,4,3,2,0:T(2,128)S(1)} %copy.436), channel_id=1, source_target_pairs={{8,0},{16,8},{24,16},{32,24},{40,32},{48,40},{56,48},{0,56},{9,1},... | collective-permute-start | bytes 129032 | tf_op jit(solution)/shard_map/ppermute | solution.py:18
  23.1 30.9 %collective-permute-start.2 = (f32[1,2,7,6,1,128]{5,1,4,3,2,0:T(2,128)S(1)}, f32[1,2,7,6,1,128]{5,1,4,3,2,0:T(2,128)S(1)}, u32[]{:S(2)}, u32[]{:S(2)}) collective-permute-start(f32[1,2,7,6,1,128]{5,1,4,3,2,0:T(2,128)S(1)} %copy.415), channel_id=1, source_target_pairs={{8,0},{16,8},{24,16},{32,24},{40,32},{48,40},{56,48},{0,56},{9,1},... | collective-permute-start | bytes 129032 | tf_op jit(solution)/shard_map/ppermute | solution.py:18
  27.7 26.4 %collective-permute-start.3 = (f32[1,2,7,6,1,128]{5,1,4,3,2,0:T(2,128)}, f32[1,2,7,6,1,128]{5,1,4,3,2,0:T(2,128)}, u32[]{:S(2)}, u32[]{:S(2)}) collective-permute-start(f32[1,2,7,6,1,128]{5,1,4,3,2,0:T(2,128)} %copy.417), channel_id=1, source_target_pairs={{0,8},{8,16},{16,24},{24,32},{32,40},{40,48},{48,56},{56,0},{1,9},... | collective-permute-start | bytes 129032 | tf_op jit(solution)/shard_map/ppermute | solution.py:17
  29.7 1.7 %copy-start.7 = (f32[2,7,4,16,128]{4,3,2,0,1:T(8,128)}, f32[2,7,4,16,128]{4,3,2,0,1:T(8,128)S(1)}, u32[]{:S(2)}) copy-start(f32[2,7,4,16,128]{4,3,2,0,1:T(8,128)S(1)} %get-tuple-element.42) | copy-start | bytes 1376260
  29.7 0.8 copy-start.5
  30.5 0.8 copy-start.3
  35.4 34.5 %collective-permute-start.10 = (f32[1,2,7,6,18,1]{4,1,5,3,2,0:T(2,128)}, f32[1,2,7,6,18,1]{4,1,5,3,2,0:T(2,128)}, u32[]{:S(2)}, u32[]{:S(2)}) collective-permute-start(f32[1,2,7,6,18,1]{4,1,5,3,2,0:T(2,128)} %copy.441), channel_id=1, source_target_pairs={{0,1},{1,2},{2,3},{3,4},{4,5},{5,6},{6,7},{7,0},{8,9},{9,10},{10,1... | collective-permute-start | bytes 18152 | tf_op jit(solution)/shard_map/ppermute | solution.py:17
  40.0 32.2 %collective-permute-start.11 = (f32[1,2,7,6,18,1]{4,1,5,3,2,0:T(2,128)}, f32[1,2,7,6,18,1]{4,1,5,3,2,0:T(2,128)}, u32[]{:S(2)}, u32[]{:S(2)}) collective-permute-start(f32[1,2,7,6,18,1]{4,1,5,3,2,0:T(2,128)} %copy.444), channel_id=1, source_target_pairs={{1,0},{2,1},{3,2},{4,3},{5,4},{6,5},{7,6},{0,7},{9,8},{10,9},{11,1... | collective-permute-start | bytes 18152 | tf_op jit(solution)/shard_map/ppermute | solution.py:18
  58.8 17.3 %collective-permute-start.4 = (f32[1,2,7,6,18,1]{4,1,5,3,2,0:T(2,128)}, f32[1,2,7,6,18,1]{4,1,5,3,2,0:T(2,128)}, u32[]{:S(2)}, u32[]{:S(2)}) collective-permute-start(f32[1,2,7,6,18,1]{4,1,5,3,2,0:T(2,128)} %copy.421), channel_id=1, source_target_pairs={{1,0},{2,1},{3,2},{4,3},{5,4},{6,5},{7,6},{0,7},{9,8},{10,9},{11,1... | collective-permute-start | bytes 18152 | tf_op jit(solution)/shard_map/ppermute | solution.py:18
  63.9 18.9 %collective-permute-start.5 = (f32[1,2,7,6,18,1]{4,1,5,3,2,0:T(2,128)}, f32[1,2,7,6,18,1]{4,1,5,3,2,0:T(2,128)}, u32[]{:S(2)}, u32[]{:S(2)}) collective-permute-start(f32[1,2,7,6,18,1]{4,1,5,3,2,0:T(2,128)} %copy.423), channel_id=1, source_target_pairs={{0,1},{1,2},{2,3},{3,4},{4,5},{5,6},{6,7},{7,0},{8,9},{9,10},{10,1... | collective-permute-start | bytes 18152 | tf_op jit(solution)/shard_map/ppermute | solution.py:17
  75.2 0.8 copy-start.15
  85.9 1.0 copy-start.4
  88.7 1.0 copy-start.6
  88.8 1.0 copy-start.8
  89.9 2.6 %collective-permute-start.12 = (f32[1,2,7,1,16,128]{5,4,3,2,1,0:T(8,128)S(1)}, f32[1,2,7,1,16,128]{5,4,3,2,1,0:T(8,128)S(1)}, u32[]{:S(2)}, u32[]{:S(2)}) collective-permute-start(f32[1,2,7,1,16,128]{5,4,3,2,1,0:T(8,128)S(1)} %copy.450), channel_id=1, source_target_pairs={{64,0},{128,64},{192,128},{256,192},{320,256},{384,320},{448,384},... | collective-permute-start | bytes 344072 | tf_op jit(solution)/shard_map/ppermute | solution.py:18
  90.2 4.2 %collective-permute-start.13 = (f32[1,2,7,1,16,128]{5,4,3,2,1,0:T(8,128)S(1)}, f32[1,2,7,1,16,128]{5,4,3,2,1,0:T(8,128)S(1)}, u32[]{:S(2)}, u32[]{:S(2)}) collective-permute-start(f32[1,2,7,1,16,128]{5,4,3,2,1,0:T(8,128)S(1)} %copy.452), channel_id=1, source_target_pairs={{0,64},{64,128},{128,192},{192,256},{256,320},{320,384},{384,448},... | collective-permute-start | bytes 344072 | tf_op jit(solution)/shard_map/ppermute | solution.py:17
  94.5 8.5 %collective-permute-start.14 = (f32[1,2,7,6,1,128]{5,1,4,3,2,0:T(2,128)S(1)}, f32[1,2,7,6,1,128]{5,1,4,3,2,0:T(2,128)S(1)}, u32[]{:S(2)}, u32[]{:S(2)}) collective-permute-start(f32[1,2,7,6,1,128]{5,1,4,3,2,0:T(2,128)S(1)} %copy.456), channel_id=1, source_target_pairs={{8,0},{16,8},{24,16},{32,24},{40,32},{48,40},{56,48},{0,56},{9,1},... | collective-permute-start | bytes 129032 | tf_op jit(solution)/shard_map/ppermute | solution.py:18
  101.0 12.5 %collective-permute-start.15 = (f32[1,2,7,6,1,128]{5,1,4,3,2,0:T(2,128)S(1)}, f32[1,2,7,6,1,128]{5,1,4,3,2,0:T(2,128)S(1)}, u32[]{:S(2)}, u32[]{:S(2)}) collective-permute-start(f32[1,2,7,6,1,128]{5,1,4,3,2,0:T(2,128)S(1)} %copy.458), channel_id=1, source_target_pairs={{0,8},{8,16},{16,24},{24,32},{32,40},{40,48},{48,56},{56,0},{1,9},... | collective-permute-start | bytes 129032 | tf_op jit(solution)/shard_map/ppermute | solution.py:17
  102.9 10.6 %copy-start.1 = (f32[2,7,4,16,128]{4,3,2,1,0:T(8,128)}, f32[2,7,4,16,128]{4,3,2,1,0:T(8,128)S(1)}, u32[]{:S(2)}) copy-start(f32[2,7,4,16,128]{4,3,2,1,0:T(8,128)S(1)} %fusion.9) | copy-start | bytes 1376260
  115.3 17.1 %collective-permute-start.16 = (f32[1,2,7,6,18,1]{4,1,5,3,2,0:T(2,128)}, f32[1,2,7,6,18,1]{4,1,5,3,2,0:T(2,128)}, u32[]{:S(2)}, u32[]{:S(2)}) collective-permute-start(f32[1,2,7,6,18,1]{4,1,5,3,2,0:T(2,128)} %copy.462), channel_id=1, source_target_pairs={{1,0},{2,1},{3,2},{4,3},{5,4},{6,5},{7,6},{0,7},{9,8},{10,9},{11,1... | collective-permute-start | bytes 18152 | tf_op jit(solution)/shard_map/ppermute | solution.py:18
  129.2 17.0 %collective-permute-start.17 = (f32[1,2,7,6,18,1]{4,1,5,3,2,0:T(2,128)}, f32[1,2,7,6,18,1]{4,1,5,3,2,0:T(2,128)}, u32[]{:S(2)}, u32[]{:S(2)}) collective-permute-start(f32[1,2,7,6,18,1]{4,1,5,3,2,0:T(2,128)} %copy.464), channel_id=1, source_target_pairs={{0,1},{1,2},{2,3},{3,4},{4,5},{5,6},{6,7},{7,0},{8,9},{9,10},{10,1... | collective-permute-start | bytes 18152 | tf_op jit(solution)/shard_map/ppermute | solution.py:17
  149.1 1.9 %copy-start.11 = (f32[2,4,16,128]{3,2,1,0:T(8,128)S(1)}, f32[2,4,16,128]{3,2,1,0:T(8,128)}, u32[]{:S(2)}) copy-start(f32[2,4,16,128]{3,2,1,0:T(8,128)} %param.10) | copy-start | bytes 196612
  149.1 1.9 %copy-start.14 = (f32[2,4,16,128]{3,2,1,0:T(8,128)S(1)}, f32[2,4,16,128]{3,2,1,0:T(8,128)}, u32[]{:S(2)}) copy-start(f32[2,4,16,128]{3,2,1,0:T(8,128)} %get-tuple-element.20) | copy-start | bytes 196612
  150.4 1.3 copy-start.2
  151.0 0.9 copy-start.9
where the time goes:
time: 154 us; the launch traced here: 153 us
  starting transfers between devices  71.1 us (46%)
  waiting for transfers between devices  31.8 us (21%)
  local copies, waits for them, and re-layouts  31.1 us (20%)
  other arithmetic  17.4 us (11%)
    ppermute x9, starting transfers between devices, extended(): after = lax.ppermute(initial, axis, down)  53.6 us
    ppermute x9, waiting for transfers between devices, extended(): before = lax.ppermute(last, axis, up)  29.1 us
    ppermute x9, starting transfers between devices, extended(): before = lax.ppermute(last, axis, up)  17.6 us
    unnamed x15, other arithmetic  7.93 us
    slice x12, local copies, waits for them, and re-layouts, extended(): last = lax.slice_in_dim(value, length - width, length, axis=dim)  7.22 us
    slice x11, local copies, waits for them, and re-layouts, extended(): initial = lax.slice_in_dim(value, 0, width, axis=dim)  6.33 us
    ppermute x7, local copies, waits for them, and re-layouts, extended(): before = lax.ppermute(last, axis, up)  6.16 us
    unnamed x44, local copies, waits for them, and re-layouts  6.03 us
  transfers between devices with their start and end apart: 18, of which 6 were waited for; matrix products, arithmetic and copies ran while one was open for 19% of the time, Pallas kernels for 0%

commit v1 on v0

v1 whole, which is shorter than its diff:
```python
import functools

import jax
import jax.numpy as jnp
from jax import lax
from jax.experimental import pallas as pl
from jax.experimental.pallas import tpu as pltpu
from jax.sharding import PartitionSpec as P

WEIGHTS = (0.25, 0.125, 0.125, 0.125, 0.125, 0.125, 0.125)
AXES = ("gx", "gy", "gz")


def partner(index, count, color):
    if color == 0:
        return index ^ 1
    return (index + 1) % count if index % 2 else (index - 1) % count


def axis_pairs(axis, color):
    count = lax.axis_size(axis)
    return [(i, partner(i, count, color)) for i in range(count)]


def cross_pairs(color):
    nx, ny, nz = (lax.axis_size(a) for a in AXES)
    pairs = []
    for x in range(nx):
        for y in range(ny):
            for z in range(nz):
                if x % 2 == 0:
                    to = (x * ny + partner(y, ny, color)) * nz + z
                else:
                    to = (x * ny + y) * nz + partner(z, nz, color)
                pairs.append(((x * ny + y) * nz + z, to))
    return pairs


def parities():
    return tuple(lax.rem(lax.axis_index(a), 2) == 0 for a in AXES)


def load(ref, *lead):
    return [ref[lead + (x,)] for x in range(ref.shape[len(lead)])]


def total(terms):
    out = terms[0]
    for t in terms[1:]:
        out = out + t
    return out


def collided(f_ref, r_ref, t_ref):
    nx = r_ref.shape[0]
    rate = load(r_ref)
    inverse = [[1.0 / t for t in load(t_ref, s)] for s in range(2)]
    f = [[load(f_ref, s, q) for q in range(7)] for s in range(2)]
    rho = [[total([f[s][q][x] for q in range(7)]) for x in range(nx)] for s in range(2)]
    c = [[[None] * nx for _ in range(7)] for _ in range(2)]
    for x in range(nx):
        reaction = rate[x] * rho[0][x] * rho[1][x]
        for s in range(2):
            source = reaction if s == 1 else -reaction
            for q in range(7):
                w = WEIGHTS[q]
                v = f[s][q][x]
                c[s][q][x] = v - (v - w * rho[s][x]) * inverse[s][x] + w * source
    return c, rho, inverse, rate


def pack_x(fields, last):
    return [v[-1] if last else v[0] for v in fields]


def pack_y(fields, last):
    rows = []
    for v in fields:
        for plane in v:
            n = plane.shape[0]
            rows.append(plane[n - 1 : n] if last else plane[0:1])
    return jnp.concatenate(rows, axis=0)


def pack_z(fields, last):
    lane = lax.broadcasted_iota(jnp.int32, (8, 128), 1)
    out = jnp.zeros((8, 128), jnp.float32)
    j = 0
    for v in fields:
        for plane in v:
            for h in range(plane.shape[0] // 8):
                part = plane[8 * h : 8 * h + 8]
                shift = (j + 1) % 128 if last else j
                moved = pltpu.roll(part, shift, axis=1) if shift else part
                out = jnp.where(lane == j, moved, out)
                j += 1
    return out


def faces(up, down, even):
    out = []
    for axis, pack in enumerate((pack_x, pack_y, pack_z)):
        a, b = pack(up[axis], True), pack(down[axis], False)
        if axis == 0:
            first = [jnp.where(even[0], u, d) for u, d in zip(a, b)]
            second = [jnp.where(even[0], d, u) for u, d in zip(a, b)]
        else:
            first, second = jnp.where(even[axis], a, b), jnp.where(even[axis], b, a)
        out.append((first, second))
    return out


def store_faces(packed, even, s_ref, own0_ref, own1_ref, x_ref):
    (x0, x1), (y0, y1), (z0, z1) = packed
    for k in range(len(x0)):
        s_ref[16 * k : 16 * k + 16] = x0[k]
        x_ref[16 * k : 16 * k + 16] = x1[k]
    base = 16 * len(x0)
    rows = y0.shape[0]
    if rows > 8:
        pad = jnp.zeros((rows - 8, 128), jnp.float32)
        z0, z1 = jnp.concatenate([z0, pad], axis=0), jnp.concatenate([z1, pad], axis=0)
    own0_ref[...] = jnp.where(even[0], y0, z0)
    own1_ref[...] = jnp.where(even[0], y1, z1)
    s_ref[base : base + rows] = jnp.where(even[0], z0, y0)
    s_ref[base + rows : base + 2 * rows] = jnp.where(even[0], z1, y1)


def load_faces(count, even, s_ref, x_ref, c0_ref, c1_ref, t_ref):
    rows = 4 * count
    x0 = [s_ref[16 * k : 16 * k + 16] for k in range(count)]
    x1 = [x_ref[16 * k : 16 * k + 16] for k in range(count)]
    mine0, mine1 = c0_ref[0:rows], c1_ref[0:rows]
    other0, other1 = t_ref[0:rows], t_ref[rows : 2 * rows]
    y0, y1 = jnp.where(even[0], mine0, other0), jnp.where(even[0], mine1, other1)
    z0 = jnp.where(even[0], other0[0:8], mine0[0:8])
    z1 = jnp.where(even[0], other1[0:8], mine1[0:8])
    above = [[jnp.where(even[0], u, d) for u, d in zip(x0, x1)]]
    below = [[jnp.where(even[0], d, u) for u, d in zip(x0, x1)]]
    for axis, (u, d) in ((1, (y0, y1)), (2, (z0, z1))):
        above.append(jnp.where(even[axis], u, d))
        below.append(jnp.where(even[axis], d, u))
    return above, below


def moved(v, axis, sign, halo, k):
    if axis == 0:
        return v[1:] + [halo[k]] if sign > 0 else [halo[k]] + v[:-1]
    nx, (n, lanes) = len(v), v[0].shape
    out = []
    for x in range(nx):
        plane = v[x]
        if axis == 1:
            row = lax.broadcasted_iota(jnp.int32, (n, lanes), 0)
            edge = halo[k * nx + x : k * nx + x + 1]
            rolled = pltpu.roll(plane, n - 1 if sign > 0 else 1, axis=0)
            out.append(jnp.where(row == (n - 1 if sign > 0 else 0), edge, rolled))
        else:
            lane = lax.broadcasted_iota(jnp.int32, (n, lanes), 1)
            parts = []
            for h in range(n // 8):
                j = (k * nx + x) * (n // 8) + h
                shift = (lanes - 1 - j) % lanes if sign > 0 else (lanes - j) % lanes
                parts.append(pltpu.roll(halo, shift, axis=1) if shift else halo)
            edge = jnp.concatenate(parts, axis=0)
            rolled = pltpu.roll(plane, lanes - 1 if sign > 0 else 1, axis=1)
            out.append(jnp.where(lane == (lanes - 1 if sign > 0 else 0), edge, rolled))
    return out


def first_kernel(f_ref, g_ref, r_ref, t_ref, s_ref, own0_ref, own1_ref, x_ref):
    even = parities()
    c, _, _, _ = collided(f_ref, r_ref, t_ref)
    up, down = [], []
    for axis in range(3):
        plus, minus = 1 + 2 * axis, 2 + 2 * axis
        up.append([load(g_ref, 0, minus), load(g_ref, 1, minus), c[0][plus], c[1][plus]])
        down.append([load(g_ref, 0, plus), load(g_ref, 1, plus), c[0][minus], c[1][minus]])
    store_faces(faces(up, down, even), even, s_ref, own0_ref, own1_ref, x_ref)


def adjoint(upstream, state, rho, inverse, rate):
    moments = [total([WEIGHTS[q] * upstream[s][q] for q in range(7)]) for s in range(2)]
    contrast = moments[1] - moments[0]
    scaled = rate * contrast
    earlier, relax = [], []
    for s in range(2):
        keep = 1.0 - inverse[s]
        add = moments[s] * inverse[s] + scaled * rho[1 - s]
        earlier.append([keep * upstream[s][q] + add for q in range(7)])
        part = total([upstream[s][q] * (state[s][q] - WEIGHTS[q] * rho[s]) for q in range(7)])
        relax.append(part * inverse[s] * inverse[s])
    return earlier, rho[0] * rho[1] * contrast, relax


def second_kernel(
    f_ref, g_ref, r_ref, t_ref, sr_ref, xr_ref, c0_ref, c1_ref, tr_ref,
    later_ref, rate_ref, relax_ref, s_ref, own0_ref, own1_ref, x_ref,
):
    even = parities()
    nx = r_ref.shape[0]
    c, _, inverse, rate = collided(f_ref, r_ref, t_ref)
    above, below = load_faces(4, even, sr_ref, xr_ref, c0_ref, c1_ref, tr_ref)
    upstream = [[load(g_ref, s, 0)] for s in range(2)]
    middle = [[c[s][0]] for s in range(2)]
    for s in range(2):
        for axis in range(3):
            plus, minus = 1 + 2 * axis, 2 + 2 * axis
            upstream[s].append(moved(load(g_ref, s, plus), axis, 1, above[axis], s))
            upstream[s].append(moved(load(g_ref, s, minus), axis, -1, below[axis], s))
            middle[s].append(moved(c[s][plus], axis, -1, below[axis], 2 + s))
            middle[s].append(moved(c[s][minus], axis, 1, above[axis], 2 + s))
    later = [[[None] * nx for _ in range(7)] for _ in range(2)]
    for x in range(nx):
        up = [[upstream[s][q][x] for q in range(7)] for s in range(2)]
        mid = [[middle[s][q][x] for q in range(7)] for s in range(2)]
        rho = [total(mid[s]) for s in range(2)]
        earlier, rate_part, relax_part = adjoint(up, mid, rho, [inverse[s][x] for s in range(2)], rate[x])
        rate_ref[x] = rate_part
        for s in range(2):
            relax_ref[s, x] = relax_part[s]
            for q in range(7):
                later[s][q][x] = earlier[s][q]
                later_ref[s, q, x] = earlier[s][q]
    up = [[later[s][2 + 2 * axis] for s in range(2)] for axis in range(3)]
    down = [[later[s][1 + 2 * axis] for s in range(2)] for axis in range(3)]
    store_faces(faces(up, down, even), even, s_ref, own0_ref, own1_ref, x_ref)


def third_kernel(
    f_ref, r_ref, t_ref, later_ref, rate_late_ref, relax_late_ref, sr_ref, xr_ref, c0_ref, c1_ref, tr_ref,
    state_ref, rate_ref, relax_ref,
):
    even = parities()
    nx = r_ref.shape[0]
    above, below = load_faces(2, even, sr_ref, xr_ref, c0_ref, c1_ref, tr_ref)
    upstream = [[load(later_ref, s, 0)] for s in range(2)]
    for s in range(2):
        for axis in range(3):
            upstream[s].append(moved(load(later_ref, s, 1 + 2 * axis), axis, 1, above[axis], s))
            upstream[s].append(moved(load(later_ref, s, 2 + 2 * axis), axis, -1, below[axis], s))
    for x in range(nx):
        up = [[upstream[s][q][x] for q in range(7)] for s in range(2)]
        state = [[f_ref[s, q, x] for q in range(7)] for s in range(2)]
        rho = [total(state[s]) for s in range(2)]
        inverse = [1.0 / t_ref[s, x] for s in range(2)]
        earlier, rate_part, relax_part = adjoint(up, state, rho, inverse, r_ref[x])
        rate_ref[x] = rate_late_ref[x] + rate_part
        for s in range(2):
            relax_ref[s, x] = relax_late_ref[s, x] + relax_part[s]
            for q in range(7):
                state_ref[s, q, x] = earlier[s][q]


def call(kernel, shapes, *args):
    return pl.pallas_call(
        kernel,
        out_shape=[jax.ShapeDtypeStruct(s, jnp.float32) for s in shapes],
        in_specs=[pl.BlockSpec(memory_space=pltpu.VMEM)] * len(args),
        out_specs=[pl.BlockSpec(memory_space=pltpu.VMEM)] * len(shapes),
        compiler_params=pltpu.CompilerParams(vmem_limit_bytes=32 * 1024 * 1024),
    )(*args)


def exchange(rows, s, own0, own1, x):
    base = s.shape[0] - 2 * rows
    s_in = lax.ppermute(s, "gx", axis_pairs("gx", 0))
    far = jnp.concatenate([own1, s_in[base + rows :]], axis=0)
    near = jnp.concatenate([own0, s_in[base : base + rows]], axis=0)
    far_in = lax.ppermute(far, AXES, cross_pairs(1))
    near_in = lax.ppermute(near, AXES, cross_pairs(0))
    x_in = lax.ppermute(x, "gx", axis_pairs("gx", 1))
    back = jnp.concatenate([near_in[rows:], far_in[rows:]], axis=0)
    back_in = lax.ppermute(back, "gx", axis_pairs("gx", 0))
    return s_in, x_in, near_in, far_in, back_in


def message_shapes(count):
    return [(16 * count + 8 * count, 128), (4 * count, 128), (4 * count, 128), (16 * count, 128)]


def on_device(checkpoint, cotangent, reaction_rate, relax_time):
    sent = call(first_kernel, message_shapes(4), checkpoint, cotangent, reaction_rate, relax_time)
    received = exchange(16, *sent)
    later, rate_late, relax_late, *sent = call(
        second_kernel,
        [checkpoint.shape, reaction_rate.shape, relax_time.shape] + message_shapes(2),
        checkpoint, cotangent, reaction_rate, relax_time, *received,
    )
    received = exchange(8, *sent)
    return tuple(
        call(
            third_kernel,
            [checkpoint.shape, reaction_rate.shape, relax_time.shape],
            checkpoint, reaction_rate, relax_time, later, rate_late, relax_late, *received,
        )
    )


def solution(mesh):
    placed = (
        P(None, None, "gx", "gy", "gz"),
        P(None, None, "gx", "gy", "gz"),
        P("gx", "gy", "gz"),
        P(None, "gx", "gy", "gz"),
    )
    return jax.shard_map(
        on_device,
        mesh=mesh,
        in_specs=placed,
        out_specs=(P(None, None, "gx", "gy", "gz"), P("gx", "gy", "gz"), P(None, "gx", "gy", "gz")),
        check_vma=False,
    )
```

time: 154 us -> 64.4 us (0.42)
  the two profiles are of different devices: /device:TPU:6 before, /device:TPU:1 now
where the time goes in v1:
time: 64.4 us; the launch traced here: 63.7 us
  starting transfers between devices  49.4 us (77%)
  local copies, waits for them, and re-layouts  6.22 us (10%)
  waiting for transfers between devices  5.74 us (9%)
  Pallas kernels  1.51 us (2%)
  between operations  0.81 us (1%)
    ppermute x2, starting transfers between devices, exchange(): far_in = lax.ppermute(far, AXES, cross_pairs(1))  23.2 us
    ppermute x2, starting transfers between devices, exchange(): s_in = lax.ppermute(s, 'gx', axis_pairs('gx', 0))  11.2 us
    ppermute x2, starting transfers between devices, exchange(): back_in = lax.ppermute(back, 'gx', axis_pairs('gx', 0))  7.34 us
    unnamed x18, local copies, waits for them, and re-layouts  4.83 us
    ppermute x2, starting transfers between devices, exchange(): x_in = lax.ppermute(x, 'gx', axis_pairs('gx', 1))  3.84 us
    ppermute x2, starting transfers between devices, exchange(): near_in = lax.ppermute(near, AXES, cross_pairs(0))  3.82 us
    ppermute x2, waiting for transfers between devices, exchange(): far_in = lax.ppermute(far, AXES, cross_pairs(1))  2.44 us
    ppermute x2, waiting for transfers between devices, exchange(): s_in = lax.ppermute(s, 'gx', axis_pairs('gx', 0))  1.69 us
  transfers between devices with their start and end apart: 10, of which 5 were waited for; matrix products, arithmetic and copies ran while one was open for 0% of the time, Pallas kernels for 0%

profile of v1, /device:TPU:1, one launch (start us, length us, event | category | flops | bytes accessed | tf_op | source)
XLA Modules:
  0.0 63.7 jit_solution(17743985039254909249)
XLA Ops:
  0.6 0.0 copy-start
  0.6 1.0 %copy-done = f32[2,7,4,16,128]{4,3,2,1,0:T(8,128)S(1)} copy-done((f32[2,7,4,16,128]{4,3,2,1,0:T(8,128)S(1)}, f32[2,7,4,16,128]{4,3,2,1,0:T(8,128)}, u32[]{:S(2)}) %copy-start) | copy-done | bytes 458776
  1.7 0.0 copy-start.1
  1.7 1.0 %copy-done.1 = f32[2,7,4,16,128]{4,3,2,1,0:T(8,128)S(1)} copy-done((f32[2,7,4,16,128]{4,3,2,1,0:T(8,128)S(1)}, f32[2,7,4,16,128]{4,3,2,1,0:T(8,128)}, u32[]{:S(2)}) %copy-start.1) | copy-done | bytes 458776
  2.7 0.0 copy-start.2
  2.7 0.8 %copy-done.2 = f32[2,4,16,128]{3,2,1,0:T(8,128)S(1)} copy-done((f32[2,4,16,128]{3,2,1,0:T(8,128)S(1)}, f32[2,4,16,128]{3,2,1,0:T(8,128)}, u32[]{:S(2)}) %copy-start.2) | copy-done | bytes 65560
  3.5 0.0 copy-start.4
  3.5 0.8 %copy-done.4 = f32[4,16,128]{2,1,0:T(8,128)S(1)} copy-done((f32[4,16,128]{2,1,0:T(8,128)S(1)}, f32[4,16,128]{2,1,0:T(8,128)}, u32[]{:S(2)}) %copy-start.4) | copy-done | bytes 32792
  4.3 0.1 shard_map.67
  4.4 8.8 %collective-permute-start = (f32[96,128]{1,0:T(8,128)S(1)}, f32[96,128]{1,0:T(8,128)S(1)}, u32[]{:S(2)}, u32[]{:S(2)}) collective-permute-start(f32[96,128]{1,0:T(8,128)S(1)} %get-tuple-element.14), channel_id=1, source_target_pairs={{0,64},{64,0},{128,192},{192,128},{256,320},{320,256},{384,448},{4... | collective-permute-start | bytes 147464 | tf_op jit(solution)/shard_map/ppermute | solution.py:267
  13.2 0.9 %collective-permute-done.sr_ref = f32[96,128]{1,0:T(8,128)S(1)} collective-permute-done((f32[96,128]{1,0:T(8,128)S(1)}, f32[96,128]{1,0:T(8,128)S(1)}, u32[]{:S(2)}, u32[]{:S(2)}) %collective-permute-start) | collective-permute-done | bytes 49184 | tf_op jit(solution)/shard_map/ppermute | solution.py:267
  14.1 1.9 %collective-permute-start.2 = (f32[32,128]{1,0:T(8,128)S(1)}, f32[32,128]{1,0:T(8,128)S(1)}, u32[]{:S(2)}, u32[]{:S(2)}) collective-permute-start(f32[32,128]{1,0:T(8,128)S(1)} %pad_maximum_fusion), channel_id=1, source_target_pairs={{0,8},{1,9},{2,10},{3,11},{4,12},{5,13},{6,14},{7,15},{8,0},{9,1},... | collective-permute-start | bytes 49160 | tf_op jit(solution)/shard_map/ppermute | solution.py:271
  16.0 13.0 %collective-permute-start.3 = (f32[32,128]{1,0:T(8,128)S(1)}, f32[32,128]{1,0:T(8,128)S(1)}, u32[]{:S(2)}, u32[]{:S(2)}) collective-permute-start(f32[32,128]{1,0:T(8,128)S(1)} %pad_maximum_fusion.1), channel_id=1, source_target_pairs={{0,56},{1,57},{2,58},{3,59},{4,60},{5,61},{6,62},{7,63},{8,16},{9,... | collective-permute-start | bytes 49160 | tf_op jit(solution)/shard_map/ppermute | solution.py:270
  29.0 1.9 %collective-permute-start.1 = (f32[64,128]{1,0:T(8,128)S(1)}, f32[64,128]{1,0:T(8,128)S(1)}, u32[]{:S(2)}, u32[]{:S(2)}) collective-permute-start(f32[64,128]{1,0:T(8,128)S(1)} %get-tuple-element.15), channel_id=1, source_target_pairs={{0,448},{64,128},{128,64},{192,256},{256,192},{320,384},{384,320},... | collective-permute-start | bytes 98312 | tf_op jit(solution)/shard_map/ppermute | solution.py:272
  30.9 0.0 collective-permute-done.2.c0_ref
  30.9 0.0 copy-start.5
  30.9 0.6 copy-done.5
  31.5 0.0 collective-permute-done.3.c1_ref
  31.5 0.0 slice-start
  31.5 0.7 %slice-done = f32[16,128]{1,0:T(8,128)S(1)} async-done(((f32[32,128]{1,0:T(8,128)}), f32[16,128]{1,0:T(8,128)S(1)}, s32[]{:S(2)}) %slice-start) | async-done | bytes 8216 | tf_op jit(solution)/shard_map/slice | solution.py:273
  32.2 0.0 copy-start.6
  32.2 4.9 %collective-permute-start.4 = (f32[32,128]{1,0:T(8,128)S(1)}, f32[32,128]{1,0:T(8,128)S(1)}, u32[]{:S(2)}, u32[]{:S(2)}) collective-permute-start(f32[32,128]{1,0:T(8,128)S(1)} %pad_maximum_fusion.2), channel_id=1, source_target_pairs={{0,64},{64,0},{128,192},{192,128},{256,320},{320,256},{384,448},{4... | collective-permute-start | bytes 49160 | tf_op jit(solution)/shard_map/ppermute | solution.py:274
  37.1 0.0 collective-permute-done.1.xr_ref
  37.1 0.8 %collective-permute-done.4.tr_ref = f32[32,128]{1,0:T(8,128)S(1)} collective-permute-done((f32[32,128]{1,0:T(8,128)S(1)}, f32[32,128]{1,0:T(8,128)S(1)}, u32[]{:S(2)}, u32[]{:S(2)}) %collective-permute-start.4) | collective-permute-done | bytes 16416 | tf_op jit(solution)/shard_map/ppermute | solution.py:274
  37.9 0.0 copy-done.6
  37.9 0.4 shard_map.68
  38.3 0.0 copy-start.3
  38.3 2.4 %collective-permute-start.5 = (f32[48,128]{1,0:T(8,128)S(1)}, f32[48,128]{1,0:T(8,128)S(1)}, u32[]{:S(2)}, u32[]{:S(2)}) collective-permute-start(f32[48,128]{1,0:T(8,128)S(1)} %get-tuple-element.21), channel_id=1, source_target_pairs={{0,64},{64,0},{128,192},{192,128},{256,320},{320,256},{384,448},{4... | collective-permute-start | bytes 73736 | tf_op jit(solution)/shard_map/ppermute | solution.py:267
  40.7 0.8 %collective-permute-done.5.sr_ref = f32[48,128]{1,0:T(8,128)S(1)} collective-permute-done((f32[48,128]{1,0:T(8,128)S(1)}, f32[48,128]{1,0:T(8,128)S(1)}, u32[]{:S(2)}, u32[]{:S(2)}) %collective-permute-start.5) | collective-permute-done | bytes 24608 | tf_op jit(solution)/shard_map/ppermute | solution.py:267
  41.6 1.9 %collective-permute-start.7 = (f32[16,128]{1,0:T(8,128)S(1)}, f32[16,128]{1,0:T(8,128)S(1)}, u32[]{:S(2)}, u32[]{:S(2)}) collective-permute-start(f32[16,128]{1,0:T(8,128)S(1)} %pad_maximum_fusion.3), channel_id=1, source_target_pairs={{0,8},{1,9},{2,10},{3,11},{4,12},{5,13},{6,14},{7,15},{8,0},{9,1},... | collective-permute-start | bytes 24584 | tf_op jit(solution)/shard_map/ppermute | solution.py:271
  43.5 10.2 %collective-permute-start.8 = (f32[16,128]{1,0:T(8,128)S(1)}, f32[16,128]{1,0:T(8,128)S(1)}, u32[]{:S(2)}, u32[]{:S(2)}) collective-permute-start(f32[16,128]{1,0:T(8,128)S(1)} %pad_maximum_fusion.4), channel_id=1, source_target_pairs={{0,56},{1,57},{2,58},{3,59},{4,60},{5,61},{6,62},{7,63},{8,16},{9,... | collective-permute-start | bytes 24584 | tf_op jit(solution)/shard_map/ppermute | solution.py:270
  53.7 1.9 %collective-permute-start.6 = (f32[32,128]{1,0:T(8,128)S(1)}, f32[32,128]{1,0:T(8,128)S(1)}, u32[]{:S(2)}, u32[]{:S(2)}) collective-permute-start(f32[32,128]{1,0:T(8,128)S(1)} %get-tuple-element.22), channel_id=1, source_target_pairs={{0,448},{64,128},{128,64},{192,256},{256,192},{320,384},{384,320},... | collective-permute-start | bytes 49160 | tf_op jit(solution)/shard_map/ppermute | solution.py:272
  55.7 0.0 collective-permute-done.7.c0_ref
  55.7 0.0 copy-start.7
  55.7 0.6 copy-done.7
  56.3 2.4 %collective-permute-done.8.c1_ref = f32[16,128]{1,0:T(8,128)S(1)} collective-permute-done((f32[16,128]{1,0:T(8,128)S(1)}, f32[16,128]{1,0:T(8,128)S(1)}, u32[]{:S(2)}, u32[]{:S(2)}) %collective-permute-start.8) | collective-permute-done | bytes 8224 | tf_op jit(solution)/shard_map/ppermute | solution.py:270
  58.7 0.0 slice-start.1
  58.7 0.7 %slice-done.1 = f32[8,128]{1,0:T(8,128)S(1)} async-done(((f32[16,128]{1,0:T(8,128)}), f32[8,128]{1,0:T(8,128)S(1)}, s32[]{:S(2)}) %slice-start.1) | async-done | bytes 4120 | tf_op jit(solution)/shard_map/slice | solution.py:273
  59.4 0.0 copy-start.8
  59.4 2.5 %collective-permute-start.9 = (f32[16,128]{1,0:T(8,128)S(1)}, f32[16,128]{1,0:T(8,128)S(1)}, u32[]{:S(2)}, u32[]{:S(2)}) collective-permute-start(f32[16,128]{1,0:T(8,128)S(1)} %pad_maximum_fusion.5), channel_id=1, source_target_pairs={{0,64},{64,0},{128,192},{192,128},{256,320},{320,256},{384,448},{4... | collective-permute-start | bytes 24584 | tf_op jit(solution)/shard_map/ppermute | solution.py:274
  61.9 0.0 collective-permute-done.6.xr_ref
  61.9 0.8 %collective-permute-done.9.tr_ref = f32[16,128]{1,0:T(8,128)S(1)} collective-permute-done((f32[16,128]{1,0:T(8,128)S(1)}, f32[16,128]{1,0:T(8,128)S(1)}, u32[]{:S(2)}, u32[]{:S(2)}) %collective-permute-start.9) | collective-permute-done | bytes 8224 | tf_op jit(solution)/shard_map/ppermute | solution.py:274
  62.7 0.0 copy-done.3
  62.7 0.0 copy-done.8
  62.7 1.0 %shard_map.69 = (f32[2,7,4,16,128]{4,3,2,1,0:T(8,128)}, f32[4,16,128]{2,1,0:T(8,128)}, f32[2,4,16,128]{3,2,1,0:T(8,128)}) custom-call(f32[2,7,4,16,128]{4,3,2,1,0:T(8,128)S(1)} %copy-done, f32[4,16,128]{2,1,0:T(8,128)S(1)} %copy-done.4, f32[2,4,16,128]{3,2,1,0:T(8,128)S(1)} %copy-done.3, f32[2,7,4,16,128]{4,3,2,1,0:T(8,128)S(1)} %get-tuple-element.18.later_ref, ...), custom_call_target="tpu_custom_call" | custom-call | tf_op jit(solution)/shard_map/pallas_call | solution.py:256
  (10 shorter events, 0.0 us)
Async XLA Ops:
  0.6 1.0 %copy-start = (f32[2,7,4,16,128]{4,3,2,1,0:T(8,128)S(1)}, f32[2,7,4,16,128]{4,3,2,1,0:T(8,128)}, u32[]{:S(2)}) copy-start(f32[2,7,4,16,128]{4,3,2,1,0:T(8,128)} %f_ref.5) | copy-start | bytes 1376260
  1.7 1.0 %copy-start.1 = (f32[2,7,4,16,128]{4,3,2,1,0:T(8,128)S(1)}, f32[2,7,4,16,128]{4,3,2,1,0:T(8,128)}, u32[]{:S(2)}) copy-start(f32[2,7,4,16,128]{4,3,2,1,0:T(8,128)} %g_ref.3) | copy-start | bytes 1376260
  2.7 0.8 %copy-start.2 = (f32[2,4,16,128]{3,2,1,0:T(8,128)S(1)}, f32[2,4,16,128]{3,2,1,0:T(8,128)}, u32[]{:S(2)}) copy-start(f32[2,4,16,128]{3,2,1,0:T(8,128)} %t_ref.5) | copy-start | bytes 196612
  3.5 0.8 %copy-start.4 = (f32[4,16,128]{2,1,0:T(8,128)S(1)}, f32[4,16,128]{2,1,0:T(8,128)}, u32[]{:S(2)}) copy-start(f32[4,16,128]{2,1,0:T(8,128)} %r_ref.5) | copy-start | bytes 98308
  4.4 9.6 %collective-permute-start = (f32[96,128]{1,0:T(8,128)S(1)}, f32[96,128]{1,0:T(8,128)S(1)}, u32[]{:S(2)}, u32[]{:S(2)}) collective-permute-start(f32[96,128]{1,0:T(8,128)S(1)} %get-tuple-element.14), channel_id=1, source_target_pairs={{0,64},{64,0},{128,192},{192,128},{256,320},{320,256},{384,448},{4... | collective-permute-start | bytes 147464 | tf_op jit(solution)/shard_map/ppermute | solution.py:267
  14.1 16.8 %collective-permute-start.2 = (f32[32,128]{1,0:T(8,128)S(1)}, f32[32,128]{1,0:T(8,128)S(1)}, u32[]{:S(2)}, u32[]{:S(2)}) collective-permute-start(f32[32,128]{1,0:T(8,128)S(1)} %pad_maximum_fusion), channel_id=1, source_target_pairs={{0,8},{1,9},{2,10},{3,11},{4,12},{5,13},{6,14},{7,15},{8,0},{9,1},... | collective-permute-start | bytes 49160 | tf_op jit(solution)/shard_map/ppermute | solution.py:271
  16.0 15.5 %collective-permute-start.3 = (f32[32,128]{1,0:T(8,128)S(1)}, f32[32,128]{1,0:T(8,128)S(1)}, u32[]{:S(2)}, u32[]{:S(2)}) collective-permute-start(f32[32,128]{1,0:T(8,128)S(1)} %pad_maximum_fusion.1), channel_id=1, source_target_pairs={{0,56},{1,57},{2,58},{3,59},{4,60},{5,61},{6,62},{7,63},{8,16},{9,... | collective-permute-start | bytes 49160 | tf_op jit(solution)/shard_map/ppermute | solution.py:270
  29.0 8.2 %collective-permute-start.1 = (f32[64,128]{1,0:T(8,128)S(1)}, f32[64,128]{1,0:T(8,128)S(1)}, u32[]{:S(2)}, u32[]{:S(2)}) collective-permute-start(f32[64,128]{1,0:T(8,128)S(1)} %get-tuple-element.15), channel_id=1, source_target_pairs={{0,448},{64,128},{128,64},{192,256},{256,192},{320,384},{384,320},... | collective-permute-start | bytes 98312 | tf_op jit(solution)/shard_map/ppermute | solution.py:272
  30.9 0.6 copy-start.5
  31.5 0.7 %slice-start = ((f32[32,128]{1,0:T(8,128)}), f32[16,128]{1,0:T(8,128)S(1)}, s32[]{:S(2)}) async-start(f32[32,128]{1,0:T(8,128)} %copy-done.5), calls=%async_computation | async-start | bytes 16384 | tf_op jit(solution)/shard_map/slice | solution.py:273
  32.2 5.7 %copy-start.6 = (f32[32,128]{1,0:T(8,128)S(1)}, f32[32,128]{1,0:T(8,128)}, u32[]{:S(2)}) copy-start(f32[32,128]{1,0:T(8,128)} %copy-done.5) | copy-start | bytes 49156
  32.2 5.7 %collective-permute-start.4 = (f32[32,128]{1,0:T(8,128)S(1)}, f32[32,128]{1,0:T(8,128)S(1)}, u32[]{:S(2)}, u32[]{:S(2)}) collective-permute-start(f32[32,128]{1,0:T(8,128)S(1)} %pad_maximum_fusion.2), channel_id=1, source_target_pairs={{0,64},{64,0},{128,192},{192,128},{256,320},{320,256},{384,448},{4... | collective-permute-start | bytes 49160 | tf_op jit(solution)/shard_map/ppermute | solution.py:274
  38.3 24.4 %copy-start.3 = (f32[2,4,16,128]{3,2,1,0:T(8,128)S(1)}, f32[2,4,16,128]{3,2,1,0:T(8,128)}, u32[]{:S(2)}) copy-start(f32[2,4,16,128]{3,2,1,0:T(8,128)} %t_ref.5) | copy-start | bytes 196612
  38.3 3.2 %collective-permute-start.5 = (f32[48,128]{1,0:T(8,128)S(1)}, f32[48,128]{1,0:T(8,128)S(1)}, u32[]{:S(2)}, u32[]{:S(2)}) collective-permute-start(f32[48,128]{1,0:T(8,128)S(1)} %get-tuple-element.21), channel_id=1, source_target_pairs={{0,64},{64,0},{128,192},{192,128},{256,320},{320,256},{384,448},{4... | collective-permute-start | bytes 73736 | tf_op jit(solution)/shard_map/ppermute | solution.py:267
  41.6 14.1 %collective-permute-start.7 = (f32[16,128]{1,0:T(8,128)S(1)}, f32[16,128]{1,0:T(8,128)S(1)}, u32[]{:S(2)}, u32[]{:S(2)}) collective-permute-start(f32[16,128]{1,0:T(8,128)S(1)} %pad_maximum_fusion.3), channel_id=1, source_target_pairs={{0,8},{1,9},{2,10},{3,11},{4,12},{5,13},{6,14},{7,15},{8,0},{9,1},... | collective-permute-start | bytes 24584 | tf_op jit(solution)/shard_map/ppermute | solution.py:271
  43.5 15.2 %collective-permute-start.8 = (f32[16,128]{1,0:T(8,128)S(1)}, f32[16,128]{1,0:T(8,128)S(1)}, u32[]{:S(2)}, u32[]{:S(2)}) collective-permute-start(f32[16,128]{1,0:T(8,128)S(1)} %pad_maximum_fusion.4), channel_id=1, source_target_pairs={{0,56},{1,57},{2,58},{3,59},{4,60},{5,61},{6,62},{7,63},{8,16},{9,... | collective-permute-start | bytes 24584 | tf_op jit(solution)/shard_map/ppermute | solution.py:270
  53.7 8.1 %collective-permute-start.6 = (f32[32,128]{1,0:T(8,128)S(1)}, f32[32,128]{1,0:T(8,128)S(1)}, u32[]{:S(2)}, u32[]{:S(2)}) collective-permute-start(f32[32,128]{1,0:T(8,128)S(1)} %get-tuple-element.22), channel_id=1, source_target_pairs={{0,448},{64,128},{128,64},{192,256},{256,192},{320,384},{384,320},... | collective-permute-start | bytes 49160 | tf_op jit(solution)/shard_map/ppermute | solution.py:272
  55.7 0.6 copy-start.7
  58.7 0.7 %slice-start.1 = ((f32[16,128]{1,0:T(8,128)}), f32[8,128]{1,0:T(8,128)S(1)}, s32[]{:S(2)}) async-start(f32[16,128]{1,0:T(8,128)} %copy-done.7), calls=%async_computation.1 | async-start | bytes 8192 | tf_op jit(solution)/shard_map/slice | solution.py:273
  59.4 3.3 %copy-start.8 = (f32[16,128]{1,0:T(8,128)S(1)}, f32[16,128]{1,0:T(8,128)}, u32[]{:S(2)}) copy-start(f32[16,128]{1,0:T(8,128)} %copy-done.7) | copy-start | bytes 24580
  59.4 3.3 %collective-permute-start.9 = (f32[16,128]{1,0:T(8,128)S(1)}, f32[16,128]{1,0:T(8,128)S(1)}, u32[]{:S(2)}, u32[]{:S(2)}) collective-permute-start(f32[16,128]{1,0:T(8,128)S(1)} %pad_maximum_fusion.5), channel_id=1, source_target_pairs={{0,64},{64,0},{128,192},{192,128},{256,320},{320,256},{384,448},{4... | collective-permute-start | bytes 24584 | tf_op jit(solution)/shard_map/ppermute | solution.py:274

commit v2 on v1

--- a/solution.py
+++ b/solution.py
@@ -97,50 +97,57 @@
     return out
 
 
-def faces(up, down, even):
-    out = []
-    for axis, pack in enumerate((pack_x, pack_y, pack_z)):
-        a, b = pack(up[axis], True), pack(down[axis], False)
-        if axis == 0:
-            first = [jnp.where(even[0], u, d) for u, d in zip(a, b)]
-            second = [jnp.where(even[0], d, u) for u, d in zip(a, b)]
-        else:
-            first, second = jnp.where(even[axis], a, b), jnp.where(even[axis], b, a)
-        out.append((first, second))
-    return out
-
-
-def store_faces(packed, even, s_ref, own0_ref, own1_ref, x_ref):
-    (x0, x1), (y0, y1), (z0, z1) = packed
-    for k in range(len(x0)):
-        s_ref[16 * k : 16 * k + 16] = x0[k]
-        x_ref[16 * k : 16 * k + 16] = x1[k]
-    base = 16 * len(x0)
-    rows = y0.shape[0]
+def store_faces(up, down, even, up_ref, down_ref, own0_ref, own1_ref):
+    count = len(up[0])
+    for k, (u, d) in enumerate(zip(pack_x(up[0], True), pack_x(down[0], False))):
+        up_ref[16 * k : 16 * k + 16] = u
+        down_ref[16 * k : 16 * k + 16] = d
+    (y0, y1), (z0, z1) = [
+        (jnp.where(even[axis], a, b), jnp.where(even[axis], b, a))
+        for axis, a, b in (
+            (1, pack_y(up[1], True), pack_y(down[1], False)),
+            (2, pack_z(up[2], True), pack_z(down[2], False)),
+        )
+    ]
+    base, rows = 16 * count, y0.shape[0]
     if rows > 8:
         pad = jnp.zeros((rows - 8, 128), jnp.float32)
         z0, z1 = jnp.concatenate([z0, pad], axis=0), jnp.concatenate([z1, pad], axis=0)
     own0_ref[...] = jnp.where(even[0], y0, z0)
     own1_ref[...] = jnp.where(even[0], y1, z1)
-    s_ref[base : base + rows] = jnp.where(even[0], z0, y0)
-    s_ref[base + rows : base + 2 * rows] = jnp.where(even[0], z1, y1)
-
-
-def load_faces(count, even, s_ref, x_ref, c0_ref, c1_ref, t_ref):
+    for ref in (up_ref, down_ref):
+        ref[base : base + rows] = jnp.where(even[0], z0, y0)
+        ref[base + rows : base + 2 * rows] = jnp.where(even[0], z1, y1)
+
+
+def load_faces(count, even, below_ref, above_ref, c1_ref, c0_ref, t_ref):
     rows = 4 * count
-    x0 = [s_ref[16 * k : 16 * k + 16] for k in range(count)]
-    x1 = [x_ref[16 * k : 16 * k + 16] for k in range(count)]
     mine0, mine1 = c0_ref[0:rows], c1_ref[0:rows]
     other0, other1 = t_ref[0:rows], t_ref[rows : 2 * rows]
     y0, y1 = jnp.where(even[0], mine0, other0), jnp.where(even[0], mine1, other1)
     z0 = jnp.where(even[0], other0[0:8], mine0[0:8])
     z1 = jnp.where(even[0], other1[0:8], mine1[0:8])
-    above = [[jnp.where(even[0], u, d) for u, d in zip(x0, x1)]]
-    below = [[jnp.where(even[0], d, u) for u, d in zip(x0, x1)]]
+    above = [[above_ref[16 * k : 16 * k + 16] for k in range(count)]]
+    below = [[below_ref[16 * k : 16 * k + 16] for k in range(count)]]
     for axis, (u, d) in ((1, (y0, y1)), (2, (z0, z1))):
         above.append(jnp.where(even[axis], u, d))
         below.append(jnp.where(even[axis], d, u))
     return above, below
+
+
+def forward_kernel(own0_ref, own1_ref, below_ref, above_ref, far_ref, near_ref):
+    even = parities()
+    rows = own0_ref.shape[0]
+    base = above_ref.shape[0] - 2 * rows
+    for own, out, at in ((own0_ref, near_ref, base), (own1_ref, far_ref, base + rows)):
+        out[0:rows] = own[...]
+        out[rows : 2 * rows] = jnp.where(even[0], above_ref[at : at + rows], below_ref[at : at + rows])
+
+
+def back_kernel(far_ref, near_ref, out_ref):
+    rows = near_ref.shape[0] // 2
+    out_ref[0:rows] = near_ref[rows : 2 * rows]
+    out_ref[rows : 2 * rows] = far_ref[rows : 2 * rows]
 
 
 def moved(v, axis, sign, halo, k):
@@ -168,7 +175,15 @@
     return out
 
 
-def first_kernel(f_ref, g_ref, r_ref, t_ref, s_ref, own0_ref, own1_ref, x_ref):
+def first_kernel(f_hbm, g_hbm, r_hbm, t_hbm, f_ref, g_ref, r_ref, t_ref, up_ref, down_ref, own0_ref, own1_ref, sems):
+    copies = [
+        pltpu.make_async_copy(a, b, sems.at[i])
+        for i, (a, b) in enumerate(((f_hbm, f_ref), (g_hbm, g_ref), (r_hbm, r_ref), (t_hbm, t_ref)))
+    ]
+    for copy in copies:
+        copy.start()
+    for copy in copies:
+        copy.wait()
     even = parities()
     c, _, _, _ = collided(f_ref, r_ref, t_ref)
     up, down = [], []
@@ -176,7 +191,7 @@
         plus, minus = 1 + 2 * axis, 2 + 2 * axis
         up.append([load(g_ref, 0, minus), load(g_ref, 1, minus), c[0][plus], c[1][plus]])
         down.append([load(g_ref, 0, plus), load(g_ref, 1, plus), c[0][minus], c[1][minus]])
-    store_faces(faces(up, down, even), even, s_ref, own0_ref, own1_ref, x_ref)
+    store_faces(up, down, even, up_ref, down_ref, own0_ref, own1_ref)
 
 
 def adjoint(upstream, state, rho, inverse, rate):
@@ -194,13 +209,13 @@
 
 
 def second_kernel(
-    f_ref, g_ref, r_ref, t_ref, sr_ref, xr_ref, c0_ref, c1_ref, tr_ref,
-    later_ref, rate_ref, relax_ref, s_ref, own0_ref, own1_ref, x_ref,
+    f_ref, g_ref, r_ref, t_ref, below_ref, above_ref, c1_ref, c0_ref, tr_ref,
+    later_ref, rate_ref, relax_ref, up_ref, down_ref, own0_ref, own1_ref,
 ):
     even = parities()
     nx = r_ref.shape[0]
     c, _, inverse, rate = collided(f_ref, r_ref, t_ref)
-    above, below = load_faces(4, even, sr_ref, xr_ref, c0_ref, c1_ref, tr_ref)
+    above, below = load_faces(4, even, below_ref, above_ref, c1_ref, c0_ref, tr_ref)
     upstream = [[load(g_ref, s, 0)] for s in range(2)]
     middle = [[c[s][0]] for s in range(2)]
     for s in range(2):
@@ -224,16 +239,16 @@
                 later_ref[s, q, x] = earlier[s][q]
     up = [[later[s][2 + 2 * axis] for s in range(2)] for axis in range(3)]
     down = [[later[s][1 + 2 * axis] for s in range(2)] for axis in range(3)]
-    store_faces(faces(up, down, even), even, s_ref, own0_ref, own1_ref, x_ref)
+    store_faces(up, down, even, up_ref, down_ref, own0_ref, own1_ref)
 
 
 def third_kernel(
-    f_ref, r_ref, t_ref, later_ref, rate_late_ref, relax_late_ref, sr_ref, xr_ref, c0_ref, c1_ref, tr_ref,
+    f_ref, r_ref, t_ref, later_ref, rate_late_ref, relax_late_ref, below_ref, above_ref, c1_ref, c0_ref, tr_ref,
     state_ref, rate_ref, relax_ref,
 ):
     even = parities()
     nx = r_ref.shape[0]
-    above, below = load_faces(2, even, sr_ref, xr_ref, c0_ref, c1_ref, tr_ref)
+    above, below = load_faces(2, even, below_ref, above_ref, c1_ref, c0_ref, tr_ref)
     upstream = [[load(later_ref, s, 0)] for s in range(2)]
     for s in range(2):
         for axis in range(3):
@@ -252,48 +267,54 @@
                 state_ref[s, q, x] = earlier[s][q]
 
 
-def call(kernel, shapes, *args):
+def call(kernel, shapes, *args, source=pltpu.VMEM, scratch=()):
     return pl.pallas_call(
         kernel,
         out_shape=[jax.ShapeDtypeStruct(s, jnp.float32) for s in shapes],
-        in_specs=[pl.BlockSpec(memory_space=pltpu.VMEM)] * len(args),
+        in_specs=[pl.BlockSpec(memory_space=source)] * len(args),
         out_specs=[pl.BlockSpec(memory_space=pltpu.VMEM)] * len(shapes),
+        scratch_shapes=list(scratch),
         compiler_params=pltpu.CompilerParams(vmem_limit_bytes=32 * 1024 * 1024),
     )(*args)
 
 
-def exchange(rows, s, own0, own1, x):
-    base = s.shape[0] - 2 * rows
-    s_in = lax.ppermute(s, "gx", axis_pairs("gx", 0))
-    far = jnp.concatenate([own1, s_in[base + rows :]], axis=0)
-    near = jnp.concatenate([own0, s_in[base : base + rows]], axis=0)
+def shifts(axis):
+    count = lax.axis_size(axis)
+    up = [(i, (i + 1) % count) for i in range(count)]
+    return up, [(j, i) for i, j in up]
+
+
+def exchange(up, down, own0, own1):
+    to_up, to_down = shifts("gx")
+    below = lax.ppermute(up, "gx", to_up)
+    above = lax.ppermute(down, "gx", to_down)
+    both = (2 * own0.shape[0], 128)
+    far, near = call(forward_kernel, [both, both], own0, own1, below, above)
     far_in = lax.ppermute(far, AXES, cross_pairs(1))
     near_in = lax.ppermute(near, AXES, cross_pairs(0))
-    x_in = lax.ppermute(x, "gx", axis_pairs("gx", 1))
-    back = jnp.concatenate([near_in[rows:], far_in[rows:]], axis=0)
+    (back,) = call(back_kernel, [both], far_in, near_in)
     back_in = lax.ppermute(back, "gx", axis_pairs("gx", 0))
-    return s_in, x_in, near_in, far_in, back_in
+    return below, above, far_in, near_in, back_in
 
 
 def message_shapes(count):
-    return [(16 * count + 8 * count, 128), (4 * count, 128), (4 * count, 128), (16 * count, 128)]
+    return [(24 * count, 128), (24 * count, 128), (4 * count, 128), (4 * count, 128)]
 
 
 def on_device(checkpoint, cotangent, reaction_rate, relax_time):
-    sent = call(first_kernel, message_shapes(4), checkpoint, cotangent, reaction_rate, relax_time)
-    received = exchange(16, *sent)
+    inputs = (checkpoint, cotangent, reaction_rate, relax_time)
+    f, g, r, t, *sent = call(
+        first_kernel, [a.shape for a in inputs] + message_shapes(4),
+        *(pltpu.with_memory_space_constraint(a, pltpu.HBM) for a in inputs),
+        source=pltpu.HBM, scratch=[pltpu.SemaphoreType.DMA((4,))],
+    )
+    received = exchange(*sent)
     later, rate_late, relax_late, *sent = call(
-        second_kernel,
-        [checkpoint.shape, reaction_rate.shape, relax_time.shape] + message_shapes(2),
-        checkpoint, cotangent, reaction_rate, relax_time, *received,
-    )
-    received = exchange(8, *sent)
+        second_kernel, [f.shape, r.shape, t.shape] + message_shapes(2), f, g, r, t, *received
+    )
+    received = exchange(*sent)
     return tuple(
-        call(
-            third_kernel,
-            [checkpoint.shape, reaction_rate.shape, relax_time.shape],
-            checkpoint, reaction_rate, relax_time, later, rate_late, relax_late, *received,
-        )
+        call(third_kernel, [f.shape, r.shape, t.shape], f, r, t, later, rate_late, relax_late, *received)
     )
 
 

time: 64.4 us -> 58.2 us (0.904)
  starting transfers between devices: 49.4 us -> 42.9 us
  local copies, waits for them, and re-layouts: 6.22 us -> 0 us
  waiting for transfers between devices: 5.74 us -> 11.5 us
  Pallas kernels: 1.51 us -> 2.75 us
    ppermute x4, starting transfers between devices: 15 us -> 8.19 us  [the longest x2 4.3 us: exchange(): above = lax.ppermute(down, 'gx', to_down)]
    unnamed x18 -> x0, local copies, waits for them, and re-layouts: 4.83 us -> none
    ppermute x2, starting transfers between devices: 23.2 us -> 27 us  [exchange(): far_in = lax.ppermute(far, AXES, cross_pairs(1))]
    ppermute x2, starting transfers between devices: 7.34 us -> 3.82 us  [exchange(): back_in = lax.ppermute(back, 'gx', axis_pairs('gx', 0))]
    ppermute x2, waiting for transfers between devices: 0.01 us -> 2.55 us  [exchange(): near_in = lax.ppermute(near, AXES, cross_pairs(0))]
    ppermute x4, waiting for transfers between devices: 1.69 us -> 4.13 us  [the longest x2 2.48 us: exchange(): above = lax.ppermute(down, 'gx', to_down)]
    slice x8 -> x0, local copies, waits for them, and re-layouts: 1.39 us -> none  [the longest x6 1.38 us: exchange(): back = jnp.concatenate([near_in[rows:], far_in[rows:]], axis=0)]
    pallas_call x3 -> x7, Pallas kernels: 1.51 us -> 2.75 us  [call(): pl.pallas_call(kernel, out_shape=[jax.ShapeDtypeStruct(s, jnp.float32) fo...]
  transfers between devices with their start and end apart: 10 -> 10, of which waited for: 5 -> 8; matrix products, arithmetic and copies ran while one was open for 0% -> 0% of each run, Pallas kernels for 0% -> 0%
where the time goes in v2:
time: 58.2 us; the launch traced here: 57.8 us
  starting transfers between devices  42.9 us (74%)
  waiting for transfers between devices  11.5 us (20%)
  Pallas kernels  2.75 us (5%)
  between operations  0.71 us (1%)
    ppermute x2, starting transfers between devices, exchange(): far_in = lax.ppermute(far, AXES, cross_pairs(1))  27 us
    ppermute x2, starting transfers between devices, exchange(): above = lax.ppermute(down, 'gx', to_down)  4.3 us
    ppermute x2, starting transfers between devices, exchange(): below = lax.ppermute(up, 'gx', to_up)  3.88 us
    ppermute x2, starting transfers between devices, exchange(): near_in = lax.ppermute(near, AXES, cross_pairs(0))  3.84 us
    ppermute x2, starting transfers between devices, exchange(): back_in = lax.ppermute(back, 'gx', axis_pairs('gx', 0))  3.82 us
    pallas_call x7, Pallas kernels, call(): pl.pallas_call(kernel, out_shape=[jax.ShapeDtypeStruct(s, jnp.float32) fo...  2.75 us
    ppermute x2, waiting for transfers between devices, exchange(): far_in = lax.ppermute(far, AXES, cross_pairs(1))  2.55 us
    ppermute x2, waiting for transfers between devices, exchange(): near_in = lax.ppermute(near, AXES, cross_pairs(0))  2.55 us
  transfers between devices with their start and end apart: 10, of which 8 were waited for; matrix products, arithmetic and copies ran while one was open for 0% of the time, Pallas kernels for 0%

profile of v2, /device:TPU:1, one launch (start us, length us, event | category | flops | bytes accessed | tf_op | source)
XLA Modules:
  0.0 57.8 jit_solution(14212501494449890227)
XLA Ops:
  0.6 1.3 %shard_map.67 = (f32[2,7,4,16,128]{4,3,2,1,0:T(8,128)S(1)}, f32[2,7,4,16,128]{4,3,2,1,0:T(8,128)S(1)}, f32[4,16,128]{2,1,0:T(8,128)S(1)}, f32[2,4,16,128]{3,2,1,...) custom-call(f32[2,7,4,16,128]{4,3,2,1,0:T(8,128)} %f_hbm.1, ...), custom_call_target="tpu_custom_call" | custom-call | tf_op jit(solution)/shard_map/pallas_call | solution.py:271
  2.0 2.6 %collective-permute-start = (f32[96,128]{1,0:T(8,128)S(1)}, f32[96,128]{1,0:T(8,128)S(1)}, u32[]{:S(2)}, u32[]{:S(2)}) collective-permute-start(f32[96,128]{1,0:T(8,128)S(1)} %get-tuple-element.26), channel_id=1, source_target_pairs={{0,64},{64,128},{128,192},{192,256},{256,320},{320,384},{384,448},... | collective-permute-start | bytes 147464 | tf_op jit(solution)/shard_map/ppermute | solution.py:289
  4.6 4.3 %collective-permute-start.1 = (f32[96,128]{1,0:T(8,128)S(1)}, f32[96,128]{1,0:T(8,128)S(1)}, u32[]{:S(2)}, u32[]{:S(2)}) collective-permute-start(f32[96,128]{1,0:T(8,128)S(1)} %get-tuple-element.27), channel_id=1, source_target_pairs={{64,0},{128,64},{192,128},{256,192},{320,256},{384,320},{448,384},... | collective-permute-start | bytes 147464 | tf_op jit(solution)/shard_map/ppermute | solution.py:290
  8.9 0.7 %collective-permute-done.below_ref = f32[96,128]{1,0:T(8,128)S(1)} collective-permute-done((f32[96,128]{1,0:T(8,128)S(1)}, f32[96,128]{1,0:T(8,128)S(1)}, u32[]{:S(2)}, u32[]{:S(2)}) %collective-permute-start) | collective-permute-done | bytes 49184 | tf_op jit(solution)/shard_map/ppermute | solution.py:289
  9.6 0.2 collective-permute-done.1.above_ref
  9.8 16.2 %collective-permute-start.2 = (f32[32,128]{1,0:T(8,128)S(1)}, f32[32,128]{1,0:T(8,128)S(1)}, u32[]{:S(2)}, u32[]{:S(2)}) collective-permute-start(f32[32,128]{1,0:T(8,128)S(1)} %get-tuple-element.30), channel_id=1, source_target_pairs={{0,56},{1,57},{2,58},{3,59},{4,60},{5,61},{6,62},{7,63},{8,16},{9,... | collective-permute-start | bytes 49160 | tf_op jit(solution)/shard_map/ppermute | solution.py:293
  26.0 1.9 %collective-permute-start.3 = (f32[32,128]{1,0:T(8,128)S(1)}, f32[32,128]{1,0:T(8,128)S(1)}, u32[]{:S(2)}, u32[]{:S(2)}) collective-permute-start(f32[32,128]{1,0:T(8,128)S(1)} %get-tuple-element.31), channel_id=1, source_target_pairs={{0,8},{1,9},{2,10},{3,11},{4,12},{5,13},{6,14},{7,15},{8,0},{9,1},... | collective-permute-start | bytes 49160 | tf_op jit(solution)/shard_map/ppermute | solution.py:294
  27.9 0.0 collective-permute-done.2.far_ref.c1_ref
  27.9 2.5 %collective-permute-done.3.near_ref.c0_ref = f32[32,128]{1,0:T(8,128)S(1)} collective-permute-done((f32[32,128]{1,0:T(8,128)S(1)}, f32[32,128]{1,0:T(8,128)S(1)}, u32[]{:S(2)}, u32[]{:S(2)}) %collective-permute-start.3) | collective-permute-done | bytes 16416 | tf_op jit(solution)/shard_map/ppermute | solution.py:294
  30.5 1.9 %collective-permute-start.4 = (f32[32,128]{1,0:T(8,128)S(1)}, f32[32,128]{1,0:T(8,128)S(1)}, u32[]{:S(2)}, u32[]{:S(2)}) collective-permute-start(f32[32,128]{1,0:T(8,128)S(1)} %shard_map.69), channel_id=1, source_target_pairs={{0,64},{64,0},{128,192},{192,128},{256,320},{320,256},{384,448},{4... | collective-permute-start | bytes 49160 | tf_op jit(solution)/shard_map/ppermute | solution.py:296
  32.4 1.1 %collective-permute-done.4.tr_ref = f32[32,128]{1,0:T(8,128)S(1)} collective-permute-done((f32[32,128]{1,0:T(8,128)S(1)}, f32[32,128]{1,0:T(8,128)S(1)}, u32[]{:S(2)}, u32[]{:S(2)}) %collective-permute-start.4) | collective-permute-done | bytes 16416 | tf_op jit(solution)/shard_map/ppermute | solution.py:296
  33.6 0.4 shard_map.70
  33.9 1.3 %collective-permute-start.5 = (f32[48,128]{1,0:T(8,128)S(1)}, f32[48,128]{1,0:T(8,128)S(1)}, u32[]{:S(2)}, u32[]{:S(2)}) collective-permute-start(f32[48,128]{1,0:T(8,128)S(1)} %get-tuple-element.35), channel_id=1, source_target_pairs={{0,64},{64,128},{128,192},{192,256},{256,320},{320,384},{384,448},... | collective-permute-start | bytes 73736 | tf_op jit(solution)/shard_map/ppermute | solution.py:289
  35.2 0.0 collective-permute-start.6
  35.2 0.9 %collective-permute-done.5.below_ref = f32[48,128]{1,0:T(8,128)S(1)} collective-permute-done((f32[48,128]{1,0:T(8,128)S(1)}, f32[48,128]{1,0:T(8,128)S(1)}, u32[]{:S(2)}, u32[]{:S(2)}) %collective-permute-start.5) | collective-permute-done | bytes 24608 | tf_op jit(solution)/shard_map/ppermute | solution.py:289
  36.2 2.3 %collective-permute-done.6.above_ref = f32[48,128]{1,0:T(8,128)S(1)} collective-permute-done((f32[48,128]{1,0:T(8,128)S(1)}, f32[48,128]{1,0:T(8,128)S(1)}, u32[]{:S(2)}, u32[]{:S(2)}) %collective-permute-start.6) | collective-permute-done | bytes 24608 | tf_op jit(solution)/shard_map/ppermute | solution.py:290
  38.5 10.8 %collective-permute-start.7 = (f32[16,128]{1,0:T(8,128)S(1)}, f32[16,128]{1,0:T(8,128)S(1)}, u32[]{:S(2)}, u32[]{:S(2)}) collective-permute-start(f32[16,128]{1,0:T(8,128)S(1)} %get-tuple-element.39), channel_id=1, source_target_pairs={{0,56},{1,57},{2,58},{3,59},{4,60},{5,61},{6,62},{7,63},{8,16},{9,... | collective-permute-start | bytes 24584 | tf_op jit(solution)/shard_map/ppermute | solution.py:293
  49.3 1.9 %collective-permute-start.8 = (f32[16,128]{1,0:T(8,128)S(1)}, f32[16,128]{1,0:T(8,128)S(1)}, u32[]{:S(2)}, u32[]{:S(2)}) collective-permute-start(f32[16,128]{1,0:T(8,128)S(1)} %get-tuple-element.40), channel_id=1, source_target_pairs={{0,8},{1,9},{2,10},{3,11},{4,12},{5,13},{6,14},{7,15},{8,0},{9,1},... | collective-permute-start | bytes 24584 | tf_op jit(solution)/shard_map/ppermute | solution.py:294
  51.2 2.5 %collective-permute-done.7.far_ref.c1_ref = f32[16,128]{1,0:T(8,128)S(1)} collective-permute-done((f32[16,128]{1,0:T(8,128)S(1)}, f32[16,128]{1,0:T(8,128)S(1)}, u32[]{:S(2)}, u32[]{:S(2)}) %collective-permute-start.7) | collective-permute-done | bytes 8224 | tf_op jit(solution)/shard_map/ppermute | solution.py:293
  53.8 0.0 collective-permute-done.8.near_ref.c0_ref
  53.8 1.9 %collective-permute-start.9 = (f32[16,128]{1,0:T(8,128)S(1)}, f32[16,128]{1,0:T(8,128)S(1)}, u32[]{:S(2)}, u32[]{:S(2)}) collective-permute-start(f32[16,128]{1,0:T(8,128)S(1)} %shard_map.72), channel_id=1, source_target_pairs={{0,64},{64,0},{128,192},{192,128},{256,320},{320,256},{384,448},{4... | collective-permute-start | bytes 24584 | tf_op jit(solution)/shard_map/ppermute | solution.py:296
  55.7 1.1 %collective-permute-done.9.tr_ref = f32[16,128]{1,0:T(8,128)S(1)} collective-permute-done((f32[16,128]{1,0:T(8,128)S(1)}, f32[16,128]{1,0:T(8,128)S(1)}, u32[]{:S(2)}, u32[]{:S(2)}) %collective-permute-start.9) | collective-permute-done | bytes 8224 | tf_op jit(solution)/shard_map/ppermute | solution.py:296
  56.8 1.0 %shard_map.73 = (f32[2,7,4,16,128]{4,3,2,1,0:T(8,128)}, f32[4,16,128]{2,1,0:T(8,128)}, f32[2,4,16,128]{3,2,1,0:T(8,128)}) custom-call(f32[2,7,4,16,128]{4,3,2,1,0:T(8,128)S(1)} %get-tuple-element.22.f_ref, f32[4,16,128]{2,1,0:T(8,128)S(1)} %get-tuple-element.23.r_ref, f32[2,4,16,128]{3,2,1,0:T(8,128)S(1)} %get-tuple-element.24.t_ref, ...), custom_call_target="tpu_custom_call" | custom-call | tf_op jit(solution)/shard_map/pallas_call | solution.py:271
  (4 shorter events, 0.0 us)
Async XLA Ops:
  2.0 7.6 %collective-permute-start = (f32[96,128]{1,0:T(8,128)S(1)}, f32[96,128]{1,0:T(8,128)S(1)}, u32[]{:S(2)}, u32[]{:S(2)}) collective-permute-start(f32[96,128]{1,0:T(8,128)S(1)} %get-tuple-element.26), channel_id=1, source_target_pairs={{0,64},{64,128},{128,192},{192,256},{256,320},{320,384},{384,448},... | collective-permute-start | bytes 147464 | tf_op jit(solution)/shard_map/ppermute | solution.py:289
  4.6 5.2 %collective-permute-start.1 = (f32[96,128]{1,0:T(8,128)S(1)}, f32[96,128]{1,0:T(8,128)S(1)}, u32[]{:S(2)}, u32[]{:S(2)}) collective-permute-start(f32[96,128]{1,0:T(8,128)S(1)} %get-tuple-element.27), channel_id=1, source_target_pairs={{64,0},{128,64},{192,128},{256,192},{320,256},{384,320},{448,384},... | collective-permute-start | bytes 147464 | tf_op jit(solution)/shard_map/ppermute | solution.py:290
  9.8 18.2 %collective-permute-start.2 = (f32[32,128]{1,0:T(8,128)S(1)}, f32[32,128]{1,0:T(8,128)S(1)}, u32[]{:S(2)}, u32[]{:S(2)}) collective-permute-start(f32[32,128]{1,0:T(8,128)S(1)} %get-tuple-element.30), channel_id=1, source_target_pairs={{0,56},{1,57},{2,58},{3,59},{4,60},{5,61},{6,62},{7,63},{8,16},{9,... | collective-permute-start | bytes 49160 | tf_op jit(solution)/shard_map/ppermute | solution.py:293
  26.0 4.5 %collective-permute-start.3 = (f32[32,128]{1,0:T(8,128)S(1)}, f32[32,128]{1,0:T(8,128)S(1)}, u32[]{:S(2)}, u32[]{:S(2)}) collective-permute-start(f32[32,128]{1,0:T(8,128)S(1)} %get-tuple-element.31), channel_id=1, source_target_pairs={{0,8},{1,9},{2,10},{3,11},{4,12},{5,13},{6,14},{7,15},{8,0},{9,1},... | collective-permute-start | bytes 49160 | tf_op jit(solution)/shard_map/ppermute | solution.py:294
  30.5 3.1 %collective-permute-start.4 = (f32[32,128]{1,0:T(8,128)S(1)}, f32[32,128]{1,0:T(8,128)S(1)}, u32[]{:S(2)}, u32[]{:S(2)}) collective-permute-start(f32[32,128]{1,0:T(8,128)S(1)} %shard_map.69), channel_id=1, source_target_pairs={{0,64},{64,0},{128,192},{192,128},{256,320},{320,256},{384,448},{4... | collective-permute-start | bytes 49160 | tf_op jit(solution)/shard_map/ppermute | solution.py:296
  33.9 2.2 %collective-permute-start.5 = (f32[48,128]{1,0:T(8,128)S(1)}, f32[48,128]{1,0:T(8,128)S(1)}, u32[]{:S(2)}, u32[]{:S(2)}) collective-permute-start(f32[48,128]{1,0:T(8,128)S(1)} %get-tuple-element.35), channel_id=1, source_target_pairs={{0,64},{64,128},{128,192},{192,256},{256,320},{320,384},{384,448},... | collective-permute-start | bytes 73736 | tf_op jit(solution)/shard_map/ppermute | solution.py:289
  35.2 3.3 %collective-permute-start.6 = (f32[48,128]{1,0:T(8,128)S(1)}, f32[48,128]{1,0:T(8,128)S(1)}, u32[]{:S(2)}, u32[]{:S(2)}) collective-permute-start(f32[48,128]{1,0:T(8,128)S(1)} %get-tuple-element.36), channel_id=1, source_target_pairs={{64,0},{128,64},{192,128},{256,192},{320,256},{384,320},{448,384},... | collective-permute-start | bytes 73736 | tf_op jit(solution)/shard_map/ppermute | solution.py:290
  38.5 15.3 %collective-permute-start.7 = (f32[16,128]{1,0:T(8,128)S(1)}, f32[16,128]{1,0:T(8,128)S(1)}, u32[]{:S(2)}, u32[]{:S(2)}) collective-permute-start(f32[16,128]{1,0:T(8,128)S(1)} %get-tuple-element.39), channel_id=1, source_target_pairs={{0,56},{1,57},{2,58},{3,59},{4,60},{5,61},{6,62},{7,63},{8,16},{9,... | collective-permute-start | bytes 24584 | tf_op jit(solution)/shard_map/ppermute | solution.py:293
  49.3 4.5 %collective-permute-start.8 = (f32[16,128]{1,0:T(8,128)S(1)}, f32[16,128]{1,0:T(8,128)S(1)}, u32[]{:S(2)}, u32[]{:S(2)}) collective-permute-start(f32[16,128]{1,0:T(8,128)S(1)} %get-tuple-element.40), channel_id=1, source_target_pairs={{0,8},{1,9},{2,10},{3,11},{4,12},{5,13},{6,14},{7,15},{8,0},{9,1},... | collective-permute-start | bytes 24584 | tf_op jit(solution)/shard_map/ppermute | solution.py:294
  53.8 3.1 %collective-permute-start.9 = (f32[16,128]{1,0:T(8,128)S(1)}, f32[16,128]{1,0:T(8,128)S(1)}, u32[]{:S(2)}, u32[]{:S(2)}) collective-permute-start(f32[16,128]{1,0:T(8,128)S(1)} %shard_map.72), channel_id=1, source_target_pairs={{0,64},{64,0},{128,192},{192,128},{256,320},{320,256},{384,448},{4... | collective-permute-start | bytes 24584 | tf_op jit(solution)/shard_map/ppermute | solution.py:296

commit v3 on v2

v3 whole, which is shorter than its diff:
```python
import jax
import jax.numpy as jnp
from jax import lax
from jax.experimental import pallas as pl
from jax.experimental.pallas import tpu as pltpu
from jax.sharding import PartitionSpec as P

WEIGHTS = (0.25, 0.125, 0.125, 0.125, 0.125, 0.125, 0.125)
AXES = ("gx", "gy", "gz")


def partner(index, count, color):
    if color == 0:
        return index ^ 1
    return (index + 1) % count if index % 2 else (index - 1) % count


def axis_pairs(axis, color):
    count = lax.axis_size(axis)
    return [(i, partner(i, count, color)) for i in range(count)]


def parities():
    return tuple(lax.rem(lax.axis_index(a), 2) == 0 for a in AXES)


def load(ref, *lead):
    return [ref[lead + (x,)] for x in range(ref.shape[len(lead)])]


def total(terms):
    out = terms[0]
    for t in terms[1:]:
        out = out + t
    return out


def collided(f_ref, r_ref, t_ref):
    nx = r_ref.shape[0]
    rate = load(r_ref)
    inverse = [[1.0 / t for t in load(t_ref, s)] for s in range(2)]
    f = [[load(f_ref, s, q) for q in range(7)] for s in range(2)]
    rho = [[total([f[s][q][x] for q in range(7)]) for x in range(nx)] for s in range(2)]
    c = [[[None] * nx for _ in range(7)] for _ in range(2)]
    for x in range(nx):
        reaction = rate[x] * rho[0][x] * rho[1][x]
        for s in range(2):
            source = reaction if s == 1 else -reaction
            for q in range(7):
                w = WEIGHTS[q]
                v = f[s][q][x]
                c[s][q][x] = v - (v - w * rho[s][x]) * inverse[s][x] + w * source
    return c, rho, inverse, rate


def pack_x(fields, last):
    return [v[-1] if last else v[0] for v in fields]


def rows_of(v, i):
    return jnp.concatenate([plane[i : i + 1] for plane in v], axis=0)


def pack_y(fields, last):
    n = fields[0][0].shape[0]
    return jnp.concatenate([rows_of(v, n - 1 if last else 0) for v in fields], axis=0)


def pack_z(fields, last, start=0, out=None):
    lane = lax.broadcasted_iota(jnp.int32, (8, 128), 1)
    out = jnp.zeros((8, 128), jnp.float32) if out is None else out
    j = start
    for v in fields:
        for plane in v:
            for h in range(plane.shape[0] // 8):
                part = plane[8 * h : 8 * h + 8]
                shift = (j + 1) % 128 if last else j
                part = pltpu.roll(part, shift, axis=1) if shift else part
                out = jnp.where(lane == j, part, out)
                j += 1
    return out


def cut(v, axis, sign):
    if axis == 0:
        zero = jnp.zeros_like(v[0])
        return v[1:] + [zero] if sign > 0 else [zero] + v[:-1]
    out = []
    for plane in v:
        n = plane.shape[axis - 1]
        at = lax.broadcasted_iota(jnp.int32, plane.shape, axis - 1)
        rolled = pltpu.roll(plane, n - 1 if sign > 0 else 1, axis=axis - 1)
        out.append(jnp.where(at == (n - 1 if sign > 0 else 0), 0.0, rolled))
    return out


def plus(a, b):
    return [x + y for x, y in zip(a, b)]


def partial_sums(g, c, axes):
    moments, density = [], []
    for s in range(2):
        m = [WEIGHTS[1] * v for v in cut(g[s][1 + 2 * axes[0]], axes[0], 1)]
        d = plus(c[s][0], cut(c[s][1 + 2 * axes[0]], axes[0], -1))
        m = plus(m, [WEIGHTS[1] * v for v in cut(g[s][2 + 2 * axes[0]], axes[0], -1)])
        d = plus(d, cut(c[s][2 + 2 * axes[0]], axes[0], 1))
        m = plus(m, [WEIGHTS[1] * v for v in cut(g[s][1 + 2 * axes[1]], axes[1], 1)])
        d = plus(d, cut(c[s][1 + 2 * axes[1]], axes[1], -1))
        m = plus(m, [WEIGHTS[1] * v for v in cut(g[s][2 + 2 * axes[1]], axes[1], -1)])
        d = plus(d, cut(c[s][2 + 2 * axes[1]], axes[1], 1))
        moments.append(plus(m, [WEIGHTS[0] * v for v in g[s][0]]))
        density.append(d)
    return moments, density


def face_fields(g, c, moments, density, inverse, rate, axis, last):
    out_q, in_q = (1 + 2 * axis, 2 + 2 * axis) if last else (2 + 2 * axis, 1 + 2 * axis)
    sign = -1 if last else 1
    inner = [cut(g[s][in_q], axis, sign) for s in range(2)]
    m = [plus(moments[s], [WEIGHTS[1] * v for v in inner[s]]) for s in range(2)]
    d = [plus(density[s], cut(c[s][out_q], axis, sign)) for s in range(2)]
    return [*inner, *m, *d, *inverse, rate]


def edge_fields(g, c, axis):
    p, m = 1 + 2 * axis, 2 + 2 * axis
    return [(g[0][p], g[0][m]), (g[1][p], g[1][m]), (c[0][m], c[0][p]), (c[1][m], c[1][p])]


def first_kernel(
    f_hbm, g_hbm, r_hbm, t_hbm, f_ref, g_ref, r_ref, t_ref, up_ref, down_ref, own0_ref, own1_ref, diag_ref, raw_ref, sems
):
    copies = [
        pltpu.make_async_copy(a, b, sems.at[i])
        for i, (a, b) in enumerate(((f_hbm, f_ref), (g_hbm, g_ref), (r_hbm, r_ref), (t_hbm, t_ref)))
    ]
    for copy in copies:
        copy.start()
    for copy in copies:
        copy.wait()
    even = parities()
    c, _, inverse, rate = collided(f_ref, r_ref, t_ref)
    g = [[load(g_ref, s, q) for q in range(7)] for s in range(2)]
    up, down = [], []
    for axis in range(3):
        p, m = 1 + 2 * axis, 2 + 2 * axis
        up.append([g[0][m], g[1][m], c[0][p], c[1][p]])
        down.append([g[0][p], g[1][p], c[0][m], c[1][m]])
    for k, (u, d) in enumerate(zip(pack_x(up[0], True), pack_x(down[0], False))):
        up_ref[16 * k : 16 * k + 16] = u
        down_ref[16 * k : 16 * k + 16] = d
    nx, n = len(rate), rate[0].shape[0]
    lane = lax.broadcasted_iota(jnp.int32, (nx, 128), 1)
    row = lax.broadcasted_iota(jnp.int32, (n, 128), 0)
    x_edge, y_edge, z_edge = (edge_fields(g, c, axis) for axis in range(3))
    y_faces, z_faces = [], []
    y_sums, z_sums = partial_sums(g, c, (0, 2)), partial_sums(g, c, (0, 1))
    for last in (False, True):
        i = n - 1 if last else 0
        raw = pack_y((up if last else down)[1], last)
        deep = pack_y(face_fields(g, c, *y_sums, inverse, rate, 1, last), last)
        x_lines = [line for a, b in x_edge for line in (a[0][i : i + 1], b[-1][i : i + 1])]
        x_lines.append(jnp.zeros((28 - 4 * len(rate) - len(x_lines), 128), jnp.float32))
        z_lines = [jnp.where(lane < 64, rows_of(a, i), rows_of(b, i)) for a, b in z_edge]
        y_faces.append((raw, jnp.concatenate([raw, deep, *x_lines], axis=0), jnp.concatenate(z_lines, axis=0)))
        raw = pack_z((up if last else down)[2], last)
        deep = pack_z(face_fields(g, c, *z_sums, inverse, rate, 2, last), last, 32, raw)
        y_lines = [[jnp.where(row < 8, u, v) for u, v in zip(a, b)] for a, b in y_edge]
        x_lines = [a[:-1] + b[-1:] for a, b in x_edge]
        z_faces.append((raw, deep, pack_z(y_lines + x_lines, last)))
    y1, y2 = jnp.where(even[1], y_faces[1][0], y_faces[0][0]), jnp.where(even[1], y_faces[0][0], y_faces[1][0])
    z1, z2 = jnp.where(even[2], z_faces[1][0], z_faces[0][0]), jnp.where(even[2], z_faces[0][0], z_faces[1][0])
    y_deep = jnp.where(even[1], y_faces[0][1], y_faces[1][1])
    y_lines = jnp.where(even[1], y_faces[0][2], y_faces[1][2])
    z_deep = jnp.where(even[2], z_faces[0][1], z_faces[1][1])
    z_lines = jnp.where(even[2], z_faces[0][2], z_faces[1][2])
    raw_ref[0:16] = y2
    raw_ref[16:24] = z2
    diag_ref[0:16] = y_lines
    diag_ref[16:24] = z_lines
    z1 = jnp.concatenate([z1, jnp.zeros_like(z1)], axis=0)
    y_all = jnp.concatenate([y_deep, y_lines], axis=0)
    z_all = jnp.concatenate([z_deep, z_lines, jnp.zeros((y_all.shape[0] - 16, 128), jnp.float32)], axis=0)
    own0_ref[...] = jnp.where(even[0], y1, z1)
    own1_ref[...] = jnp.where(even[0], y_all, z_all)
    for ref in (up_ref, down_ref):
        ref[64:80] = jnp.where(even[0], z1, y1)
        ref[80:160] = jnp.where(even[0], z_all, y_all)


def forward_kernel(own0_ref, own1_ref, below_ref, above_ref, y_ref, z_ref, near_ref):
    even = parities()
    near_ref[0:16] = own0_ref[...]
    near_ref[16:32] = jnp.where(even[0], above_ref[64:80], below_ref[64:80])
    share = jnp.where(even[0], above_ref[80:160], below_ref[80:160])
    y_ref[0:80] = own1_ref[...]
    y_ref[80:160] = share
    z_ref[0:16] = own1_ref[0:16]
    z_ref[16:32] = share[0:16]


def back_kernel(y_ref, z_ref, near_ref, out_ref):
    even = parities()
    out_ref[0:16] = near_ref[16:32]
    out_ref[16:32] = jnp.where(even[0], y_ref[80:96], z_ref[16:32])
    out_ref[32:96] = y_ref[96:160]


def moved(v, axis, sign, halo, k):
    if axis == 0:
        return v[1:] + [halo[k]] if sign > 0 else [halo[k]] + v[:-1]
    nx, (n, lanes) = len(v), v[0].shape
    out = []
    for x in range(nx):
        plane = v[x]
        if axis == 1:
            row = lax.broadcasted_iota(jnp.int32, (n, lanes), 0)
            edge = halo[k * nx + x : k * nx + x + 1]
            rolled = pltpu.roll(plane, n - 1 if sign > 0 else 1, axis=0)
            out.append(jnp.where(row == (n - 1 if sign > 0 else 0), edge, rolled))
        else:
            lane = lax.broadcasted_iota(jnp.int32, (n, lanes), 1)
            parts = []
            for h in range(n // 8):
                j = (k * nx + x) * (n // 8) + h
                shift = (lanes - 1 - j) % lanes if sign > 0 else (lanes - j) % lanes
                parts.append(pltpu.roll(halo, shift, axis=1) if shift else halo)
            edge = jnp.concatenate(parts, axis=0)
            rolled = pltpu.roll(plane, lanes - 1 if sign > 0 else 1, axis=1)
            out.append(jnp.where(lane == (lanes - 1 if sign > 0 else 0), edge, rolled))
    return out


def adjoint(upstream, state, rho, inverse, rate):
    moments = [total([WEIGHTS[q] * upstream[s][q] for q in range(7)]) for s in range(2)]
    contrast = moments[1] - moments[0]
    scaled = rate * contrast
    earlier, relax = [], []
    for s in range(2):
        keep = 1.0 - inverse[s]
        add = moments[s] * inverse[s] + scaled * rho[1 - s]
        earlier.append([keep * upstream[s][q] + add for q in range(7)])
        part = total([upstream[s][q] * (state[s][q] - WEIGHTS[q] * rho[s]) for q in range(7)])
        relax.append(part * inverse[s] * inverse[s])
    return earlier, rho[0] * rho[1] * contrast, relax


def second_kernel(
    f_ref, g_ref, r_ref, t_ref, below_ref, above_ref, y_ref, z_ref, near_ref, back_ref,
    later_ref, rate_ref, relax_ref, deep_ref, up_ref, down_ref, y1_ref, y2_ref, z1_ref, z2_ref,
):
    even = parities()
    nx = r_ref.shape[0]
    c, _, inverse, rate = collided(f_ref, r_ref, t_ref)
    y1 = jnp.where(even[0], near_ref[0:16], back_ref[0:16])
    z1 = jnp.where(even[0], back_ref[0:8], near_ref[0:8])
    y2 = jnp.where(even[0], y_ref[0:80], back_ref[16:96])
    z2 = jnp.where(even[0], back_ref[16:32], z_ref[0:16])
    deep_ref[0:80] = y2
    deep_ref[80:96] = z2
    above = [[above_ref[16 * k : 16 * k + 16] for k in range(4)]]
    below = [[below_ref[16 * k : 16 * k + 16] for k in range(4)]]
    for axis, a, b in ((1, y1, y2[0:16]), (2, z1, z2[0:8])):
        above.append(jnp.where(even[axis], a, b))
        below.append(jnp.where(even[axis], b, a))
    upstream = [[load(g_ref, s, 0)] for s in range(2)]
    middle = [[c[s][0]] for s in range(2)]
    for s in range(2):
        for axis in range(3):
            p, m = 1 + 2 * axis, 2 + 2 * axis
            upstream[s].append(moved(load(g_ref, s, p), axis, 1, above[axis], s))
            upstream[s].append(moved(load(g_ref, s, m), axis, -1, below[axis], s))
            middle[s].append(moved(c[s][p], axis, -1, below[axis], 2 + s))
            middle[s].append(moved(c[s][m], axis, 1, above[axis], 2 + s))
    later = [[[None] * nx for _ in range(7)] for _ in range(2)]
    for x in range(nx):
        up = [[upstream[s][q][x] for q in range(7)] for s in range(2)]
        mid = [[middle[s][q][x] for q in range(7)] for s in range(2)]
        rho = [total(mid[s]) for s in range(2)]
        earlier, rate_part, relax_part = adjoint(up, mid, rho, [inverse[s][x] for s in range(2)], rate[x])
        rate_ref[x] = rate_part
        for s in range(2):
            relax_ref[s, x] = relax_part[s]
            for q in range(7):
                later[s][q][x] = earlier[s][q]
                later_ref[s, q, x] = earlier[s][q]
    for ref, last in ((up_ref, True), (down_ref, False)):
        for s, face in enumerate(pack_x([later[s][2 if last else 1] for s in range(2)], last)):
            ref[16 * s : 16 * s + 16] = face
        ref[32:40] = y2[52:60]
        ref[40:48] = z2[8:16]
    for axis, pack, first, second in ((1, pack_y, y1_ref, y2_ref), (2, pack_z, z1_ref, z2_ref)):
        a = pack([later[s][2 + 2 * axis] for s in range(2)], True)
        b = pack([later[s][1 + 2 * axis] for s in range(2)], False)
        first[0:8] = jnp.where(even[axis], a, b)
        second[0:8] = jnp.where(even[axis], b, a)
    for ref in (y1_ref, y2_ref):
        ref[8:16] = z2[8:16]
    for ref in (z1_ref, z2_ref):
        ref[8:24] = y2[64:80]


def later_beyond(inner, moments, density, inverse, rate):
    scaled = rate * (moments[1] - moments[0])
    return [(1.0 - inverse[s]) * inner[s] + moments[s] * inverse[s] + scaled * density[1 - s] for s in range(2)]


def beyond_y(deep, own, x_above, x_below, z_above, z_below):
    nx = 4
    field = lambda k: deep[16 + nx * k : 16 + nx * k + nx]
    lane = lax.broadcasted_iota(jnp.int32, (nx, 128), 1)
    added = []
    for k in range(4):
        zero = jnp.zeros((nx - 2, 128), jnp.float32)
        x_part = jnp.concatenate([x_below[2 * k + 1 : 2 * k + 2], zero, x_above[2 * k : 2 * k + 1]], axis=0)
        high = pltpu.roll(z_above[nx * k : nx * k + nx], 127, axis=1)
        low = pltpu.roll(z_below[nx * k : nx * k + nx], 1, axis=1)
        z_part = jnp.where(lane == 127, high, jnp.where(lane == 0, low, 0.0))
        added.append(own[nx * k : nx * k + nx] + x_part + z_part)
    moments = [field(2 + s) + WEIGHTS[1] * added[s] for s in range(2)]
    density = [field(4 + s) + added[2 + s] for s in range(2)]
    out = later_beyond([field(0), field(1)], moments, density, [field(6), field(7)], field(8))
    return jnp.concatenate(out, axis=0)


def beyond_z(deep, own, x_above, x_below, y_above, y_below):
    lane = lax.broadcasted_iota(jnp.int32, (8, 128), 1)
    row = lax.broadcasted_iota(jnp.int32, (8, 128), 0)

    def at(v, shift):
        shift = shift % 128
        return pltpu.roll(v, shift, axis=1) if shift else v

    field = lambda k: at(deep, -32 - 8 * k)
    odd = lax.rem(lane, 2) == 1
    y_high, y_low = pltpu.roll(y_above, 7, axis=0), pltpu.roll(y_below, 1, axis=0)
    added = []
    for k in range(4):
        x_part = jnp.where(lane >= 6, at(x_above, 6 - 32 - 8 * k), 0.0)
        x_part = jnp.where(lane < 2, at(x_below, -6 - 32 - 8 * k), x_part)
        y_part = jnp.where((row == 7) & odd, at(y_high, 1 - 8 * k), 0.0)
        y_part = jnp.where((row == 0) & ~odd, at(y_low, -1 - 8 * k), y_part)
        added.append(at(own, -8 * k) + x_part + y_part)
    moments = [field(2 + s) + WEIGHTS[1] * added[s] for s in range(2)]
    density = [field(4 + s) + added[2 + s] for s in range(2)]
    out = later_beyond([field(0), field(1)], moments, density, [field(6), field(7)], field(8))
    return jnp.where(lane < 8, out[0], pltpu.roll(out[1], 8, axis=1))


def third_kernel(
    f_ref, r_ref, t_ref, later_ref, rate_late_ref, relax_late_ref, deep_ref, raw_ref, diag_ref,
    below_ref, above_ref, y1_ref, y2_ref, z1_ref, z2_ref, state_ref, rate_ref, relax_ref,
):
    even = parities()
    nx = r_ref.shape[0]
    far_y = far_along_y(lax.axis_index("gy"), lax.axis_size("gy"))
    far_z = far_along_z(lax.axis_index("gz"), lax.axis_size("gz"))
    lines1, lines2 = z1_ref[8:24], jnp.where(far_z, diag_ref[0:16], z2_ref[8:24])
    y2 = beyond_y(
        deep_ref[0:80], raw_ref[0:16], above_ref[32:40], below_ref[32:40],
        jnp.where(even[2], lines1, lines2), jnp.where(even[2], lines2, lines1),
    )
    lines1, lines2 = y1_ref[8:16], jnp.where(far_y, diag_ref[16:24], y2_ref[8:16])
    z2 = beyond_z(
        deep_ref[80:88], raw_ref[16:24], above_ref[40:48], below_ref[40:48],
        jnp.where(even[1], lines1, lines2), jnp.where(even[1], lines2, lines1),
    )
    y2 = jnp.where(far_y, y2, y2_ref[0:8])
    z2 = jnp.where(far_z, z2, z2_ref[0:8])
    above = [[above_ref[16 * k : 16 * k + 16] for k in range(2)]]
    below = [[below_ref[16 * k : 16 * k + 16] for k in range(2)]]
    for axis, a, b in ((1, y1_ref[0:8], y2), (2, z1_ref[0:8], z2)):
        above.append(jnp.where(even[axis], a, b))
        below.append(jnp.where(even[axis], b, a))
    upstream = [[load(later_ref, s, 0)] for s in range(2)]
    for s in range(2):
        for axis in range(3):
            upstream[s].append(moved(load(later_ref, s, 1 + 2 * axis), axis, 1, above[axis], s))
            upstream[s].append(moved(load(later_ref, s, 2 + 2 * axis), axis, -1, below[axis], s))
    for x in range(nx):
        up = [[upstream[s][q][x] for q in range(7)] for s in range(2)]
        state = [[f_ref[s, q, x] for q in range(7)] for s in range(2)]
        rho = [total(state[s]) for s in range(2)]
        inverse = [1.0 / t_ref[s, x] for s in range(2)]
        earlier, rate_part, relax_part = adjoint(up, state, rho, inverse, r_ref[x])
        rate_ref[x] = rate_late_ref[x] + rate_part
        for s in range(2):
            relax_ref[s, x] = relax_late_ref[s, x] + relax_part[s]
            for q in range(7):
                state_ref[s, q, x] = earlier[s][q]


def call(kernel, shapes, *args, source=pltpu.VMEM, scratch=()):
    return pl.pallas_call(
        kernel,
        out_shape=[jax.ShapeDtypeStruct(s, jnp.float32) for s in shapes],
        in_specs=[pl.BlockSpec(memory_space=source)] * len(args),
        out_specs=[pl.BlockSpec(memory_space=pltpu.VMEM)] * len(shapes),
        scratch_shapes=list(scratch),
        compiler_params=pltpu.CompilerParams(vmem_limit_bytes=32 * 1024 * 1024),
    )(*args)


def shifts(axis):
    count = lax.axis_size(axis)
    up = [(i, (i + 1) % count) for i in range(count)]
    return up, [(j, i) for i, j in up]


def far_along_y(index, count):
    return (index == 0) | (index == count - 1)


def far_along_z(index, count):
    half = count // 2
    return (index % half == 0) | (index % half == half - 1)


def grid_pairs(move):
    counts = tuple(lax.axis_size(a) for a in AXES)
    nx, ny, nz = counts
    pairs = []
    for x in range(nx):
        for y in range(ny):
            for z in range(nz):
                to = move(x, y, z, counts)
                if to is not None:
                    pairs.append(((x * ny + y) * nz + z, (to[0] * ny + to[1]) * nz + to[2]))
    return pairs


def near_move(x, y, z, counts):
    return (x, partner(y, counts[1], 0), z) if x % 2 == 0 else (x, y, partner(z, counts[2], 0))


def second_y_move(x, y, z, counts):
    return (x, partner(y, counts[1], 1), z) if x % 2 == 0 else None


def second_z_move(x, y, z, counts):
    return (x, y, partner(z, counts[2], 1)) if x % 2 == 1 else None


def diagonal_move(x, y, z, counts):
    if far_along_y(y, counts[1]) and far_along_z(z, counts[2]):
        return (x, partner(y, counts[1], 1), partner(z, counts[2], 1))
    return None


def first_exchange(up, down, own0, own1, diag):
    to_up, to_down = shifts("gx")
    below = lax.ppermute(up, "gx", to_up)
    above = lax.ppermute(down, "gx", to_down)
    y, z, near = call(forward_kernel, [(160, 128), (32, 128), (32, 128)], own0, own1, below, above)
    y_in = lax.ppermute(y, AXES, grid_pairs(second_y_move))
    z_in = lax.ppermute(z, AXES, grid_pairs(second_z_move))
    diag_in = lax.ppermute(diag, AXES, grid_pairs(diagonal_move))
    near_in = lax.ppermute(near, AXES, grid_pairs(near_move))
    (back,) = call(back_kernel, [(96, 128)], y_in, z_in, near_in)
    back_in = lax.ppermute(back, "gx", axis_pairs("gx", 0))
    return (below, above, y_in, z_in, near_in, back_in), diag_in


def second_exchange(up, down, y1, y2, z1, z2):
    to_up, to_down = shifts("gx")
    below = lax.ppermute(up, "gx", to_up)
    above = lax.ppermute(down, "gx", to_down)
    received = [below, above]
    for axis, far, a, b in (("gy", far_along_y, y1, y2), ("gz", far_along_z, z1, z2)):
        count = lax.axis_size(axis)
        received.append(lax.ppermute(a, axis, axis_pairs(axis, 0)))
        near = [(i, j) for i, j in axis_pairs(axis, 1) if not far(i, count)]
        received.append(lax.ppermute(b, axis, near))
    return received


def on_device(checkpoint, cotangent, reaction_rate, relax_time):
    inputs = (checkpoint, cotangent, reaction_rate, relax_time)
    messages = [(160, 128), (160, 128), (16, 128), (80, 128), (24, 128), (24, 128)]
    f, g, r, t, *sent, raw = call(
        first_kernel, [a.shape for a in inputs] + messages,
        *(pltpu.with_memory_space_constraint(a, pltpu.HBM) for a in inputs),
        source=pltpu.HBM, scratch=[pltpu.SemaphoreType.DMA((4,))],
    )
    received, diag_in = first_exchange(*sent)
    messages = [(96, 128), (48, 128), (48, 128), (16, 128), (16, 128), (24, 128), (24, 128)]
    later, rate_late, relax_late, deep, *sent = call(
        second_kernel, [f.shape, r.shape, t.shape] + messages, f, g, r, t, *received
    )
    received = second_exchange(*sent)
    return tuple(
        call(
            third_kernel, [f.shape, r.shape, t.shape],
            f, r, t, later, rate_late, relax_late, deep, raw, diag_in, *received,
        )
    )


def solution(mesh):
    placed = (
        P(None, None, "gx", "gy", "gz"),
        P(None, None, "gx", "gy", "gz"),
        P("gx", "gy", "gz"),
        P(None, "gx", "gy", "gz"),
    )
    return jax.shard_map(
        on_device,
        mesh=mesh,
        in_specs=placed,
        out_specs=(P(None, None, "gx", "gy", "gz"), P("gx", "gy", "gz"), P(None, "gx", "gy", "gz")),
        check_vma=False,
    )
```

time: 58.2 us -> 56.9 us (0.978)
  the two profiles are of different devices: /device:TPU:1 before, /device:TPU:48 now
where the time goes in v3:
time: 56.9 us; the launch traced here: 56.6 us
  starting transfers between devices  44.8 us (79%)
  waiting for transfers between devices  7.64 us (13%)
  Pallas kernels  3.33 us (6%)
  between operations  0.78 us (1%)
    ppermute x2, starting transfers between devices, second_exchange(): received.append(lax.ppermute(a, axis, axis_pairs(axis, 0)))  12.5 us
    ppermute x1, starting transfers between devices, first_exchange(): near_in = lax.ppermute(near, AXES, grid_pairs(near_move))  11.3 us
    ppermute x2, starting transfers between devices, second_exchange(): received.append(lax.ppermute(b, axis, near))  6.24 us
    ppermute x1, starting transfers between devices, first_exchange(): y_in = lax.ppermute(y, AXES, grid_pairs(second_y_move))  3.83 us
    ppermute x1, starting transfers between devices, first_exchange(): back_in = lax.ppermute(back, 'gx', axis_pairs('gx', 0))  3.65 us
    ppermute x2, waiting for transfers between devices, second_exchange(): received.append(lax.ppermute(b, axis, near))  3.62 us
    pallas_call x5, Pallas kernels, call(): pl.pallas_call(kernel, out_shape=[jax.ShapeDtypeStruct(s, jnp.float32) fo...  3.33 us
    ppermute x1, starting transfers between devices, first_exchange(): above = lax.ppermute(down, 'gx', to_down)  2.94 us
  transfers between devices with their start and end apart: 13, of which 4 were waited for; matrix products, arithmetic and copies ran while one was open for 0% of the time, Pallas kernels for 1%

profile of v3, /device:TPU:48, one launch (start us, length us, event | category | flops | bytes accessed | tf_op | source)
XLA Modules:
  0.0 56.6 jit_solution(8984136134274124030)
XLA Ops:
  0.6 1.8 %shard_map.67 = (f32[2,7,4,16,128]{4,3,2,1,0:T(8,128)S(1)}, f32[2,7,4,16,128]{4,3,2,1,0:T(8,128)S(1)}, f32[4,16,128]{2,1,0:T(8,128)S(1)}, f32[2,4,16,128]{3,2,1,...) custom-call(f32[2,7,4,16,128]{4,3,2,1,0:T(8,128)} %f_hbm.1, ...), custom_call_target="tpu_custom_call" | custom-call | tf_op jit(solution)/shard_map/pallas_call | solution.py:395
  2.4 0.0 collective-permute-start
  2.4 2.9 %collective-permute-start.1 = (f32[160,128]{1,0:T(8,128)S(1)}, f32[160,128]{1,0:T(8,128)S(1)}, u32[]{:S(2)}, u32[]{:S(2)}) collective-permute-start(f32[160,128]{1,0:T(8,128)S(1)} %get-tuple-element.31), channel_id=1, source_target_pairs={{64,0},{128,64},{192,128},{256,192},{320,256},{384,320},{448,384},... | collective-permute-start | bytes 245768 | tf_op jit(solution)/shard_map/ppermute | solution.py:454
  5.4 2.1 %collective-permute-done.below_ref = f32[160,128]{1,0:T(8,128)S(1)} collective-permute-done((f32[160,128]{1,0:T(8,128)S(1)}, f32[160,128]{1,0:T(8,128)S(1)}, u32[]{:S(2)}, u32[]{:S(2)}) %collective-permute-start) | collective-permute-done | bytes 81952 | tf_op jit(solution)/shard_map/ppermute | solution.py:453
  7.5 0.0 collective-permute-done.1.above_ref
  7.5 3.8 %collective-permute-start.2 = (f32[160,128]{1,0:T(8,128)S(1)}, f32[160,128]{1,0:T(8,128)S(1)}, u32[]{:S(2)}, u32[]{:S(2)}) collective-permute-start(f32[160,128]{1,0:T(8,128)S(1)} %get-tuple-element.34), channel_id=1, source_target_pairs={{0,56},{1,57},{2,58},{3,59},{4,60},{5,61},{6,62},{7,63},{8,16},{9,... | collective-permute-start | bytes 245768 | tf_op jit(solution)/shard_map/ppermute | solution.py:456
  11.4 0.7 %collective-permute-start.3 = (f32[32,128]{1,0:T(8,128)S(1)}, f32[32,128]{1,0:T(8,128)S(1)}, u32[]{:S(2)}, u32[]{:S(2)}) collective-permute-start(f32[32,128]{1,0:T(8,128)S(1)} %get-tuple-element.35), channel_id=1, source_target_pairs={{64,71},{65,66},{66,65},{67,68},{68,67},{69,70},{70,69},{71,64},{7... | collective-permute-start | bytes 49160 | tf_op jit(solution)/shard_map/ppermute | solution.py:457
  12.0 11.3 %collective-permute-start.4 = (f32[32,128]{1,0:T(8,128)S(1)}, f32[32,128]{1,0:T(8,128)S(1)}, u32[]{:S(2)}, u32[]{:S(2)}) collective-permute-start(f32[32,128]{1,0:T(8,128)S(1)} %get-tuple-element.36), channel_id=1, source_target_pairs={{0,8},{1,9},{2,10},{3,11},{4,12},{5,13},{6,14},{7,15},{8,0},{9,1},... | collective-permute-start | bytes 49160 | tf_op jit(solution)/shard_map/ppermute | solution.py:459
  23.4 0.0 collective-permute-done.3.z_ref
  23.4 1.7 %collective-permute-done.4.near_ref = f32[32,128]{1,0:T(8,128)S(1)} collective-permute-done((f32[32,128]{1,0:T(8,128)S(1)}, f32[32,128]{1,0:T(8,128)S(1)}, u32[]{:S(2)}, u32[]{:S(2)}) %collective-permute-start.4) | collective-permute-done | bytes 16416 | tf_op jit(solution)/shard_map/ppermute | solution.py:459
  25.1 0.0 collective-permute-done.2.y_ref
  25.1 3.7 %collective-permute-start.5 = (f32[96,128]{1,0:T(8,128)S(1)}, f32[96,128]{1,0:T(8,128)S(1)}, u32[]{:S(2)}, u32[]{:S(2)}) collective-permute-start(f32[96,128]{1,0:T(8,128)S(1)} %shard_map.69), channel_id=1, source_target_pairs={{0,64},{64,0},{128,192},{192,128},{256,320},{320,256},{384,448},{4... | collective-permute-start | bytes 147464 | tf_op jit(solution)/shard_map/ppermute | solution.py:461
  28.8 0.7 %collective-permute-start.6 = (f32[24,128]{1,0:T(8,128)S(1)}, f32[24,128]{1,0:T(8,128)S(1)}, u32[]{:S(2)}, u32[]{:S(2)}) collective-permute-start(f32[24,128]{1,0:T(8,128)S(1)} %get-tuple-element.42), channel_id=1, source_target_pairs={{0,63},{3,60},{4,59},{7,56},{56,7},{59,4},{60,3},{63,0},{64,127},{... | collective-permute-start | bytes 36872 | tf_op jit(solution)/shard_map/ppermute | solution.py:458
  29.4 0.2 collective-permute-done.5.back_ref
  29.6 0.4 shard_map.70
  30.0 0.4 collective-permute-start.7
  30.4 2.6 %collective-permute-start.8 = (f32[48,128]{1,0:T(8,128)S(1)}, f32[48,128]{1,0:T(8,128)S(1)}, u32[]{:S(2)}, u32[]{:S(2)}) collective-permute-start(f32[48,128]{1,0:T(8,128)S(1)} %get-tuple-element.44), channel_id=1, source_target_pairs={{64,0},{128,64},{192,128},{256,192},{320,256},{384,320},{448,384},... | collective-permute-start | bytes 73736 | tf_op jit(solution)/shard_map/ppermute | solution.py:468
  33.0 2.9 %collective-permute-start.9 = (f32[16,128]{1,0:T(8,128)S(1)}, f32[16,128]{1,0:T(8,128)S(1)}, u32[]{:S(2)}, u32[]{:S(2)}) collective-permute-start(f32[16,128]{1,0:T(8,128)S(1)} %get-tuple-element.45), channel_id=1, source_target_pairs={{0,8},{8,0},{16,24},{24,16},{32,40},{40,32},{48,56},{56,48},{1,9},... | collective-permute-start | bytes 24584 | tf_op jit(solution)/shard_map/ppermute | solution.py:472
  35.9 9.6 %collective-permute-start.11 = (f32[24,128]{1,0:T(8,128)S(1)}, f32[24,128]{1,0:T(8,128)S(1)}, u32[]{:S(2)}, u32[]{:S(2)}) collective-permute-start(f32[24,128]{1,0:T(8,128)S(1)} %get-tuple-element.47), channel_id=1, source_target_pairs={{0,1},{1,0},{2,3},{3,2},{4,5},{5,4},{6,7},{7,6},{8,9},{9,8},{10,11... | collective-permute-start | bytes 36872 | tf_op jit(solution)/shard_map/ppermute | solution.py:472
  45.5 0.0 collective-permute-done.6.diag_ref
  45.5 4.3 %collective-permute-start.12 = (f32[24,128]{1,0:T(8,128)S(1)}, f32[24,128]{1,0:T(8,128)S(1)}, u32[]{:S(2)}, u32[]{:S(2)}) collective-permute-start(f32[24,128]{1,0:T(8,128)S(1)} %get-tuple-element.48), channel_id=1, source_target_pairs={{1,2},{2,1},{5,6},{6,5},{9,10},{10,9},{13,14},{14,13},{17,18},{18,... | collective-permute-start | bytes 36872 | tf_op jit(solution)/shard_map/ppermute | solution.py:474
  49.8 0.0 collective-permute-done.9.y1_ref
  49.9 1.9 %collective-permute-start.10 = (f32[16,128]{1,0:T(8,128)S(1)}, f32[16,128]{1,0:T(8,128)S(1)}, u32[]{:S(2)}, u32[]{:S(2)}) collective-permute-start(f32[16,128]{1,0:T(8,128)S(1)} %get-tuple-element.46), channel_id=1, source_target_pairs={{8,16},{16,8},{24,32},{32,24},{40,48},{48,40},{9,17},{17,9},{25,33... | collective-permute-start | bytes 24584 | tf_op jit(solution)/shard_map/ppermute | solution.py:474
  51.8 3.6 %collective-permute-done.10.y2_ref = f32[16,128]{1,0:T(8,128)S(1)} collective-permute-done((f32[16,128]{1,0:T(8,128)S(1)}, f32[16,128]{1,0:T(8,128)S(1)}, u32[]{:S(2)}, u32[]{:S(2)}) %collective-permute-start.10) | collective-permute-done | bytes 8224 | tf_op jit(solution)/shard_map/ppermute | solution.py:474
  55.4 0.0 collective-permute-done.11.z1_ref
  55.4 0.0 collective-permute-done.12.z2_ref
  55.4 0.0 collective-permute-done.7.below_ref
  55.4 0.0 collective-permute-done.8.above_ref
  55.4 1.1 %shard_map.71 = (f32[2,7,4,16,128]{4,3,2,1,0:T(8,128)}, f32[4,16,128]{2,1,0:T(8,128)}, f32[2,4,16,128]{3,2,1,0:T(8,128)}) custom-call(f32[2,7,4,16,128]{4,3,2,1,0:T(8,128)S(1)} %get-tuple-element.26.f_ref, f32[4,16,128]{2,1,0:T(8,128)S(1)} %get-tuple-element.27.r_ref, f32[2,4,16,128]{3,2,1,0:T(8,128)S(1)} %get-tuple-element.28.t_ref, ...), custom_call_target="tpu_custom_call" | custom-call | tf_op jit(solution)/shard_map/pallas_call | solution.py:395
  (2 shorter events, 0.0 us)
Async XLA Ops:
  2.4 5.1 %collective-permute-start = (f32[160,128]{1,0:T(8,128)S(1)}, f32[160,128]{1,0:T(8,128)S(1)}, u32[]{:S(2)}, u32[]{:S(2)}) collective-permute-start(f32[160,128]{1,0:T(8,128)S(1)} %get-tuple-element.30), channel_id=1, source_target_pairs={{0,64},{64,128},{128,192},{192,256},{256,320},{320,384},{384,448},... | collective-permute-start | bytes 245768 | tf_op jit(solution)/shard_map/ppermute | solution.py:453
  2.4 5.1 %collective-permute-start.1 = (f32[160,128]{1,0:T(8,128)S(1)}, f32[160,128]{1,0:T(8,128)S(1)}, u32[]{:S(2)}, u32[]{:S(2)}) collective-permute-start(f32[160,128]{1,0:T(8,128)S(1)} %get-tuple-element.31), channel_id=1, source_target_pairs={{64,0},{128,64},{192,128},{256,192},{320,256},{384,320},{448,384},... | collective-permute-start | bytes 245768 | tf_op jit(solution)/shard_map/ppermute | solution.py:454
  7.5 17.6 %collective-permute-start.2 = (f32[160,128]{1,0:T(8,128)S(1)}, f32[160,128]{1,0:T(8,128)S(1)}, u32[]{:S(2)}, u32[]{:S(2)}) collective-permute-start(f32[160,128]{1,0:T(8,128)S(1)} %get-tuple-element.34), channel_id=1, source_target_pairs={{0,56},{1,57},{2,58},{3,59},{4,60},{5,61},{6,62},{7,63},{8,16},{9,... | collective-permute-start | bytes 245768 | tf_op jit(solution)/shard_map/ppermute | solution.py:456
  11.4 12.0 %collective-permute-start.3 = (f32[32,128]{1,0:T(8,128)S(1)}, f32[32,128]{1,0:T(8,128)S(1)}, u32[]{:S(2)}, u32[]{:S(2)}) collective-permute-start(f32[32,128]{1,0:T(8,128)S(1)} %get-tuple-element.35), channel_id=1, source_target_pairs={{64,71},{65,66},{66,65},{67,68},{68,67},{69,70},{70,69},{71,64},{7... | collective-permute-start | bytes 49160 | tf_op jit(solution)/shard_map/ppermute | solution.py:457
  12.0 13.1 %collective-permute-start.4 = (f32[32,128]{1,0:T(8,128)S(1)}, f32[32,128]{1,0:T(8,128)S(1)}, u32[]{:S(2)}, u32[]{:S(2)}) collective-permute-start(f32[32,128]{1,0:T(8,128)S(1)} %get-tuple-element.36), channel_id=1, source_target_pairs={{0,8},{1,9},{2,10},{3,11},{4,12},{5,13},{6,14},{7,15},{8,0},{9,1},... | collective-permute-start | bytes 49160 | tf_op jit(solution)/shard_map/ppermute | solution.py:459
  25.1 4.5 %collective-permute-start.5 = (f32[96,128]{1,0:T(8,128)S(1)}, f32[96,128]{1,0:T(8,128)S(1)}, u32[]{:S(2)}, u32[]{:S(2)}) collective-permute-start(f32[96,128]{1,0:T(8,128)S(1)} %shard_map.69), channel_id=1, source_target_pairs={{0,64},{64,0},{128,192},{192,128},{256,320},{320,256},{384,448},{4... | collective-permute-start | bytes 147464 | tf_op jit(solution)/shard_map/ppermute | solution.py:461
  28.8 16.7 %collective-permute-start.6 = (f32[24,128]{1,0:T(8,128)S(1)}, f32[24,128]{1,0:T(8,128)S(1)}, u32[]{:S(2)}, u32[]{:S(2)}) collective-permute-start(f32[24,128]{1,0:T(8,128)S(1)} %get-tuple-element.42), channel_id=1, source_target_pairs={{0,63},{3,60},{4,59},{7,56},{56,7},{59,4},{60,3},{63,0},{64,127},{... | collective-permute-start | bytes 36872 | tf_op jit(solution)/shard_map/ppermute | solution.py:458
  30.0 25.4 %collective-permute-start.7 = (f32[48,128]{1,0:T(8,128)S(1)}, f32[48,128]{1,0:T(8,128)S(1)}, u32[]{:S(2)}, u32[]{:S(2)}) collective-permute-start(f32[48,128]{1,0:T(8,128)S(1)} %get-tuple-element.43), channel_id=1, source_target_pairs={{0,64},{64,128},{128,192},{192,256},{256,320},{320,384},{384,448},... | collective-permute-start | bytes 73736 | tf_op jit(solution)/shard_map/ppermute | solution.py:467
  30.4 25.0 %collective-permute-start.8 = (f32[48,128]{1,0:T(8,128)S(1)}, f32[48,128]{1,0:T(8,128)S(1)}, u32[]{:S(2)}, u32[]{:S(2)}) collective-permute-start(f32[48,128]{1,0:T(8,128)S(1)} %get-tuple-element.44), channel_id=1, source_target_pairs={{64,0},{128,64},{192,128},{256,192},{320,256},{384,320},{448,384},... | collective-permute-start | bytes 73736 | tf_op jit(solution)/shard_map/ppermute | solution.py:468
  33.0 16.9 %collective-permute-start.9 = (f32[16,128]{1,0:T(8,128)S(1)}, f32[16,128]{1,0:T(8,128)S(1)}, u32[]{:S(2)}, u32[]{:S(2)}) collective-permute-start(f32[16,128]{1,0:T(8,128)S(1)} %get-tuple-element.45), channel_id=1, source_target_pairs={{0,8},{8,0},{16,24},{24,16},{32,40},{40,32},{48,56},{56,48},{1,9},... | collective-permute-start | bytes 24584 | tf_op jit(solution)/shard_map/ppermute | solution.py:472
  35.9 19.5 %collective-permute-start.11 = (f32[24,128]{1,0:T(8,128)S(1)}, f32[24,128]{1,0:T(8,128)S(1)}, u32[]{:S(2)}, u32[]{:S(2)}) collective-permute-start(f32[24,128]{1,0:T(8,128)S(1)} %get-tuple-element.47), channel_id=1, source_target_pairs={{0,1},{1,0},{2,3},{3,2},{4,5},{5,4},{6,7},{7,6},{8,9},{9,8},{10,11... | collective-permute-start | bytes 36872 | tf_op jit(solution)/shard_map/ppermute | solution.py:472
  45.5 9.9 %collective-permute-start.12 = (f32[24,128]{1,0:T(8,128)S(1)}, f32[24,128]{1,0:T(8,128)S(1)}, u32[]{:S(2)}, u32[]{:S(2)}) collective-permute-start(f32[24,128]{1,0:T(8,128)S(1)} %get-tuple-element.48), channel_id=1, source_target_pairs={{1,2},{2,1},{5,6},{6,5},{9,10},{10,9},{13,14},{14,13},{17,18},{18,... | collective-permute-start | bytes 36872 | tf_op jit(solution)/shard_map/ppermute | solution.py:474
  49.9 5.5 %collective-permute-start.10 = (f32[16,128]{1,0:T(8,128)S(1)}, f32[16,128]{1,0:T(8,128)S(1)}, u32[]{:S(2)}, u32[]{:S(2)}) collective-permute-start(f32[16,128]{1,0:T(8,128)S(1)} %get-tuple-element.46), channel_id=1, source_target_pairs={{8,16},{16,8},{24,32},{32,24},{40,48},{48,40},{9,17},{17,9},{25,33... | collective-permute-start | bytes 24584 | tf_op jit(solution)/shard_map/ppermute | solution.py:474

commit v4 on v3

--- a/solution.py
+++ b/solution.py
@@ -179,6 +179,7 @@
     raw_ref[16:24] = z2
     diag_ref[0:16] = y_lines
     diag_ref[16:24] = z_lines
+    diag_ref[24:40] = jnp.zeros((16, 128), jnp.float32)
     z1 = jnp.concatenate([z1, jnp.zeros_like(z1)], axis=0)
     y_all = jnp.concatenate([y_deep, y_lines], axis=0)
     z_all = jnp.concatenate([z_deep, z_lines, jnp.zeros((y_all.shape[0] - 16, 128), jnp.float32)], axis=0)
@@ -198,10 +199,12 @@
     y_ref[80:160] = share
     z_ref[0:16] = own1_ref[0:16]
     z_ref[16:32] = share[0:16]
-
-
-def back_kernel(y_ref, z_ref, near_ref, out_ref):
+    z_ref[32:48] = share[0:16]
+
+
+def back_kernel(z_ref, y_ref, diag_ref, near_ref, out_ref, lines_ref):
     even = parities()
+    lines_ref[...] = diag_ref[...]
     out_ref[0:16] = near_ref[16:32]
     out_ref[16:32] = jnp.where(even[0], y_ref[80:96], z_ref[16:32])
     out_ref[32:96] = y_ref[96:160]
@@ -247,7 +250,7 @@
 
 
 def second_kernel(
-    f_ref, g_ref, r_ref, t_ref, below_ref, above_ref, y_ref, z_ref, near_ref, back_ref,
+    f_ref, g_ref, r_ref, t_ref, below_ref, above_ref, z_ref, y_ref, near_ref, back_ref,
     later_ref, rate_ref, relax_ref, deep_ref, up_ref, down_ref, y1_ref, y2_ref, z1_ref, z2_ref,
 ):
     even = parities()
@@ -452,14 +455,14 @@
     to_up, to_down = shifts("gx")
     below = lax.ppermute(up, "gx", to_up)
     above = lax.ppermute(down, "gx", to_down)
-    y, z, near = call(forward_kernel, [(160, 128), (32, 128), (32, 128)], own0, own1, below, above)
+    y, z, near = call(forward_kernel, [(160, 128), (48, 128), (32, 128)], own0, own1, below, above)
+    z_in = lax.ppermute(z, AXES, grid_pairs(second_z_move))
     y_in = lax.ppermute(y, AXES, grid_pairs(second_y_move))
-    z_in = lax.ppermute(z, AXES, grid_pairs(second_z_move))
     diag_in = lax.ppermute(diag, AXES, grid_pairs(diagonal_move))
     near_in = lax.ppermute(near, AXES, grid_pairs(near_move))
-    (back,) = call(back_kernel, [(96, 128)], y_in, z_in, near_in)
+    back, lines = call(back_kernel, [(96, 128), diag.shape], z_in, y_in, diag_in, near_in)
     back_in = lax.ppermute(back, "gx", axis_pairs("gx", 0))
-    return (below, above, y_in, z_in, near_in, back_in), diag_in
+    return (below, above, z_in, y_in, near_in, back_in), lines
 
 
 def second_exchange(up, down, y1, y2, z1, z2):
@@ -477,7 +480,7 @@
 
 def on_device(checkpoint, cotangent, reaction_rate, relax_time):
     inputs = (checkpoint, cotangent, reaction_rate, relax_time)
-    messages = [(160, 128), (160, 128), (16, 128), (80, 128), (24, 128), (24, 128)]
+    messages = [(160, 128), (160, 128), (16, 128), (80, 128), (40, 128), (24, 128)]
     f, g, r, t, *sent, raw = call(
         first_kernel, [a.shape for a in inputs] + messages,
         *(pltpu.with_memory_space_constraint(a, pltpu.HBM) for a in inputs),

time: 56.9 us -> 54.8 us (0.963)
  starting transfers between devices: 44.8 us -> 42.1 us
  waiting for transfers between devices: 7.64 us -> 8.31 us
    ppermute x2, starting transfers between devices: 12.5 us -> 10.1 us  [second_exchange(): received.append(lax.ppermute(a, axis, axis_pairs(axis, 0)))]
    ppermute x1, waiting for transfers between devices: 0.19 us -> 0.86 us  [first_exchange(): back_in = lax.ppermute(back, 'gx', axis_pairs('gx', 0))]
  transfers between devices with their start and end apart: 13 -> 13, of which waited for: 4 -> 4; matrix products, arithmetic and copies ran while one was open for 0% -> 0% of each run, Pallas kernels for 1% -> 0%
where the time goes in v4:
time: 54.8 us; the launch traced here: 54.5 us
  starting transfers between devices  42.1 us (77%)
  waiting for transfers between devices  8.31 us (15%)
  Pallas kernels  3.32 us (6%)
  between operations  0.77 us (1%)
    ppermute x1, starting transfers between devices, first_exchange(): near_in = lax.ppermute(near, AXES, grid_pairs(near_move))  11.3 us
    ppermute x2, starting transfers between devices, second_exchange(): received.append(lax.ppermute(a, axis, axis_pairs(axis, 0)))  10.1 us
    ppermute x2, starting transfers between devices, second_exchange(): received.append(lax.ppermute(b, axis, near))  5.91 us
    ppermute x1, starting transfers between devices, first_exchange(): y_in = lax.ppermute(y, AXES, grid_pairs(second_y_move))  3.83 us
    ppermute x1, starting transfers between devices, first_exchange(): back_in = lax.ppermute(back, 'gx', axis_pairs('gx', 0))  3.65 us
    ppermute x2, waiting for transfers between devices, second_exchange(): received.append(lax.ppermute(b, axis, near))  3.62 us
    pallas_call x5, Pallas kernels, call(): pl.pallas_call(kernel, out_shape=[jax.ShapeDtypeStruct(s, jnp.float32) fo...  3.32 us
    ppermute x1, starting transfers between devices, first_exchange(): above = lax.ppermute(down, 'gx', to_down)  2.94 us
  transfers between devices with their start and end apart: 13, of which 4 were waited for; matrix products, arithmetic and copies ran while one was open for 0% of the time, Pallas kernels for 0%

profile of v4, /device:TPU:48, one launch (start us, length us, event | category | flops | bytes accessed | tf_op | source)
XLA Modules:
  0.0 54.5 jit_solution(697468576961877947)
XLA Ops:
  0.6 1.8 %shard_map.67 = (f32[2,7,4,16,128]{4,3,2,1,0:T(8,128)S(1)}, f32[2,7,4,16,128]{4,3,2,1,0:T(8,128)S(1)}, f32[4,16,128]{2,1,0:T(8,128)S(1)}, f32[2,4,16,128]{3,2,1,...) custom-call(f32[2,7,4,16,128]{4,3,2,1,0:T(8,128)} %f_hbm.1, ...), custom_call_target="tpu_custom_call" | custom-call | tf_op jit(solution)/shard_map/pallas_call | solution.py:398
  2.4 0.0 collective-permute-start
  2.4 2.9 %collective-permute-start.1 = (f32[160,128]{1,0:T(8,128)S(1)}, f32[160,128]{1,0:T(8,128)S(1)}, u32[]{:S(2)}, u32[]{:S(2)}) collective-permute-start(f32[160,128]{1,0:T(8,128)S(1)} %get-tuple-element.33), channel_id=1, source_target_pairs={{64,0},{128,64},{192,128},{256,192},{320,256},{384,320},{448,384},... | collective-permute-start | bytes 245768 | tf_op jit(solution)/shard_map/ppermute | solution.py:457
  5.4 2.1 %collective-permute-done.below_ref = f32[160,128]{1,0:T(8,128)S(1)} collective-permute-done((f32[160,128]{1,0:T(8,128)S(1)}, f32[160,128]{1,0:T(8,128)S(1)}, u32[]{:S(2)}, u32[]{:S(2)}) %collective-permute-start) | collective-permute-done | bytes 81952 | tf_op jit(solution)/shard_map/ppermute | solution.py:456
  7.5 0.0 collective-permute-done.1.above_ref
  7.5 3.8 %collective-permute-start.3 = (f32[160,128]{1,0:T(8,128)S(1)}, f32[160,128]{1,0:T(8,128)S(1)}, u32[]{:S(2)}, u32[]{:S(2)}) collective-permute-start(f32[160,128]{1,0:T(8,128)S(1)} %get-tuple-element.37), channel_id=1, source_target_pairs={{0,56},{1,57},{2,58},{3,59},{4,60},{5,61},{6,62},{7,63},{8,16},{9,... | collective-permute-start | bytes 245768 | tf_op jit(solution)/shard_map/ppermute | solution.py:460
  11.4 0.7 %collective-permute-start.2 = (f32[48,128]{1,0:T(8,128)S(1)}, f32[48,128]{1,0:T(8,128)S(1)}, u32[]{:S(2)}, u32[]{:S(2)}) collective-permute-start(f32[48,128]{1,0:T(8,128)S(1)} %get-tuple-element.36), channel_id=1, source_target_pairs={{64,71},{65,66},{66,65},{67,68},{68,67},{69,70},{70,69},{71,64},{7... | collective-permute-start | bytes 73736 | tf_op jit(solution)/shard_map/ppermute | solution.py:459
  12.0 0.7 %collective-permute-start.5 = (f32[40,128]{1,0:T(8,128)S(1)}, f32[40,128]{1,0:T(8,128)S(1)}, u32[]{:S(2)}, u32[]{:S(2)}) collective-permute-start(f32[40,128]{1,0:T(8,128)S(1)} %get-tuple-element.39), channel_id=1, source_target_pairs={{0,63},{3,60},{4,59},{7,56},{56,7},{59,4},{60,3},{63,0},{64,127},{... | collective-permute-start | bytes 61448 | tf_op jit(solution)/shard_map/ppermute | solution.py:461
  12.7 11.3 %collective-permute-start.4 = (f32[32,128]{1,0:T(8,128)S(1)}, f32[32,128]{1,0:T(8,128)S(1)}, u32[]{:S(2)}, u32[]{:S(2)}) collective-permute-start(f32[32,128]{1,0:T(8,128)S(1)} %get-tuple-element.38), channel_id=1, source_target_pairs={{0,8},{1,9},{2,10},{3,11},{4,12},{5,13},{6,14},{7,15},{8,0},{9,1},... | collective-permute-start | bytes 49160 | tf_op jit(solution)/shard_map/ppermute | solution.py:462
  24.1 0.0 collective-permute-done.5.diag_ref
  24.1 1.7 %collective-permute-done.4.near_ref = f32[32,128]{1,0:T(8,128)S(1)} collective-permute-done((f32[32,128]{1,0:T(8,128)S(1)}, f32[32,128]{1,0:T(8,128)S(1)}, u32[]{:S(2)}, u32[]{:S(2)}) %collective-permute-start.4) | collective-permute-done | bytes 16416 | tf_op jit(solution)/shard_map/ppermute | solution.py:462
  25.8 0.0 collective-permute-done.2.z_ref
  25.8 0.0 collective-permute-done.3.y_ref
  25.8 3.7 %collective-permute-start.6 = (f32[96,128]{1,0:T(8,128)S(1)}, f32[96,128]{1,0:T(8,128)S(1)}, u32[]{:S(2)}, u32[]{:S(2)}) collective-permute-start(f32[96,128]{1,0:T(8,128)S(1)} %get-tuple-element.40), channel_id=1, source_target_pairs={{0,64},{64,0},{128,192},{192,128},{256,320},{320,256},{384,448},{4... | collective-permute-start | bytes 147464 | tf_op jit(solution)/shard_map/ppermute | solution.py:464
  29.4 0.9 %collective-permute-done.6.back_ref = f32[96,128]{1,0:T(8,128)S(1)} collective-permute-done((f32[96,128]{1,0:T(8,128)S(1)}, f32[96,128]{1,0:T(8,128)S(1)}, u32[]{:S(2)}, u32[]{:S(2)}) %collective-permute-start.6) | collective-permute-done | bytes 49184 | tf_op jit(solution)/shard_map/ppermute | solution.py:464
  30.3 0.4 shard_map.70
  30.7 0.4 collective-permute-start.7
  31.1 2.6 %collective-permute-start.8 = (f32[48,128]{1,0:T(8,128)S(1)}, f32[48,128]{1,0:T(8,128)S(1)}, u32[]{:S(2)}, u32[]{:S(2)}) collective-permute-start(f32[48,128]{1,0:T(8,128)S(1)} %get-tuple-element.48), channel_id=1, source_target_pairs={{64,0},{128,64},{192,128},{256,192},{320,256},{384,320},{448,384},... | collective-permute-start | bytes 73736 | tf_op jit(solution)/shard_map/ppermute | solution.py:471
  33.7 6.4 %collective-permute-start.9 = (f32[16,128]{1,0:T(8,128)S(1)}, f32[16,128]{1,0:T(8,128)S(1)}, u32[]{:S(2)}, u32[]{:S(2)}) collective-permute-start(f32[16,128]{1,0:T(8,128)S(1)} %get-tuple-element.49), channel_id=1, source_target_pairs={{0,8},{8,0},{16,24},{24,16},{32,40},{40,32},{48,56},{56,48},{1,9},... | collective-permute-start | bytes 24584 | tf_op jit(solution)/shard_map/ppermute | solution.py:475
  40.1 3.6 %collective-permute-start.11 = (f32[24,128]{1,0:T(8,128)S(1)}, f32[24,128]{1,0:T(8,128)S(1)}, u32[]{:S(2)}, u32[]{:S(2)}) collective-permute-start(f32[24,128]{1,0:T(8,128)S(1)} %get-tuple-element.51), channel_id=1, source_target_pairs={{0,1},{1,0},{2,3},{3,2},{4,5},{5,4},{6,7},{7,6},{8,9},{9,8},{10,11... | collective-permute-start | bytes 36872 | tf_op jit(solution)/shard_map/ppermute | solution.py:475
  43.7 4.0 %collective-permute-start.12 = (f32[24,128]{1,0:T(8,128)S(1)}, f32[24,128]{1,0:T(8,128)S(1)}, u32[]{:S(2)}, u32[]{:S(2)}) collective-permute-start(f32[24,128]{1,0:T(8,128)S(1)} %get-tuple-element.52), channel_id=1, source_target_pairs={{1,2},{2,1},{5,6},{6,5},{9,10},{10,9},{13,14},{14,13},{17,18},{18,... | collective-permute-start | bytes 36872 | tf_op jit(solution)/shard_map/ppermute | solution.py:477
  47.7 0.0 collective-permute-done.9.y1_ref
  47.7 1.9 %collective-permute-start.10 = (f32[16,128]{1,0:T(8,128)S(1)}, f32[16,128]{1,0:T(8,128)S(1)}, u32[]{:S(2)}, u32[]{:S(2)}) collective-permute-start(f32[16,128]{1,0:T(8,128)S(1)} %get-tuple-element.50), channel_id=1, source_target_pairs={{8,16},{16,8},{24,32},{32,24},{40,48},{48,40},{9,17},{17,9},{25,33... | collective-permute-start | bytes 24584 | tf_op jit(solution)/shard_map/ppermute | solution.py:477
  49.7 3.6 %collective-permute-done.10.y2_ref = f32[16,128]{1,0:T(8,128)S(1)} collective-permute-done((f32[16,128]{1,0:T(8,128)S(1)}, f32[16,128]{1,0:T(8,128)S(1)}, u32[]{:S(2)}, u32[]{:S(2)}) %collective-permute-start.10) | collective-permute-done | bytes 8224 | tf_op jit(solution)/shard_map/ppermute | solution.py:477
  53.3 0.0 collective-permute-done.11.z1_ref
  53.3 0.0 collective-permute-done.12.z2_ref
  53.3 0.0 collective-permute-done.7.below_ref
  53.3 0.0 collective-permute-done.8.above_ref
  53.3 1.1 %shard_map.71 = (f32[2,7,4,16,128]{4,3,2,1,0:T(8,128)}, f32[4,16,128]{2,1,0:T(8,128)}, f32[2,4,16,128]{3,2,1,0:T(8,128)}) custom-call(f32[2,7,4,16,128]{4,3,2,1,0:T(8,128)S(1)} %get-tuple-element.28.f_ref, f32[4,16,128]{2,1,0:T(8,128)S(1)} %get-tuple-element.29.r_ref, f32[2,4,16,128]{3,2,1,0:T(8,128)S(1)} %get-tuple-element.30.t_ref, ...), custom_call_target="tpu_custom_call" | custom-call | tf_op jit(solution)/shard_map/pallas_call | solution.py:398
  (2 shorter events, 0.0 us)
Async XLA Ops:
  2.4 5.1 %collective-permute-start = (f32[160,128]{1,0:T(8,128)S(1)}, f32[160,128]{1,0:T(8,128)S(1)}, u32[]{:S(2)}, u32[]{:S(2)}) collective-permute-start(f32[160,128]{1,0:T(8,128)S(1)} %get-tuple-element.32), channel_id=1, source_target_pairs={{0,64},{64,128},{128,192},{192,256},{256,320},{320,384},{384,448},... | collective-permute-start | bytes 245768 | tf_op jit(solution)/shard_map/ppermute | solution.py:456
  2.4 5.1 %collective-permute-start.1 = (f32[160,128]{1,0:T(8,128)S(1)}, f32[160,128]{1,0:T(8,128)S(1)}, u32[]{:S(2)}, u32[]{:S(2)}) collective-permute-start(f32[160,128]{1,0:T(8,128)S(1)} %get-tuple-element.33), channel_id=1, source_target_pairs={{64,0},{128,64},{192,128},{256,192},{320,256},{384,320},{448,384},... | collective-permute-start | bytes 245768 | tf_op jit(solution)/shard_map/ppermute | solution.py:457
  7.5 18.2 %collective-permute-start.3 = (f32[160,128]{1,0:T(8,128)S(1)}, f32[160,128]{1,0:T(8,128)S(1)}, u32[]{:S(2)}, u32[]{:S(2)}) collective-permute-start(f32[160,128]{1,0:T(8,128)S(1)} %get-tuple-element.37), channel_id=1, source_target_pairs={{0,56},{1,57},{2,58},{3,59},{4,60},{5,61},{6,62},{7,63},{8,16},{9,... | collective-permute-start | bytes 245768 | tf_op jit(solution)/shard_map/ppermute | solution.py:460
  11.4 14.4 %collective-permute-start.2 = (f32[48,128]{1,0:T(8,128)S(1)}, f32[48,128]{1,0:T(8,128)S(1)}, u32[]{:S(2)}, u32[]{:S(2)}) collective-permute-start(f32[48,128]{1,0:T(8,128)S(1)} %get-tuple-element.36), channel_id=1, source_target_pairs={{64,71},{65,66},{66,65},{67,68},{68,67},{69,70},{70,69},{71,64},{7... | collective-permute-start | bytes 73736 | tf_op jit(solution)/shard_map/ppermute | solution.py:459
  12.0 12.0 %collective-permute-start.5 = (f32[40,128]{1,0:T(8,128)S(1)}, f32[40,128]{1,0:T(8,128)S(1)}, u32[]{:S(2)}, u32[]{:S(2)}) collective-permute-start(f32[40,128]{1,0:T(8,128)S(1)} %get-tuple-element.39), channel_id=1, source_target_pairs={{0,63},{3,60},{4,59},{7,56},{56,7},{59,4},{60,3},{63,0},{64,127},{... | collective-permute-start | bytes 61448 | tf_op jit(solution)/shard_map/ppermute | solution.py:461
  12.7 13.1 %collective-permute-start.4 = (f32[32,128]{1,0:T(8,128)S(1)}, f32[32,128]{1,0:T(8,128)S(1)}, u32[]{:S(2)}, u32[]{:S(2)}) collective-permute-start(f32[32,128]{1,0:T(8,128)S(1)} %get-tuple-element.38), channel_id=1, source_target_pairs={{0,8},{1,9},{2,10},{3,11},{4,12},{5,13},{6,14},{7,15},{8,0},{9,1},... | collective-permute-start | bytes 49160 | tf_op jit(solution)/shard_map/ppermute | solution.py:462
  25.8 4.5 %collective-permute-start.6 = (f32[96,128]{1,0:T(8,128)S(1)}, f32[96,128]{1,0:T(8,128)S(1)}, u32[]{:S(2)}, u32[]{:S(2)}) collective-permute-start(f32[96,128]{1,0:T(8,128)S(1)} %get-tuple-element.40), channel_id=1, source_target_pairs={{0,64},{64,0},{128,192},{192,128},{256,320},{320,256},{384,448},{4... | collective-permute-start | bytes 147464 | tf_op jit(solution)/shard_map/ppermute | solution.py:464
  30.7 22.6 %collective-permute-start.7 = (f32[48,128]{1,0:T(8,128)S(1)}, f32[48,128]{1,0:T(8,128)S(1)}, u32[]{:S(2)}, u32[]{:S(2)}) collective-permute-start(f32[48,128]{1,0:T(8,128)S(1)} %get-tuple-element.47), channel_id=1, source_target_pairs={{0,64},{64,128},{128,192},{192,256},{256,320},{320,384},{384,448},... | collective-permute-start | bytes 73736 | tf_op jit(solution)/shard_map/ppermute | solution.py:470
  31.1 22.3 %collective-permute-start.8 = (f32[48,128]{1,0:T(8,128)S(1)}, f32[48,128]{1,0:T(8,128)S(1)}, u32[]{:S(2)}, u32[]{:S(2)}) collective-permute-start(f32[48,128]{1,0:T(8,128)S(1)} %get-tuple-element.48), channel_id=1, source_target_pairs={{64,0},{128,64},{192,128},{256,192},{320,256},{384,320},{448,384},... | collective-permute-start | bytes 73736 | tf_op jit(solution)/shard_map/ppermute | solution.py:471
  33.7 14.1 %collective-permute-start.9 = (f32[16,128]{1,0:T(8,128)S(1)}, f32[16,128]{1,0:T(8,128)S(1)}, u32[]{:S(2)}, u32[]{:S(2)}) collective-permute-start(f32[16,128]{1,0:T(8,128)S(1)} %get-tuple-element.49), channel_id=1, source_target_pairs={{0,8},{8,0},{16,24},{24,16},{32,40},{40,32},{48,56},{56,48},{1,9},... | collective-permute-start | bytes 24584 | tf_op jit(solution)/shard_map/ppermute | solution.py:475
  40.1 13.2 %collective-permute-start.11 = (f32[24,128]{1,0:T(8,128)S(1)}, f32[24,128]{1,0:T(8,128)S(1)}, u32[]{:S(2)}, u32[]{:S(2)}) collective-permute-start(f32[24,128]{1,0:T(8,128)S(1)} %get-tuple-element.51), channel_id=1, source_target_pairs={{0,1},{1,0},{2,3},{3,2},{4,5},{5,4},{6,7},{7,6},{8,9},{9,8},{10,11... | collective-permute-start | bytes 36872 | tf_op jit(solution)/shard_map/ppermute | solution.py:475
  43.7 9.6 %collective-permute-start.12 = (f32[24,128]{1,0:T(8,128)S(1)}, f32[24,128]{1,0:T(8,128)S(1)}, u32[]{:S(2)}, u32[]{:S(2)}) collective-permute-start(f32[24,128]{1,0:T(8,128)S(1)} %get-tuple-element.52), channel_id=1, source_target_pairs={{1,2},{2,1},{5,6},{6,5},{9,10},{10,9},{13,14},{14,13},{17,18},{18,... | collective-permute-start | bytes 36872 | tf_op jit(solution)/shard_map/ppermute | solution.py:477
  47.7 5.5 %collective-permute-start.10 = (f32[16,128]{1,0:T(8,128)S(1)}, f32[16,128]{1,0:T(8,128)S(1)}, u32[]{:S(2)}, u32[]{:S(2)}) collective-permute-start(f32[16,128]{1,0:T(8,128)S(1)} %get-tuple-element.50), channel_id=1, source_target_pairs={{8,16},{16,8},{24,32},{32,24},{40,48},{48,40},{9,17},{17,9},{25,33... | collective-permute-start | bytes 24584 | tf_op jit(solution)/shard_map/ppermute | solution.py:477

commit v5 on v4

--- a/solution.py
+++ b/solution.py
@@ -204,7 +204,7 @@
 
 def back_kernel(z_ref, y_ref, diag_ref, near_ref, out_ref, lines_ref):
     even = parities()
-    lines_ref[...] = diag_ref[...]
+    lines_ref[...] = diag_ref[0:24]
     out_ref[0:16] = near_ref[16:32]
     out_ref[16:32] = jnp.where(even[0], y_ref[80:96], z_ref[16:32])
     out_ref[32:96] = y_ref[96:160]
@@ -251,7 +251,7 @@
 
 def second_kernel(
     f_ref, g_ref, r_ref, t_ref, below_ref, above_ref, z_ref, y_ref, near_ref, back_ref,
-    later_ref, rate_ref, relax_ref, deep_ref, up_ref, down_ref, y1_ref, y2_ref, z1_ref, z2_ref,
+    later_ref, rate_ref, relax_ref, deep_ref, up_ref, down_ref, y1_ref, z1_ref, relay_ref,
 ):
     even = parities()
     nx = r_ref.shape[0]
@@ -293,15 +293,16 @@
             ref[16 * s : 16 * s + 16] = face
         ref[32:40] = y2[52:60]
         ref[40:48] = z2[8:16]
-    for axis, pack, first, second in ((1, pack_y, y1_ref, y2_ref), (2, pack_z, z1_ref, z2_ref)):
+    for axis, pack, ref in ((1, pack_y, y1_ref), (2, pack_z, z1_ref)):
         a = pack([later[s][2 + 2 * axis] for s in range(2)], True)
         b = pack([later[s][1 + 2 * axis] for s in range(2)], False)
-        first[0:8] = jnp.where(even[axis], a, b)
-        second[0:8] = jnp.where(even[axis], b, a)
-    for ref in (y1_ref, y2_ref):
-        ref[8:16] = z2[8:16]
-    for ref in (z1_ref, z2_ref):
-        ref[8:24] = y2[64:80]
+        ref[0:8] = jnp.where(even[axis], a, b)
+    y1_ref[8:16] = z2[8:16]
+    z1_ref[8:24] = y2[64:80]
+    relay_ref[0:16] = y2[64:80]
+    relay_ref[16:24] = z2[8:16]
+    relay_ref[24:40] = y2[0:16]
+    relay_ref[40:48] = z2[0:8]
 
 
 def later_beyond(inner, moments, density, inverse, rate):
@@ -351,26 +352,43 @@
     return jnp.where(lane < 8, out[0], pltpu.roll(out[1], 8, axis=1))
 
 
+def z_lines_of(packed, last):
+    row, lane = (lax.broadcasted_iota(jnp.int32, (16, 128), d) for d in (0, 1))
+    edge = jnp.where(last, packed[7:8], packed[0:1])
+    wanted = lane == 2 * row + jnp.where(last, 1, 0)
+    return jnp.broadcast_to(jnp.sum(jnp.where(wanted, edge, 0.0), axis=1, keepdims=True), (16, 128))
+
+
+def y_lines_of(rows, last):
+    row, lane = (lax.broadcasted_iota(jnp.int32, (16, 128), d) for d in (0, 1))
+    wanted = lane == jnp.where(last, 127, 0)
+    edge = jnp.sum(jnp.where(wanted, rows, 0.0), axis=1, keepdims=True)
+    return jnp.broadcast_to(jnp.sum(jnp.where(lane // 2 == row, edge, 0.0), axis=0, keepdims=True), (8, 128))
+
+
 def third_kernel(
     f_ref, r_ref, t_ref, later_ref, rate_late_ref, relax_late_ref, deep_ref, raw_ref, diag_ref,
-    below_ref, above_ref, y1_ref, y2_ref, z1_ref, z2_ref, state_ref, rate_ref, relax_ref,
+    below_ref, above_ref, y1_ref, z1_ref, relay_ref, state_ref, rate_ref, relax_ref,
 ):
     even = parities()
     nx = r_ref.shape[0]
     far_y = far_along_y(lax.axis_index("gy"), lax.axis_size("gy"))
     far_z = far_along_z(lax.axis_index("gz"), lax.axis_size("gz"))
-    lines1, lines2 = z1_ref[8:24], jnp.where(far_z, diag_ref[0:16], z2_ref[8:24])
+    alike = far_y == far_z
+    lines1 = z1_ref[8:24]
+    lines2 = jnp.where(far_y, relay_ref[0:16], z_lines_of(relay_ref[40:48], even[1]))
+    lines2 = jnp.where(alike, diag_ref[0:16], lines2)
     y2 = beyond_y(
         deep_ref[0:80], raw_ref[0:16], above_ref[32:40], below_ref[32:40],
         jnp.where(even[2], lines1, lines2), jnp.where(even[2], lines2, lines1),
     )
-    lines1, lines2 = y1_ref[8:16], jnp.where(far_y, diag_ref[16:24], y2_ref[8:16])
+    lines1 = y1_ref[8:16]
+    lines2 = jnp.where(far_z, relay_ref[16:24], y_lines_of(relay_ref[24:40], even[2]))
+    lines2 = jnp.where(alike, diag_ref[16:24], lines2)
     z2 = beyond_z(
         deep_ref[80:88], raw_ref[16:24], above_ref[40:48], below_ref[40:48],
         jnp.where(even[1], lines1, lines2), jnp.where(even[1], lines2, lines1),
     )
-    y2 = jnp.where(far_y, y2, y2_ref[0:8])
-    z2 = jnp.where(far_z, z2, z2_ref[0:8])
     above = [[above_ref[16 * k : 16 * k + 16] for k in range(2)]]
     below = [[below_ref[16 * k : 16 * k + 16] for k in range(2)]]
     for axis, a, b in ((1, y1_ref[0:8], y2), (2, z1_ref[0:8], z2)):
@@ -446,9 +464,16 @@
 
 
 def diagonal_move(x, y, z, counts):
-    if far_along_y(y, counts[1]) and far_along_z(z, counts[2]):
+    if far_along_y(y, counts[1]) == far_along_z(z, counts[2]):
         return (x, partner(y, counts[1], 1), partner(z, counts[2], 1))
     return None
+
+
+def relay_move(x, y, z, counts):
+    far_y, far_z = far_along_y(y, counts[1]), far_along_z(z, counts[2])
+    if far_y and not far_z:
+        return (x, y, partner(z, counts[2], 1))
+    return (x, partner(y, counts[1], 1), z) if far_z and not far_y else None
 
 
 def first_exchange(up, down, own0, own1, diag):
@@ -460,22 +485,20 @@
     y_in = lax.ppermute(y, AXES, grid_pairs(second_y_move))
     diag_in = lax.ppermute(diag, AXES, grid_pairs(diagonal_move))
     near_in = lax.ppermute(near, AXES, grid_pairs(near_move))
-    back, lines = call(back_kernel, [(96, 128), diag.shape], z_in, y_in, diag_in, near_in)
+    back, lines = call(back_kernel, [(96, 128), (24, 128)], z_in, y_in, diag_in, near_in)
     back_in = lax.ppermute(back, "gx", axis_pairs("gx", 0))
     return (below, above, z_in, y_in, near_in, back_in), lines
 
 
-def second_exchange(up, down, y1, y2, z1, z2):
+def second_exchange(up, down, y1, z1, relay):
     to_up, to_down = shifts("gx")
-    below = lax.ppermute(up, "gx", to_up)
-    above = lax.ppermute(down, "gx", to_down)
-    received = [below, above]
-    for axis, far, a, b in (("gy", far_along_y, y1, y2), ("gz", far_along_z, z1, z2)):
-        count = lax.axis_size(axis)
-        received.append(lax.ppermute(a, axis, axis_pairs(axis, 0)))
-        near = [(i, j) for i, j in axis_pairs(axis, 1) if not far(i, count)]
-        received.append(lax.ppermute(b, axis, near))
-    return received
+    return (
+        lax.ppermute(up, "gx", to_up),
+        lax.ppermute(down, "gx", to_down),
+        lax.ppermute(y1, "gy", axis_pairs("gy", 0)),
+        lax.ppermute(z1, "gz", axis_pairs("gz", 0)),
+        lax.ppermute(relay, AXES, grid_pairs(relay_move)),
+    )
 
 
 def on_device(checkpoint, cotangent, reaction_rate, relax_time):
@@ -487,7 +510,7 @@
         source=pltpu.HBM, scratch=[pltpu.SemaphoreType.DMA((4,))],
     )
     received, diag_in = first_exchange(*sent)
-    messages = [(96, 128), (48, 128), (48, 128), (16, 128), (16, 128), (24, 128), (24, 128)]
+    messages = [(96, 128), (48, 128), (48, 128), (16, 128), (24, 128), (48, 128)]
     later, rate_late, relax_late, deep, *sent = call(
         second_kernel, [f.shape, r.shape, t.shape] + messages, f, g, r, t, *received
     )

time: 54.8 us -> 51.2 us (0.934)
  the two profiles are of different devices: /device:TPU:48 before, /device:TPU:8 now
where the time goes in v5:
time: 51.2 us; the launch traced here: 50.9 us
  starting transfers between devices  37.6 us (73%)
  waiting for transfers between devices  9.05 us (18%)
  Pallas kernels  3.46 us (7%)
  between operations  0.75 us (1%)
    ppermute x1, starting transfers between devices, first_exchange(): y_in = lax.ppermute(y, AXES, grid_pairs(second_y_move))  13.2 us
    ppermute x1, starting transfers between devices, first_exchange(): back_in = lax.ppermute(back, 'gx', axis_pairs('gx', 0))  5.86 us
    ppermute x1, starting transfers between devices, second_exchange(): lax.ppermute(relay, AXES, grid_pairs(relay_move))  3.78 us
    ppermute x1, waiting for transfers between devices, first_exchange(): near_in = lax.ppermute(near, AXES, grid_pairs(near_move))  3.69 us
    pallas_call x5, Pallas kernels, call(): pl.pallas_call(kernel, out_shape=[jax.ShapeDtypeStruct(s, jnp.float32) fo...  3.46 us
    ppermute x1, starting transfers between devices, second_exchange(): lax.ppermute(y1, 'gy', axis_pairs('gy', 0))  3.18 us
    ppermute x1, starting transfers between devices, first_exchange(): above = lax.ppermute(down, 'gx', to_down)  2.94 us
    ppermute x1, starting transfers between devices, second_exchange(): lax.ppermute(down, 'gx', to_down)  2.61 us
  transfers between devices with their start and end apart: 12, of which 4 were waited for; matrix products, arithmetic and copies ran while one was open for 0% of the time, Pallas kernels for 0%

profile of v5, /device:TPU:8, one launch (start us, length us, event | category | flops | bytes accessed | tf_op | source)
XLA Modules:
  0.0 50.9 jit_solution(589145220940775450)
XLA Ops:
  0.6 1.8 %shard_map.67 = (f32[2,7,4,16,128]{4,3,2,1,0:T(8,128)S(1)}, f32[2,7,4,16,128]{4,3,2,1,0:T(8,128)S(1)}, f32[4,16,128]{2,1,0:T(8,128)S(1)}, f32[2,4,16,128]{3,2,1,...) custom-call(f32[2,7,4,16,128]{4,3,2,1,0:T(8,128)} %f_hbm.1, ...), custom_call_target="tpu_custom_call" | custom-call | tf_op jit(solution)/shard_map/pallas_call | solution.py:416
  2.4 0.0 collective-permute-start
  2.4 2.9 %collective-permute-start.1 = (f32[160,128]{1,0:T(8,128)S(1)}, f32[160,128]{1,0:T(8,128)S(1)}, u32[]{:S(2)}, u32[]{:S(2)}) collective-permute-start(f32[160,128]{1,0:T(8,128)S(1)} %get-tuple-element.32), channel_id=1, source_target_pairs={{64,0},{128,64},{192,128},{256,192},{320,256},{384,320},{448,384},... | collective-permute-start | bytes 245768 | tf_op jit(solution)/shard_map/ppermute | solution.py:482
  5.4 2.1 %collective-permute-done.below_ref = f32[160,128]{1,0:T(8,128)S(1)} collective-permute-done((f32[160,128]{1,0:T(8,128)S(1)}, f32[160,128]{1,0:T(8,128)S(1)}, u32[]{:S(2)}, u32[]{:S(2)}) %collective-permute-start) | collective-permute-done | bytes 81952 | tf_op jit(solution)/shard_map/ppermute | solution.py:481
  7.5 0.0 collective-permute-done.1.above_ref
  7.5 13.2 %collective-permute-start.3 = (f32[160,128]{1,0:T(8,128)S(1)}, f32[160,128]{1,0:T(8,128)S(1)}, u32[]{:S(2)}, u32[]{:S(2)}) collective-permute-start(f32[160,128]{1,0:T(8,128)S(1)} %get-tuple-element.36), channel_id=1, source_target_pairs={{0,56},{1,57},{2,58},{3,59},{4,60},{5,61},{6,62},{7,63},{8,16},{9,... | collective-permute-start | bytes 245768 | tf_op jit(solution)/shard_map/ppermute | solution.py:485
  20.7 0.7 %collective-permute-start.2 = (f32[48,128]{1,0:T(8,128)S(1)}, f32[48,128]{1,0:T(8,128)S(1)}, u32[]{:S(2)}, u32[]{:S(2)}) collective-permute-start(f32[48,128]{1,0:T(8,128)S(1)} %get-tuple-element.35), channel_id=1, source_target_pairs={{64,71},{65,66},{66,65},{67,68},{68,67},{69,70},{70,69},{71,64},{7... | collective-permute-start | bytes 73736 | tf_op jit(solution)/shard_map/ppermute | solution.py:484
  21.4 0.7 %collective-permute-start.5 = (f32[40,128]{1,0:T(8,128)S(1)}, f32[40,128]{1,0:T(8,128)S(1)}, u32[]{:S(2)}, u32[]{:S(2)}) collective-permute-start(f32[40,128]{1,0:T(8,128)S(1)} %get-tuple-element.38), channel_id=1, source_target_pairs={{0,63},{3,60},{4,59},{7,56},{9,18},{10,17},{13,22},{14,21},{17,10}... | collective-permute-start | bytes 61448 | tf_op jit(solution)/shard_map/ppermute | solution.py:486
  22.0 1.9 %collective-permute-start.4 = (f32[32,128]{1,0:T(8,128)S(1)}, f32[32,128]{1,0:T(8,128)S(1)}, u32[]{:S(2)}, u32[]{:S(2)}) collective-permute-start(f32[32,128]{1,0:T(8,128)S(1)} %get-tuple-element.37), channel_id=1, source_target_pairs={{0,8},{1,9},{2,10},{3,11},{4,12},{5,13},{6,14},{7,15},{8,0},{9,1},... | collective-permute-start | bytes 49160 | tf_op jit(solution)/shard_map/ppermute | solution.py:487
  24.0 0.0 collective-permute-done.5.diag_ref
  24.0 3.7 %collective-permute-done.4.near_ref = f32[32,128]{1,0:T(8,128)S(1)} collective-permute-done((f32[32,128]{1,0:T(8,128)S(1)}, f32[32,128]{1,0:T(8,128)S(1)}, u32[]{:S(2)}, u32[]{:S(2)}) %collective-permute-start.4) | collective-permute-done | bytes 16416 | tf_op jit(solution)/shard_map/ppermute | solution.py:487
  27.7 0.0 collective-permute-done.2.z_ref
  27.7 0.0 collective-permute-done.3.y_ref
  27.7 5.9 %collective-permute-start.6 = (f32[96,128]{1,0:T(8,128)S(1)}, f32[96,128]{1,0:T(8,128)S(1)}, u32[]{:S(2)}, u32[]{:S(2)}) collective-permute-start(f32[96,128]{1,0:T(8,128)S(1)} %get-tuple-element.39), channel_id=1, source_target_pairs={{0,64},{64,0},{128,192},{192,128},{256,320},{320,256},{384,448},{4... | collective-permute-start | bytes 147464 | tf_op jit(solution)/shard_map/ppermute | solution.py:489
  33.6 0.9 %collective-permute-done.6.back_ref = f32[96,128]{1,0:T(8,128)S(1)} collective-permute-done((f32[96,128]{1,0:T(8,128)S(1)}, f32[96,128]{1,0:T(8,128)S(1)}, u32[]{:S(2)}, u32[]{:S(2)}) %collective-permute-start.6) | collective-permute-done | bytes 49184 | tf_op jit(solution)/shard_map/ppermute | solution.py:489
  34.4 0.4 shard_map.70
  34.8 0.4 collective-permute-start.7
  35.2 2.6 %collective-permute-start.8 = (f32[48,128]{1,0:T(8,128)S(1)}, f32[48,128]{1,0:T(8,128)S(1)}, u32[]{:S(2)}, u32[]{:S(2)}) collective-permute-start(f32[48,128]{1,0:T(8,128)S(1)} %get-tuple-element.47), channel_id=1, source_target_pairs={{64,0},{128,64},{192,128},{256,192},{320,256},{384,320},{448,384},... | collective-permute-start | bytes 73736 | tf_op jit(solution)/shard_map/ppermute | solution.py:497
  37.8 3.8 %collective-permute-start.11 = (f32[48,128]{1,0:T(8,128)S(1)}, f32[48,128]{1,0:T(8,128)S(1)}, u32[]{:S(2)}, u32[]{:S(2)}) collective-permute-start(f32[48,128]{1,0:T(8,128)S(1)} %get-tuple-element.50), channel_id=1, source_target_pairs={{1,2},{2,1},{5,6},{6,5},{8,16},{11,19},{12,20},{15,23},{16,8},{19,... | collective-permute-start | bytes 73736 | tf_op jit(solution)/shard_map/ppermute | solution.py:500
  41.6 2.4 %collective-permute-start.10 = (f32[24,128]{1,0:T(8,128)S(1)}, f32[24,128]{1,0:T(8,128)S(1)}, u32[]{:S(2)}, u32[]{:S(2)}) collective-permute-start(f32[24,128]{1,0:T(8,128)S(1)} %get-tuple-element.49), channel_id=1, source_target_pairs={{0,1},{1,0},{2,3},{3,2},{4,5},{5,4},{6,7},{7,6},{8,9},{9,8},{10,11... | collective-permute-start | bytes 36872 | tf_op jit(solution)/shard_map/ppermute | solution.py:499
  44.0 3.2 %collective-permute-start.9 = (f32[16,128]{1,0:T(8,128)S(1)}, f32[16,128]{1,0:T(8,128)S(1)}, u32[]{:S(2)}, u32[]{:S(2)}) collective-permute-start(f32[16,128]{1,0:T(8,128)S(1)} %get-tuple-element.48), channel_id=1, source_target_pairs={{0,8},{8,0},{16,24},{24,16},{32,40},{40,32},{48,56},{56,48},{1,9},... | collective-permute-start | bytes 24584 | tf_op jit(solution)/shard_map/ppermute | solution.py:498
  47.2 2.4 %collective-permute-done.9.y1_ref = f32[16,128]{1,0:T(8,128)S(1)} collective-permute-done((f32[16,128]{1,0:T(8,128)S(1)}, f32[16,128]{1,0:T(8,128)S(1)}, u32[]{:S(2)}, u32[]{:S(2)}) %collective-permute-start.9) | collective-permute-done | bytes 8224 | tf_op jit(solution)/shard_map/ppermute | solution.py:498
  49.6 0.0 collective-permute-done.10.z1_ref
  49.6 0.0 collective-permute-done.7.below_ref
  49.6 0.0 collective-permute-done.8.above_ref
  49.6 0.0 collective-permute-done.11.relay_ref
  49.6 1.3 %shard_map.71 = (f32[2,7,4,16,128]{4,3,2,1,0:T(8,128)}, f32[4,16,128]{2,1,0:T(8,128)}, f32[2,4,16,128]{3,2,1,0:T(8,128)}) custom-call(f32[2,7,4,16,128]{4,3,2,1,0:T(8,128)S(1)} %get-tuple-element.27.f_ref, f32[4,16,128]{2,1,0:T(8,128)S(1)} %get-tuple-element.28.r_ref, f32[2,4,16,128]{3,2,1,0:T(8,128)S(1)} %get-tuple-element.29.t_ref, ...), custom_call_target="tpu_custom_call" | custom-call | tf_op jit(solution)/shard_map/pallas_call | solution.py:416
  (2 shorter events, 0.0 us)
Async XLA Ops:
  2.4 5.1 %collective-permute-start = (f32[160,128]{1,0:T(8,128)S(1)}, f32[160,128]{1,0:T(8,128)S(1)}, u32[]{:S(2)}, u32[]{:S(2)}) collective-permute-start(f32[160,128]{1,0:T(8,128)S(1)} %get-tuple-element.31), channel_id=1, source_target_pairs={{0,64},{64,128},{128,192},{192,256},{256,320},{320,384},{384,448},... | collective-permute-start | bytes 245768 | tf_op jit(solution)/shard_map/ppermute | solution.py:481
  2.4 5.1 %collective-permute-start.1 = (f32[160,128]{1,0:T(8,128)S(1)}, f32[160,128]{1,0:T(8,128)S(1)}, u32[]{:S(2)}, u32[]{:S(2)}) collective-permute-start(f32[160,128]{1,0:T(8,128)S(1)} %get-tuple-element.32), channel_id=1, source_target_pairs={{64,0},{128,64},{192,128},{256,192},{320,256},{384,320},{448,384},... | collective-permute-start | bytes 245768 | tf_op jit(solution)/shard_map/ppermute | solution.py:482
  7.5 20.1 %collective-permute-start.3 = (f32[160,128]{1,0:T(8,128)S(1)}, f32[160,128]{1,0:T(8,128)S(1)}, u32[]{:S(2)}, u32[]{:S(2)}) collective-permute-start(f32[160,128]{1,0:T(8,128)S(1)} %get-tuple-element.36), channel_id=1, source_target_pairs={{0,56},{1,57},{2,58},{3,59},{4,60},{5,61},{6,62},{7,63},{8,16},{9,... | collective-permute-start | bytes 245768 | tf_op jit(solution)/shard_map/ppermute | solution.py:485
  20.7 7.0 %collective-permute-start.2 = (f32[48,128]{1,0:T(8,128)S(1)}, f32[48,128]{1,0:T(8,128)S(1)}, u32[]{:S(2)}, u32[]{:S(2)}) collective-permute-start(f32[48,128]{1,0:T(8,128)S(1)} %get-tuple-element.35), channel_id=1, source_target_pairs={{64,71},{65,66},{66,65},{67,68},{68,67},{69,70},{70,69},{71,64},{7... | collective-permute-start | bytes 73736 | tf_op jit(solution)/shard_map/ppermute | solution.py:484
  21.4 2.6 %collective-permute-start.5 = (f32[40,128]{1,0:T(8,128)S(1)}, f32[40,128]{1,0:T(8,128)S(1)}, u32[]{:S(2)}, u32[]{:S(2)}) collective-permute-start(f32[40,128]{1,0:T(8,128)S(1)} %get-tuple-element.38), channel_id=1, source_target_pairs={{0,63},{3,60},{4,59},{7,56},{9,18},{10,17},{13,22},{14,21},{17,10}... | collective-permute-start | bytes 61448 | tf_op jit(solution)/shard_map/ppermute | solution.py:486
  22.0 5.6 %collective-permute-start.4 = (f32[32,128]{1,0:T(8,128)S(1)}, f32[32,128]{1,0:T(8,128)S(1)}, u32[]{:S(2)}, u32[]{:S(2)}) collective-permute-start(f32[32,128]{1,0:T(8,128)S(1)} %get-tuple-element.37), channel_id=1, source_target_pairs={{0,8},{1,9},{2,10},{3,11},{4,12},{5,13},{6,14},{7,15},{8,0},{9,1},... | collective-permute-start | bytes 49160 | tf_op jit(solution)/shard_map/ppermute | solution.py:487
  27.7 6.7 %collective-permute-start.6 = (f32[96,128]{1,0:T(8,128)S(1)}, f32[96,128]{1,0:T(8,128)S(1)}, u32[]{:S(2)}, u32[]{:S(2)}) collective-permute-start(f32[96,128]{1,0:T(8,128)S(1)} %get-tuple-element.39), channel_id=1, source_target_pairs={{0,64},{64,0},{128,192},{192,128},{256,320},{320,256},{384,448},{4... | collective-permute-start | bytes 147464 | tf_op jit(solution)/shard_map/ppermute | solution.py:489
  34.8 14.8 %collective-permute-start.7 = (f32[48,128]{1,0:T(8,128)S(1)}, f32[48,128]{1,0:T(8,128)S(1)}, u32[]{:S(2)}, u32[]{:S(2)}) collective-permute-start(f32[48,128]{1,0:T(8,128)S(1)} %get-tuple-element.46), channel_id=1, source_target_pairs={{0,64},{64,128},{128,192},{192,256},{256,320},{320,384},{384,448},... | collective-permute-start | bytes 73736 | tf_op jit(solution)/shard_map/ppermute | solution.py:496
  35.2 14.4 %collective-permute-start.8 = (f32[48,128]{1,0:T(8,128)S(1)}, f32[48,128]{1,0:T(8,128)S(1)}, u32[]{:S(2)}, u32[]{:S(2)}) collective-permute-start(f32[48,128]{1,0:T(8,128)S(1)} %get-tuple-element.47), channel_id=1, source_target_pairs={{64,0},{128,64},{192,128},{256,192},{320,256},{384,320},{448,384},... | collective-permute-start | bytes 73736 | tf_op jit(solution)/shard_map/ppermute | solution.py:497
  37.8 11.8 %collective-permute-start.11 = (f32[48,128]{1,0:T(8,128)S(1)}, f32[48,128]{1,0:T(8,128)S(1)}, u32[]{:S(2)}, u32[]{:S(2)}) collective-permute-start(f32[48,128]{1,0:T(8,128)S(1)} %get-tuple-element.50), channel_id=1, source_target_pairs={{1,2},{2,1},{5,6},{6,5},{8,16},{11,19},{12,20},{15,23},{16,8},{19,... | collective-permute-start | bytes 73736 | tf_op jit(solution)/shard_map/ppermute | solution.py:500
  41.6 8.0 %collective-permute-start.10 = (f32[24,128]{1,0:T(8,128)S(1)}, f32[24,128]{1,0:T(8,128)S(1)}, u32[]{:S(2)}, u32[]{:S(2)}) collective-permute-start(f32[24,128]{1,0:T(8,128)S(1)} %get-tuple-element.49), channel_id=1, source_target_pairs={{0,1},{1,0},{2,3},{3,2},{4,5},{5,4},{6,7},{7,6},{8,9},{9,8},{10,11... | collective-permute-start | bytes 36872 | tf_op jit(solution)/shard_map/ppermute | solution.py:499
  44.0 5.5 %collective-permute-start.9 = (f32[16,128]{1,0:T(8,128)S(1)}, f32[16,128]{1,0:T(8,128)S(1)}, u32[]{:S(2)}, u32[]{:S(2)}) collective-permute-start(f32[16,128]{1,0:T(8,128)S(1)} %get-tuple-element.48), channel_id=1, source_target_pairs={{0,8},{8,0},{16,24},{24,16},{32,40},{40,32},{48,56},{56,48},{1,9},... | collective-permute-start | bytes 24584 | tf_op jit(solution)/shard_map/ppermute | solution.py:498

commit v6 on v5

--- a/solution.py
+++ b/solution.py
@@ -179,7 +179,8 @@
     raw_ref[16:24] = z2
     diag_ref[0:16] = y_lines
     diag_ref[16:24] = z_lines
-    diag_ref[24:40] = jnp.zeros((16, 128), jnp.float32)
+    rest = diag_ref.shape[0] - 24
+    diag_ref[24:] = jnp.zeros((rest, 128), jnp.float32)
     z1 = jnp.concatenate([z1, jnp.zeros_like(z1)], axis=0)
     y_all = jnp.concatenate([y_deep, y_lines], axis=0)
     z_all = jnp.concatenate([z_deep, z_lines, jnp.zeros((y_all.shape[0] - 16, 128), jnp.float32)], axis=0)
@@ -202,9 +203,8 @@
     z_ref[32:48] = share[0:16]
 
 
-def back_kernel(z_ref, y_ref, diag_ref, near_ref, out_ref, lines_ref):
+def back_kernel(z_ref, y_ref, near_ref, out_ref):
     even = parities()
-    lines_ref[...] = diag_ref[0:24]
     out_ref[0:16] = near_ref[16:32]
     out_ref[16:32] = jnp.where(even[0], y_ref[80:96], z_ref[16:32])
     out_ref[32:96] = y_ref[96:160]
@@ -485,9 +485,9 @@
     y_in = lax.ppermute(y, AXES, grid_pairs(second_y_move))
     diag_in = lax.ppermute(diag, AXES, grid_pairs(diagonal_move))
     near_in = lax.ppermute(near, AXES, grid_pairs(near_move))
-    back, lines = call(back_kernel, [(96, 128), (24, 128)], z_in, y_in, diag_in, near_in)
+    (back,) = call(back_kernel, [(96, 128)], z_in, y_in, near_in)
     back_in = lax.ppermute(back, "gx", axis_pairs("gx", 0))
-    return (below, above, z_in, y_in, near_in, back_in), lines
+    return (below, above, z_in, y_in, near_in, back_in), diag_in
 
 
 def second_exchange(up, down, y1, z1, relay):
@@ -503,7 +503,7 @@
 
 def on_device(checkpoint, cotangent, reaction_rate, relax_time):
     inputs = (checkpoint, cotangent, reaction_rate, relax_time)
-    messages = [(160, 128), (160, 128), (16, 128), (80, 128), (40, 128), (24, 128)]
+    messages = [(160, 128), (160, 128), (16, 128), (80, 128), (152, 128), (24, 128)]
     f, g, r, t, *sent, raw = call(
         first_kernel, [a.shape for a in inputs] + messages,
         *(pltpu.with_memory_space_constraint(a, pltpu.HBM) for a in inputs),

time: 51.2 us -> 48.7 us (0.951)
  waiting for transfers between devices: 9.05 us -> 7.64 us
  starting transfers between devices: 37.6 us -> 36.4 us
    ppermute x1, starting transfers between devices: 3.78 us -> 1.91 us  [second_exchange(): lax.ppermute(relay, AXES, grid_pairs(relay_move))]
    ppermute x1, starting transfers between devices: 3.18 us -> 4.92 us  [second_exchange(): lax.ppermute(y1, 'gy', axis_pairs('gy', 0))]
    ppermute x1, starting transfers between devices: 5.86 us -> 4.6 us  [first_exchange(): back_in = lax.ppermute(back, 'gx', axis_pairs('gx', 0))]
    ppermute x1, waiting for transfers between devices: 2.36 us -> 1.61 us  [second_exchange(): lax.ppermute(y1, 'gy', axis_pairs('gy', 0))]
    ppermute x1, waiting for transfers between devices: 3.69 us -> 3.03 us  [first_exchange(): near_in = lax.ppermute(near, AXES, grid_pairs(near_move))]
  transfers between devices with their start and end apart: 12 -> 12, of which waited for: 4 -> 4; matrix products, arithmetic and copies ran while one was open for 0% -> 0% of each run, Pallas kernels for 0% -> 1%
where the time goes in v6:
time: 48.7 us; the launch traced here: 48.3 us
  starting transfers between devices  36.4 us (75%)
  waiting for transfers between devices  7.64 us (16%)
  Pallas kernels  3.47 us (7%)
  between operations  0.75 us (2%)
    ppermute x1, starting transfers between devices, first_exchange(): y_in = lax.ppermute(y, AXES, grid_pairs(second_y_move))  13.2 us
    ppermute x1, starting transfers between devices, second_exchange(): lax.ppermute(y1, 'gy', axis_pairs('gy', 0))  4.92 us
    ppermute x1, starting transfers between devices, first_exchange(): back_in = lax.ppermute(back, 'gx', axis_pairs('gx', 0))  4.6 us
    pallas_call x5, Pallas kernels, call(): pl.pallas_call(kernel, out_shape=[jax.ShapeDtypeStruct(s, jnp.float32) fo...  3.47 us
    ppermute x1, waiting for transfers between devices, first_exchange(): near_in = lax.ppermute(near, AXES, grid_pairs(near_move))  3.03 us
    ppermute x1, starting transfers between devices, first_exchange(): above = lax.ppermute(down, 'gx', to_down)  2.94 us
    ppermute x1, starting transfers between devices, second_exchange(): lax.ppermute(z1, 'gz', axis_pairs('gz', 0))  2.66 us
    ppermute x1, starting transfers between devices, second_exchange(): lax.ppermute(down, 'gx', to_down)  2.61 us
  transfers between devices with their start and end apart: 12, of which 4 were waited for; matrix products, arithmetic and copies ran while one was open for 0% of the time, Pallas kernels for 1%

profile of v6, /device:TPU:8, one launch (start us, length us, event | category | flops | bytes accessed | tf_op | source)
XLA Modules:
  0.0 48.3 jit_solution(5828031401734848309)
XLA Ops:
  0.6 1.8 %shard_map.67 = (f32[2,7,4,16,128]{4,3,2,1,0:T(8,128)S(1)}, f32[2,7,4,16,128]{4,3,2,1,0:T(8,128)S(1)}, f32[4,16,128]{2,1,0:T(8,128)S(1)}, f32[2,4,16,128]{3,2,1,...) custom-call(f32[2,7,4,16,128]{4,3,2,1,0:T(8,128)} %f_hbm.1, ...), custom_call_target="tpu_custom_call" | custom-call | tf_op jit(solution)/shard_map/pallas_call | solution.py:416
  2.4 0.0 collective-permute-start
  2.4 2.9 %collective-permute-start.1 = (f32[160,128]{1,0:T(8,128)S(1)}, f32[160,128]{1,0:T(8,128)S(1)}, u32[]{:S(2)}, u32[]{:S(2)}) collective-permute-start(f32[160,128]{1,0:T(8,128)S(1)} %get-tuple-element.30), channel_id=1, source_target_pairs={{64,0},{128,64},{192,128},{256,192},{320,256},{384,320},{448,384},... | collective-permute-start | bytes 245768 | tf_op jit(solution)/shard_map/ppermute | solution.py:482
  5.4 2.1 %collective-permute-done.below_ref = f32[160,128]{1,0:T(8,128)S(1)} collective-permute-done((f32[160,128]{1,0:T(8,128)S(1)}, f32[160,128]{1,0:T(8,128)S(1)}, u32[]{:S(2)}, u32[]{:S(2)}) %collective-permute-start) | collective-permute-done | bytes 81952 | tf_op jit(solution)/shard_map/ppermute | solution.py:481
  7.5 0.0 collective-permute-done.1.above_ref
  7.5 13.2 %collective-permute-start.3 = (f32[160,128]{1,0:T(8,128)S(1)}, f32[160,128]{1,0:T(8,128)S(1)}, u32[]{:S(2)}, u32[]{:S(2)}) collective-permute-start(f32[160,128]{1,0:T(8,128)S(1)} %get-tuple-element.34), channel_id=1, source_target_pairs={{0,56},{1,57},{2,58},{3,59},{4,60},{5,61},{6,62},{7,63},{8,16},{9,... | collective-permute-start | bytes 245768 | tf_op jit(solution)/shard_map/ppermute | solution.py:485
  20.7 0.7 %collective-permute-start.2 = (f32[48,128]{1,0:T(8,128)S(1)}, f32[48,128]{1,0:T(8,128)S(1)}, u32[]{:S(2)}, u32[]{:S(2)}) collective-permute-start(f32[48,128]{1,0:T(8,128)S(1)} %get-tuple-element.33), channel_id=1, source_target_pairs={{64,71},{65,66},{66,65},{67,68},{68,67},{69,70},{70,69},{71,64},{7... | collective-permute-start | bytes 73736 | tf_op jit(solution)/shard_map/ppermute | solution.py:484
  21.4 1.9 %collective-permute-start.4 = (f32[32,128]{1,0:T(8,128)S(1)}, f32[32,128]{1,0:T(8,128)S(1)}, u32[]{:S(2)}, u32[]{:S(2)}) collective-permute-start(f32[32,128]{1,0:T(8,128)S(1)} %get-tuple-element.35), channel_id=1, source_target_pairs={{0,8},{1,9},{2,10},{3,11},{4,12},{5,13},{6,14},{7,15},{8,0},{9,1},... | collective-permute-start | bytes 49160 | tf_op jit(solution)/shard_map/ppermute | solution.py:487
  23.3 0.7 %collective-permute-start.6 = (f32[152,128]{1,0:T(8,128)S(1)}, f32[152,128]{1,0:T(8,128)S(1)}, u32[]{:S(2)}, u32[]{:S(2)}) collective-permute-start(f32[152,128]{1,0:T(8,128)S(1)} %get-tuple-element.41), channel_id=1, source_target_pairs={{0,63},{3,60},{4,59},{7,56},{9,18},{10,17},{13,22},{14,21},{17,10}... | collective-permute-start | bytes 233480 | tf_op jit(solution)/shard_map/ppermute | solution.py:486
  24.0 3.0 %collective-permute-done.4.near_ref = f32[32,128]{1,0:T(8,128)S(1)} collective-permute-done((f32[32,128]{1,0:T(8,128)S(1)}, f32[32,128]{1,0:T(8,128)S(1)}, u32[]{:S(2)}, u32[]{:S(2)}) %collective-permute-start.4) | collective-permute-done | bytes 16416 | tf_op jit(solution)/shard_map/ppermute | solution.py:487
  27.0 0.0 collective-permute-done.2.z_ref
  27.0 0.0 collective-permute-done.3.y_ref
  27.0 4.6 %collective-permute-start.5 = (f32[96,128]{1,0:T(8,128)S(1)}, f32[96,128]{1,0:T(8,128)S(1)}, u32[]{:S(2)}, u32[]{:S(2)}) collective-permute-start(f32[96,128]{1,0:T(8,128)S(1)} %shard_map.69), channel_id=1, source_target_pairs={{0,64},{64,0},{128,192},{192,128},{256,320},{320,256},{384,448},{4... | collective-permute-start | bytes 147464 | tf_op jit(solution)/shard_map/ppermute | solution.py:489
  31.6 0.9 %collective-permute-done.5.back_ref = f32[96,128]{1,0:T(8,128)S(1)} collective-permute-done((f32[96,128]{1,0:T(8,128)S(1)}, f32[96,128]{1,0:T(8,128)S(1)}, u32[]{:S(2)}, u32[]{:S(2)}) %collective-permute-start.5) | collective-permute-done | bytes 49184 | tf_op jit(solution)/shard_map/ppermute | solution.py:489
  32.5 0.4 shard_map.70
  32.9 0.4 collective-permute-start.7
  33.3 2.6 %collective-permute-start.8 = (f32[48,128]{1,0:T(8,128)S(1)}, f32[48,128]{1,0:T(8,128)S(1)}, u32[]{:S(2)}, u32[]{:S(2)}) collective-permute-start(f32[48,128]{1,0:T(8,128)S(1)} %get-tuple-element.43), channel_id=1, source_target_pairs={{64,0},{128,64},{192,128},{256,192},{320,256},{384,320},{448,384},... | collective-permute-start | bytes 73736 | tf_op jit(solution)/shard_map/ppermute | solution.py:497
  35.9 1.9 %collective-permute-start.11 = (f32[48,128]{1,0:T(8,128)S(1)}, f32[48,128]{1,0:T(8,128)S(1)}, u32[]{:S(2)}, u32[]{:S(2)}) collective-permute-start(f32[48,128]{1,0:T(8,128)S(1)} %get-tuple-element.46), channel_id=1, source_target_pairs={{1,2},{2,1},{5,6},{6,5},{8,16},{11,19},{12,20},{15,23},{16,8},{19,... | collective-permute-start | bytes 73736 | tf_op jit(solution)/shard_map/ppermute | solution.py:500
  37.8 2.7 %collective-permute-start.10 = (f32[24,128]{1,0:T(8,128)S(1)}, f32[24,128]{1,0:T(8,128)S(1)}, u32[]{:S(2)}, u32[]{:S(2)}) collective-permute-start(f32[24,128]{1,0:T(8,128)S(1)} %get-tuple-element.45), channel_id=1, source_target_pairs={{0,1},{1,0},{2,3},{3,2},{4,5},{5,4},{6,7},{7,6},{8,9},{9,8},{10,11... | collective-permute-start | bytes 36872 | tf_op jit(solution)/shard_map/ppermute | solution.py:499
  40.5 0.0 collective-permute-done.6.diag_ref
  40.5 4.9 %collective-permute-start.9 = (f32[16,128]{1,0:T(8,128)S(1)}, f32[16,128]{1,0:T(8,128)S(1)}, u32[]{:S(2)}, u32[]{:S(2)}) collective-permute-start(f32[16,128]{1,0:T(8,128)S(1)} %get-tuple-element.44), channel_id=1, source_target_pairs={{0,8},{8,0},{16,24},{24,16},{32,40},{40,32},{48,56},{56,48},{1,9},... | collective-permute-start | bytes 24584 | tf_op jit(solution)/shard_map/ppermute | solution.py:498
  45.4 1.6 %collective-permute-done.9.y1_ref = f32[16,128]{1,0:T(8,128)S(1)} collective-permute-done((f32[16,128]{1,0:T(8,128)S(1)}, f32[16,128]{1,0:T(8,128)S(1)}, u32[]{:S(2)}, u32[]{:S(2)}) %collective-permute-start.9) | collective-permute-done | bytes 8224 | tf_op jit(solution)/shard_map/ppermute | solution.py:498
  47.0 0.0 collective-permute-done.10.z1_ref
  47.0 0.0 collective-permute-done.7.below_ref
  47.0 0.0 collective-permute-done.8.above_ref
  47.0 0.0 collective-permute-done.11.relay_ref
  47.0 1.3 %shard_map.71 = (f32[2,7,4,16,128]{4,3,2,1,0:T(8,128)}, f32[4,16,128]{2,1,0:T(8,128)}, f32[2,4,16,128]{3,2,1,0:T(8,128)}) custom-call(f32[2,7,4,16,128]{4,3,2,1,0:T(8,128)S(1)} %get-tuple-element.25.f_ref, f32[4,16,128]{2,1,0:T(8,128)S(1)} %get-tuple-element.26.r_ref, f32[2,4,16,128]{3,2,1,0:T(8,128)S(1)} %get-tuple-element.27.t_ref, ...), custom_call_target="tpu_custom_call" | custom-call | tf_op jit(solution)/shard_map/pallas_call | solution.py:416
  (2 shorter events, 0.0 us)
Async XLA Ops:
  2.4 5.1 %collective-permute-start = (f32[160,128]{1,0:T(8,128)S(1)}, f32[160,128]{1,0:T(8,128)S(1)}, u32[]{:S(2)}, u32[]{:S(2)}) collective-permute-start(f32[160,128]{1,0:T(8,128)S(1)} %get-tuple-element.29), channel_id=1, source_target_pairs={{0,64},{64,128},{128,192},{192,256},{256,320},{320,384},{384,448},... | collective-permute-start | bytes 245768 | tf_op jit(solution)/shard_map/ppermute | solution.py:481
  2.4 5.1 %collective-permute-start.1 = (f32[160,128]{1,0:T(8,128)S(1)}, f32[160,128]{1,0:T(8,128)S(1)}, u32[]{:S(2)}, u32[]{:S(2)}) collective-permute-start(f32[160,128]{1,0:T(8,128)S(1)} %get-tuple-element.30), channel_id=1, source_target_pairs={{64,0},{128,64},{192,128},{256,192},{320,256},{384,320},{448,384},... | collective-permute-start | bytes 245768 | tf_op jit(solution)/shard_map/ppermute | solution.py:482
  7.5 19.5 %collective-permute-start.3 = (f32[160,128]{1,0:T(8,128)S(1)}, f32[160,128]{1,0:T(8,128)S(1)}, u32[]{:S(2)}, u32[]{:S(2)}) collective-permute-start(f32[160,128]{1,0:T(8,128)S(1)} %get-tuple-element.34), channel_id=1, source_target_pairs={{0,56},{1,57},{2,58},{3,59},{4,60},{5,61},{6,62},{7,63},{8,16},{9,... | collective-permute-start | bytes 245768 | tf_op jit(solution)/shard_map/ppermute | solution.py:485
  20.7 6.3 %collective-permute-start.2 = (f32[48,128]{1,0:T(8,128)S(1)}, f32[48,128]{1,0:T(8,128)S(1)}, u32[]{:S(2)}, u32[]{:S(2)}) collective-permute-start(f32[48,128]{1,0:T(8,128)S(1)} %get-tuple-element.33), channel_id=1, source_target_pairs={{64,71},{65,66},{66,65},{67,68},{68,67},{69,70},{70,69},{71,64},{7... | collective-permute-start | bytes 73736 | tf_op jit(solution)/shard_map/ppermute | solution.py:484
  21.4 5.6 %collective-permute-start.4 = (f32[32,128]{1,0:T(8,128)S(1)}, f32[32,128]{1,0:T(8,128)S(1)}, u32[]{:S(2)}, u32[]{:S(2)}) collective-permute-start(f32[32,128]{1,0:T(8,128)S(1)} %get-tuple-element.35), channel_id=1, source_target_pairs={{0,8},{1,9},{2,10},{3,11},{4,12},{5,13},{6,14},{7,15},{8,0},{9,1},... | collective-permute-start | bytes 49160 | tf_op jit(solution)/shard_map/ppermute | solution.py:487
  23.3 17.2 %collective-permute-start.6 = (f32[152,128]{1,0:T(8,128)S(1)}, f32[152,128]{1,0:T(8,128)S(1)}, u32[]{:S(2)}, u32[]{:S(2)}) collective-permute-start(f32[152,128]{1,0:T(8,128)S(1)} %get-tuple-element.41), channel_id=1, source_target_pairs={{0,63},{3,60},{4,59},{7,56},{9,18},{10,17},{13,22},{14,21},{17,10}... | collective-permute-start | bytes 233480 | tf_op jit(solution)/shard_map/ppermute | solution.py:486
  27.0 5.5 %collective-permute-start.5 = (f32[96,128]{1,0:T(8,128)S(1)}, f32[96,128]{1,0:T(8,128)S(1)}, u32[]{:S(2)}, u32[]{:S(2)}) collective-permute-start(f32[96,128]{1,0:T(8,128)S(1)} %shard_map.69), channel_id=1, source_target_pairs={{0,64},{64,0},{128,192},{192,128},{256,320},{320,256},{384,448},{4... | collective-permute-start | bytes 147464 | tf_op jit(solution)/shard_map/ppermute | solution.py:489
  32.9 14.1 %collective-permute-start.7 = (f32[48,128]{1,0:T(8,128)S(1)}, f32[48,128]{1,0:T(8,128)S(1)}, u32[]{:S(2)}, u32[]{:S(2)}) collective-permute-start(f32[48,128]{1,0:T(8,128)S(1)} %get-tuple-element.42), channel_id=1, source_target_pairs={{0,64},{64,128},{128,192},{192,256},{256,320},{320,384},{384,448},... | collective-permute-start | bytes 73736 | tf_op jit(solution)/shard_map/ppermute | solution.py:496
  33.3 13.7 %collective-permute-start.8 = (f32[48,128]{1,0:T(8,128)S(1)}, f32[48,128]{1,0:T(8,128)S(1)}, u32[]{:S(2)}, u32[]{:S(2)}) collective-permute-start(f32[48,128]{1,0:T(8,128)S(1)} %get-tuple-element.43), channel_id=1, source_target_pairs={{64,0},{128,64},{192,128},{256,192},{320,256},{384,320},{448,384},... | collective-permute-start | bytes 73736 | tf_op jit(solution)/shard_map/ppermute | solution.py:497
  35.9 11.1 %collective-permute-start.11 = (f32[48,128]{1,0:T(8,128)S(1)}, f32[48,128]{1,0:T(8,128)S(1)}, u32[]{:S(2)}, u32[]{:S(2)}) collective-permute-start(f32[48,128]{1,0:T(8,128)S(1)} %get-tuple-element.46), channel_id=1, source_target_pairs={{1,2},{2,1},{5,6},{6,5},{8,16},{11,19},{12,20},{15,23},{16,8},{19,... | collective-permute-start | bytes 73736 | tf_op jit(solution)/shard_map/ppermute | solution.py:500
  37.8 9.2 %collective-permute-start.10 = (f32[24,128]{1,0:T(8,128)S(1)}, f32[24,128]{1,0:T(8,128)S(1)}, u32[]{:S(2)}, u32[]{:S(2)}) collective-permute-start(f32[24,128]{1,0:T(8,128)S(1)} %get-tuple-element.45), channel_id=1, source_target_pairs={{0,1},{1,0},{2,3},{3,2},{4,5},{5,4},{6,7},{7,6},{8,9},{9,8},{10,11... | collective-permute-start | bytes 36872 | tf_op jit(solution)/shard_map/ppermute | solution.py:499
  40.5 6.5 %collective-permute-start.9 = (f32[16,128]{1,0:T(8,128)S(1)}, f32[16,128]{1,0:T(8,128)S(1)}, u32[]{:S(2)}, u32[]{:S(2)}) collective-permute-start(f32[16,128]{1,0:T(8,128)S(1)} %get-tuple-element.44), channel_id=1, source_target_pairs={{0,8},{8,0},{16,24},{24,16},{32,40},{40,32},{48,56},{56,48},{1,9},... | collective-permute-start | bytes 24584 | tf_op jit(solution)/shard_map/ppermute | solution.py:498

commit v7 on v6

--- a/solution.py
+++ b/solution.py
@@ -186,21 +186,21 @@
     z_all = jnp.concatenate([z_deep, z_lines, jnp.zeros((y_all.shape[0] - 16, 128), jnp.float32)], axis=0)
     own0_ref[...] = jnp.where(even[0], y1, z1)
     own1_ref[...] = jnp.where(even[0], y_all, z_all)
-    for ref in (up_ref, down_ref):
-        ref[64:80] = jnp.where(even[0], z1, y1)
-        ref[80:160] = jnp.where(even[0], z_all, y_all)
-
-
-def forward_kernel(own0_ref, own1_ref, below_ref, above_ref, y_ref, z_ref, near_ref):
+    up_ref[64:80] = z1
+    up_ref[80:96] = z_all[0:16]
+    down_ref[64:80] = y1
+    down_ref[80:160] = y_all
+
+
+def forward_kernel(own0_ref, own1_ref, above_ref, below_ref, y_ref, near_ref, z_ref):
     even = parities()
     near_ref[0:16] = own0_ref[...]
     near_ref[16:32] = jnp.where(even[0], above_ref[64:80], below_ref[64:80])
-    share = jnp.where(even[0], above_ref[80:160], below_ref[80:160])
+    near_ref[32:40] = jnp.zeros((8, 128), jnp.float32)
     y_ref[0:80] = own1_ref[...]
-    y_ref[80:160] = share
+    y_ref[80:160] = above_ref[80:160]
     z_ref[0:16] = own1_ref[0:16]
-    z_ref[16:32] = share[0:16]
-    z_ref[32:48] = share[0:16]
+    z_ref[16:32] = below_ref[80:96]
 
 
 def back_kernel(z_ref, y_ref, near_ref, out_ref):
@@ -478,9 +478,9 @@
 
 def first_exchange(up, down, own0, own1, diag):
     to_up, to_down = shifts("gx")
+    above = lax.ppermute(down, "gx", to_down)
     below = lax.ppermute(up, "gx", to_up)
-    above = lax.ppermute(down, "gx", to_down)
-    y, z, near = call(forward_kernel, [(160, 128), (48, 128), (32, 128)], own0, own1, below, above)
+    y, near, z = call(forward_kernel, [(160, 128), (40, 128), (32, 128)], own0, own1, above, below)
     z_in = lax.ppermute(z, AXES, grid_pairs(second_z_move))
     y_in = lax.ppermute(y, AXES, grid_pairs(second_y_move))
     diag_in = lax.ppermute(diag, AXES, grid_pairs(diagonal_move))
@@ -503,7 +503,7 @@
 
 def on_device(checkpoint, cotangent, reaction_rate, relax_time):
     inputs = (checkpoint, cotangent, reaction_rate, relax_time)
-    messages = [(160, 128), (160, 128), (16, 128), (80, 128), (152, 128), (24, 128)]
+    messages = [(96, 128), (160, 128), (16, 128), (80, 128), (136, 128), (24, 128)]
     f, g, r, t, *sent, raw = call(
         first_kernel, [a.shape for a in inputs] + messages,
         *(pltpu.with_memory_space_constraint(a, pltpu.HBM) for a in inputs),

time: 48.7 us -> 49.3 us (1.012)
  waiting for transfers between devices: 7.64 us -> 12 us
  starting transfers between devices: 36.4 us -> 32.9 us
    ppermute x1, starting transfers between devices: 4.92 us -> 1.92 us  [second_exchange(): lax.ppermute(y1, 'gy', axis_pairs('gy', 0))]
    ppermute x1, starting transfers between devices: 4.6 us -> 1.92 us  [first_exchange(): back_in = lax.ppermute(back, 'gx', axis_pairs('gx', 0))]
    ppermute x1, waiting for transfers between devices: 2.12 us -> 4.72 us  [first_exchange(): below = lax.ppermute(up, 'gx', to_up)]
    ppermute x1, waiting for transfers between devices: 1.61 us -> 3.62 us  [second_exchange(): lax.ppermute(y1, 'gy', axis_pairs('gy', 0))]
    ppermute x1, starting transfers between devices: 1.91 us -> 3.47 us  [second_exchange(): lax.ppermute(relay, AXES, grid_pairs(relay_move))]
    ppermute x1, starting transfers between devices: 2.66 us -> 4 us  [second_exchange(): lax.ppermute(z1, 'gz', axis_pairs('gz', 0))]
    ppermute x1, starting transfers between devices: 2.94 us -> 2.21 us  [first_exchange(): above = lax.ppermute(down, 'gx', to_down)]
    ppermute x1, waiting for transfers between devices: 3.03 us -> 2.39 us  [first_exchange(): near_in = lax.ppermute(near, AXES, grid_pairs(near_move))]
where the time goes in v7:
time: 49.3 us; the launch traced here: 49 us
  starting transfers between devices  32.9 us (67%)
  waiting for transfers between devices  12 us (24%)
  Pallas kernels  3.44 us (7%)
  between operations  0.75 us (2%)
    ppermute x1, starting transfers between devices, first_exchange(): y_in = lax.ppermute(y, AXES, grid_pairs(second_y_move))  13.2 us
    ppermute x1, waiting for transfers between devices, first_exchange(): below = lax.ppermute(up, 'gx', to_up)  4.72 us
    ppermute x1, starting transfers between devices, second_exchange(): lax.ppermute(z1, 'gz', axis_pairs('gz', 0))  4 us
    ppermute x1, waiting for transfers between devices, second_exchange(): lax.ppermute(y1, 'gy', axis_pairs('gy', 0))  3.62 us
    ppermute x1, starting transfers between devices, second_exchange(): lax.ppermute(relay, AXES, grid_pairs(relay_move))  3.47 us
    pallas_call x5, Pallas kernels, call(): pl.pallas_call(kernel, out_shape=[jax.ShapeDtypeStruct(s, jnp.float32) fo...  3.44 us
    ppermute x1, starting transfers between devices, second_exchange(): lax.ppermute(down, 'gx', to_down)  2.8 us
    ppermute x1, waiting for transfers between devices, first_exchange(): near_in = lax.ppermute(near, AXES, grid_pairs(near_move))  2.39 us
  transfers between devices with their start and end apart: 12, of which 4 were waited for; matrix products, arithmetic and copies ran while one was open for 0% of the time, Pallas kernels for 1%

profile of v7, /device:TPU:8, one launch (start us, length us, event | category | flops | bytes accessed | tf_op | source)
XLA Modules:
  0.0 49.0 jit_solution(9230051020179123923)
XLA Ops:
  0.6 1.8 %shard_map.67 = (f32[2,7,4,16,128]{4,3,2,1,0:T(8,128)S(1)}, f32[2,7,4,16,128]{4,3,2,1,0:T(8,128)S(1)}, f32[4,16,128]{2,1,0:T(8,128)S(1)}, f32[2,4,16,128]{3,2,1,...) custom-call(f32[2,7,4,16,128]{4,3,2,1,0:T(8,128)} %f_hbm.1, ...), custom_call_target="tpu_custom_call" | custom-call | tf_op jit(solution)/shard_map/pallas_call | solution.py:416
  2.4 2.2 %collective-permute-start.1 = (f32[160,128]{1,0:T(8,128)S(1)}, f32[160,128]{1,0:T(8,128)S(1)}, u32[]{:S(2)}, u32[]{:S(2)}) collective-permute-start(f32[160,128]{1,0:T(8,128)S(1)} %get-tuple-element.30), channel_id=1, source_target_pairs={{64,0},{128,64},{192,128},{256,192},{320,256},{384,320},{448,384},... | collective-permute-start | bytes 245768 | tf_op jit(solution)/shard_map/ppermute | solution.py:481
  4.6 0.0 collective-permute-start
  4.6 4.7 %collective-permute-done.below_ref = f32[96,128]{1,0:T(8,128)S(1)} collective-permute-done((f32[96,128]{1,0:T(8,128)S(1)}, f32[96,128]{1,0:T(8,128)S(1)}, u32[]{:S(2)}, u32[]{:S(2)}) %collective-permute-start) | collective-permute-done | bytes 49184 | tf_op jit(solution)/shard_map/ppermute | solution.py:482
  9.4 0.0 collective-permute-done.1.above_ref
  9.4 13.2 %collective-permute-start.3 = (f32[160,128]{1,0:T(8,128)S(1)}, f32[160,128]{1,0:T(8,128)S(1)}, u32[]{:S(2)}, u32[]{:S(2)}) collective-permute-start(f32[160,128]{1,0:T(8,128)S(1)} %get-tuple-element.34), channel_id=1, source_target_pairs={{0,56},{1,57},{2,58},{3,59},{4,60},{5,61},{6,62},{7,63},{8,16},{9,... | collective-permute-start | bytes 245768 | tf_op jit(solution)/shard_map/ppermute | solution.py:485
  22.5 1.9 %collective-permute-start.4 = (f32[40,128]{1,0:T(8,128)S(1)}, f32[40,128]{1,0:T(8,128)S(1)}, u32[]{:S(2)}, u32[]{:S(2)}) collective-permute-start(f32[40,128]{1,0:T(8,128)S(1)} %get-tuple-element.35), channel_id=1, source_target_pairs={{0,8},{1,9},{2,10},{3,11},{4,12},{5,13},{6,14},{7,15},{8,0},{9,1},... | collective-permute-start | bytes 61448 | tf_op jit(solution)/shard_map/ppermute | solution.py:487
  24.5 0.7 %collective-permute-start.2 = (f32[32,128]{1,0:T(8,128)S(1)}, f32[32,128]{1,0:T(8,128)S(1)}, u32[]{:S(2)}, u32[]{:S(2)}) collective-permute-start(f32[32,128]{1,0:T(8,128)S(1)} %get-tuple-element.33), channel_id=1, source_target_pairs={{64,71},{65,66},{66,65},{67,68},{68,67},{69,70},{70,69},{71,64},{7... | collective-permute-start | bytes 49160 | tf_op jit(solution)/shard_map/ppermute | solution.py:484
  25.1 0.7 %collective-permute-start.6 = (f32[136,128]{1,0:T(8,128)S(1)}, f32[136,128]{1,0:T(8,128)S(1)}, u32[]{:S(2)}, u32[]{:S(2)}) collective-permute-start(f32[136,128]{1,0:T(8,128)S(1)} %get-tuple-element.41), channel_id=1, source_target_pairs={{0,63},{3,60},{4,59},{7,56},{9,18},{10,17},{13,22},{14,21},{17,10}... | collective-permute-start | bytes 208904 | tf_op jit(solution)/shard_map/ppermute | solution.py:486
  25.8 0.0 collective-permute-done.2.z_ref
  25.8 2.4 %collective-permute-done.4.near_ref = f32[40,128]{1,0:T(8,128)S(1)} collective-permute-done((f32[40,128]{1,0:T(8,128)S(1)}, f32[40,128]{1,0:T(8,128)S(1)}, u32[]{:S(2)}, u32[]{:S(2)}) %collective-permute-start.4) | collective-permute-done | bytes 20512 | tf_op jit(solution)/shard_map/ppermute | solution.py:487
  28.2 0.0 collective-permute-done.3.y_ref
  28.2 1.9 %collective-permute-start.5 = (f32[96,128]{1,0:T(8,128)S(1)}, f32[96,128]{1,0:T(8,128)S(1)}, u32[]{:S(2)}, u32[]{:S(2)}) collective-permute-start(f32[96,128]{1,0:T(8,128)S(1)} %shard_map.69), channel_id=1, source_target_pairs={{0,64},{64,0},{128,192},{192,128},{256,320},{320,256},{384,448},{4... | collective-permute-start | bytes 147464 | tf_op jit(solution)/shard_map/ppermute | solution.py:489
  30.2 1.2 %collective-permute-done.5.back_ref = f32[96,128]{1,0:T(8,128)S(1)} collective-permute-done((f32[96,128]{1,0:T(8,128)S(1)}, f32[96,128]{1,0:T(8,128)S(1)}, u32[]{:S(2)}, u32[]{:S(2)}) %collective-permute-start.5) | collective-permute-done | bytes 49184 | tf_op jit(solution)/shard_map/ppermute | solution.py:489
  31.4 0.4 shard_map.70
  31.8 0.2 collective-permute-start.7
  31.9 2.8 %collective-permute-start.8 = (f32[48,128]{1,0:T(8,128)S(1)}, f32[48,128]{1,0:T(8,128)S(1)}, u32[]{:S(2)}, u32[]{:S(2)}) collective-permute-start(f32[48,128]{1,0:T(8,128)S(1)} %get-tuple-element.43), channel_id=1, source_target_pairs={{64,0},{128,64},{192,128},{256,192},{320,256},{384,320},{448,384},... | collective-permute-start | bytes 73736 | tf_op jit(solution)/shard_map/ppermute | solution.py:497
  34.7 3.5 %collective-permute-start.11 = (f32[48,128]{1,0:T(8,128)S(1)}, f32[48,128]{1,0:T(8,128)S(1)}, u32[]{:S(2)}, u32[]{:S(2)}) collective-permute-start(f32[48,128]{1,0:T(8,128)S(1)} %get-tuple-element.46), channel_id=1, source_target_pairs={{1,2},{2,1},{5,6},{6,5},{8,16},{11,19},{12,20},{15,23},{16,8},{19,... | collective-permute-start | bytes 73736 | tf_op jit(solution)/shard_map/ppermute | solution.py:500
  38.2 4.0 %collective-permute-start.10 = (f32[24,128]{1,0:T(8,128)S(1)}, f32[24,128]{1,0:T(8,128)S(1)}, u32[]{:S(2)}, u32[]{:S(2)}) collective-permute-start(f32[24,128]{1,0:T(8,128)S(1)} %get-tuple-element.45), channel_id=1, source_target_pairs={{0,1},{1,0},{2,3},{3,2},{4,5},{5,4},{6,7},{7,6},{8,9},{9,8},{10,11... | collective-permute-start | bytes 36872 | tf_op jit(solution)/shard_map/ppermute | solution.py:499
  42.2 0.0 collective-permute-done.6.diag_ref
  42.2 1.9 %collective-permute-start.9 = (f32[16,128]{1,0:T(8,128)S(1)}, f32[16,128]{1,0:T(8,128)S(1)}, u32[]{:S(2)}, u32[]{:S(2)}) collective-permute-start(f32[16,128]{1,0:T(8,128)S(1)} %get-tuple-element.44), channel_id=1, source_target_pairs={{0,8},{8,0},{16,24},{24,16},{32,40},{40,32},{48,56},{56,48},{1,9},... | collective-permute-start | bytes 24584 | tf_op jit(solution)/shard_map/ppermute | solution.py:498
  44.1 3.6 %collective-permute-done.9.y1_ref = f32[16,128]{1,0:T(8,128)S(1)} collective-permute-done((f32[16,128]{1,0:T(8,128)S(1)}, f32[16,128]{1,0:T(8,128)S(1)}, u32[]{:S(2)}, u32[]{:S(2)}) %collective-permute-start.9) | collective-permute-done | bytes 8224 | tf_op jit(solution)/shard_map/ppermute | solution.py:498
  47.8 0.0 collective-permute-done.10.z1_ref
  47.8 0.0 collective-permute-done.7.below_ref
  47.8 0.0 collective-permute-done.8.above_ref
  47.8 0.0 collective-permute-done.11.relay_ref
  47.8 1.2 %shard_map.71 = (f32[2,7,4,16,128]{4,3,2,1,0:T(8,128)}, f32[4,16,128]{2,1,0:T(8,128)}, f32[2,4,16,128]{3,2,1,0:T(8,128)}) custom-call(f32[2,7,4,16,128]{4,3,2,1,0:T(8,128)S(1)} %get-tuple-element.25.f_ref, f32[4,16,128]{2,1,0:T(8,128)S(1)} %get-tuple-element.26.r_ref, f32[2,4,16,128]{3,2,1,0:T(8,128)S(1)} %get-tuple-element.27.t_ref, ...), custom_call_target="tpu_custom_call" | custom-call | tf_op jit(solution)/shard_map/pallas_call | solution.py:416
  (2 shorter events, 0.0 us)
Async XLA Ops:
  2.4 6.9 %collective-permute-start.1 = (f32[160,128]{1,0:T(8,128)S(1)}, f32[160,128]{1,0:T(8,128)S(1)}, u32[]{:S(2)}, u32[]{:S(2)}) collective-permute-start(f32[160,128]{1,0:T(8,128)S(1)} %get-tuple-element.30), channel_id=1, source_target_pairs={{64,0},{128,64},{192,128},{256,192},{320,256},{384,320},{448,384},... | collective-permute-start | bytes 245768 | tf_op jit(solution)/shard_map/ppermute | solution.py:481
  4.6 4.7 %collective-permute-start = (f32[96,128]{1,0:T(8,128)S(1)}, f32[96,128]{1,0:T(8,128)S(1)}, u32[]{:S(2)}, u32[]{:S(2)}) collective-permute-start(f32[96,128]{1,0:T(8,128)S(1)} %get-tuple-element.29), channel_id=1, source_target_pairs={{0,64},{64,128},{128,192},{192,256},{256,320},{320,384},{384,448},... | collective-permute-start | bytes 147464 | tf_op jit(solution)/shard_map/ppermute | solution.py:482
  9.4 18.8 %collective-permute-start.3 = (f32[160,128]{1,0:T(8,128)S(1)}, f32[160,128]{1,0:T(8,128)S(1)}, u32[]{:S(2)}, u32[]{:S(2)}) collective-permute-start(f32[160,128]{1,0:T(8,128)S(1)} %get-tuple-element.34), channel_id=1, source_target_pairs={{0,56},{1,57},{2,58},{3,59},{4,60},{5,61},{6,62},{7,63},{8,16},{9,... | collective-permute-start | bytes 245768 | tf_op jit(solution)/shard_map/ppermute | solution.py:485
  22.5 5.7 %collective-permute-start.4 = (f32[40,128]{1,0:T(8,128)S(1)}, f32[40,128]{1,0:T(8,128)S(1)}, u32[]{:S(2)}, u32[]{:S(2)}) collective-permute-start(f32[40,128]{1,0:T(8,128)S(1)} %get-tuple-element.35), channel_id=1, source_target_pairs={{0,8},{1,9},{2,10},{3,11},{4,12},{5,13},{6,14},{7,15},{8,0},{9,1},... | collective-permute-start | bytes 61448 | tf_op jit(solution)/shard_map/ppermute | solution.py:487
  24.5 1.3 %collective-permute-start.2 = (f32[32,128]{1,0:T(8,128)S(1)}, f32[32,128]{1,0:T(8,128)S(1)}, u32[]{:S(2)}, u32[]{:S(2)}) collective-permute-start(f32[32,128]{1,0:T(8,128)S(1)} %get-tuple-element.33), channel_id=1, source_target_pairs={{64,71},{65,66},{66,65},{67,68},{68,67},{69,70},{70,69},{71,64},{7... | collective-permute-start | bytes 49160 | tf_op jit(solution)/shard_map/ppermute | solution.py:484
  25.1 17.1 %collective-permute-start.6 = (f32[136,128]{1,0:T(8,128)S(1)}, f32[136,128]{1,0:T(8,128)S(1)}, u32[]{:S(2)}, u32[]{:S(2)}) collective-permute-start(f32[136,128]{1,0:T(8,128)S(1)} %get-tuple-element.41), channel_id=1, source_target_pairs={{0,63},{3,60},{4,59},{7,56},{9,18},{10,17},{13,22},{14,21},{17,10}... | collective-permute-start | bytes 208904 | tf_op jit(solution)/shard_map/ppermute | solution.py:486
  28.2 3.1 %collective-permute-start.5 = (f32[96,128]{1,0:T(8,128)S(1)}, f32[96,128]{1,0:T(8,128)S(1)}, u32[]{:S(2)}, u32[]{:S(2)}) collective-permute-start(f32[96,128]{1,0:T(8,128)S(1)} %shard_map.69), channel_id=1, source_target_pairs={{0,64},{64,0},{128,192},{192,128},{256,320},{320,256},{384,448},{4... | collective-permute-start | bytes 147464 | tf_op jit(solution)/shard_map/ppermute | solution.py:489
  31.8 16.0 %collective-permute-start.7 = (f32[48,128]{1,0:T(8,128)S(1)}, f32[48,128]{1,0:T(8,128)S(1)}, u32[]{:S(2)}, u32[]{:S(2)}) collective-permute-start(f32[48,128]{1,0:T(8,128)S(1)} %get-tuple-element.42), channel_id=1, source_target_pairs={{0,64},{64,128},{128,192},{192,256},{256,320},{320,384},{384,448},... | collective-permute-start | bytes 73736 | tf_op jit(solution)/shard_map/ppermute | solution.py:496
  31.9 15.8 %collective-permute-start.8 = (f32[48,128]{1,0:T(8,128)S(1)}, f32[48,128]{1,0:T(8,128)S(1)}, u32[]{:S(2)}, u32[]{:S(2)}) collective-permute-start(f32[48,128]{1,0:T(8,128)S(1)} %get-tuple-element.43), channel_id=1, source_target_pairs={{64,0},{128,64},{192,128},{256,192},{320,256},{384,320},{448,384},... | collective-permute-start | bytes 73736 | tf_op jit(solution)/shard_map/ppermute | solution.py:497
  34.7 13.1 %collective-permute-start.11 = (f32[48,128]{1,0:T(8,128)S(1)}, f32[48,128]{1,0:T(8,128)S(1)}, u32[]{:S(2)}, u32[]{:S(2)}) collective-permute-start(f32[48,128]{1,0:T(8,128)S(1)} %get-tuple-element.46), channel_id=1, source_target_pairs={{1,2},{2,1},{5,6},{6,5},{8,16},{11,19},{12,20},{15,23},{16,8},{19,... | collective-permute-start | bytes 73736 | tf_op jit(solution)/shard_map/ppermute | solution.py:500
  38.2 9.6 %collective-permute-start.10 = (f32[24,128]{1,0:T(8,128)S(1)}, f32[24,128]{1,0:T(8,128)S(1)}, u32[]{:S(2)}, u32[]{:S(2)}) collective-permute-start(f32[24,128]{1,0:T(8,128)S(1)} %get-tuple-element.45), channel_id=1, source_target_pairs={{0,1},{1,0},{2,3},{3,2},{4,5},{5,4},{6,7},{7,6},{8,9},{9,8},{10,11... | collective-permute-start | bytes 36872 | tf_op jit(solution)/shard_map/ppermute | solution.py:499
  42.2 5.5 %collective-permute-start.9 = (f32[16,128]{1,0:T(8,128)S(1)}, f32[16,128]{1,0:T(8,128)S(1)}, u32[]{:S(2)}, u32[]{:S(2)}) collective-permute-start(f32[16,128]{1,0:T(8,128)S(1)} %get-tuple-element.44), channel_id=1, source_target_pairs={{0,8},{8,0},{16,24},{24,16},{32,40},{40,32},{48,56},{56,48},{1,9},... | collective-permute-start | bytes 24584 | tf_op jit(solution)/shard_map/ppermute | solution.py:498

commit v8 on v6

--- a/solution.py
+++ b/solution.py
@@ -191,16 +191,16 @@
         ref[80:160] = jnp.where(even[0], z_all, y_all)
 
 
-def forward_kernel(own0_ref, own1_ref, below_ref, above_ref, y_ref, z_ref, near_ref):
+def forward_kernel(own0_ref, own1_ref, below_ref, above_ref, y_ref, near_ref, z_ref):
     even = parities()
     near_ref[0:16] = own0_ref[...]
     near_ref[16:32] = jnp.where(even[0], above_ref[64:80], below_ref[64:80])
+    near_ref[32:40] = jnp.zeros((8, 128), jnp.float32)
     share = jnp.where(even[0], above_ref[80:160], below_ref[80:160])
     y_ref[0:80] = own1_ref[...]
     y_ref[80:160] = share
     z_ref[0:16] = own1_ref[0:16]
     z_ref[16:32] = share[0:16]
-    z_ref[32:48] = share[0:16]
 
 
 def back_kernel(z_ref, y_ref, near_ref, out_ref):
@@ -480,7 +480,7 @@
     to_up, to_down = shifts("gx")
     below = lax.ppermute(up, "gx", to_up)
     above = lax.ppermute(down, "gx", to_down)
-    y, z, near = call(forward_kernel, [(160, 128), (48, 128), (32, 128)], own0, own1, below, above)
+    y, near, z = call(forward_kernel, [(160, 128), (40, 128), (32, 128)], own0, own1, below, above)
     z_in = lax.ppermute(z, AXES, grid_pairs(second_z_move))
     y_in = lax.ppermute(y, AXES, grid_pairs(second_y_move))
     diag_in = lax.ppermute(diag, AXES, grid_pairs(diagonal_move))
@@ -503,7 +503,7 @@
 
 def on_device(checkpoint, cotangent, reaction_rate, relax_time):
     inputs = (checkpoint, cotangent, reaction_rate, relax_time)
-    messages = [(160, 128), (160, 128), (16, 128), (80, 128), (152, 128), (24, 128)]
+    messages = [(160, 128), (160, 128), (16, 128), (80, 128), (136, 128), (24, 128)]
     f, g, r, t, *sent, raw = call(
         first_kernel, [a.shape for a in inputs] + messages,
         *(pltpu.with_memory_space_constraint(a, pltpu.HBM) for a in inputs),

time: 48.7 us -> 48.9 us (level)
  the two profiles are of different devices: /device:TPU:8 before, /device:TPU:112 now
where the time goes in v8:
time: 48.9 us; the launch traced here: 48.6 us
  starting transfers between devices  37.4 us (76%)
  waiting for transfers between devices  6.96 us (14%)
  Pallas kernels  3.46 us (7%)
  between operations  0.77 us (2%)
    ppermute x1, starting transfers between devices, second_exchange(): lax.ppermute(z1, 'gz', axis_pairs('gz', 0))  13.7 us
    ppermute x1, starting transfers between devices, first_exchange(): diag_in = lax.ppermute(diag, AXES, grid_pairs(diagonal_move))  5.62 us
    ppermute x1, starting transfers between devices, first_exchange(): y_in = lax.ppermute(y, AXES, grid_pairs(second_y_move))  5.04 us
    ppermute x1, waiting for transfers between devices, second_exchange(): lax.ppermute(y1, 'gy', axis_pairs('gy', 0))  3.62 us
    pallas_call x5, Pallas kernels, call(): pl.pallas_call(kernel, out_shape=[jax.ShapeDtypeStruct(s, jnp.float32) fo...  3.46 us
    ppermute x1, starting transfers between devices, first_exchange(): above = lax.ppermute(down, 'gx', to_down)  2.94 us
    ppermute x1, starting transfers between devices, second_exchange(): lax.ppermute(down, 'gx', to_down)  2.8 us
    ppermute x1, waiting for transfers between devices, first_exchange(): below = lax.ppermute(up, 'gx', to_up)  2.12 us
  transfers between devices with their start and end apart: 12, of which 3 were waited for; matrix products, arithmetic and copies ran while one was open for 0% of the time, Pallas kernels for 1%

profile of v8, /device:TPU:112, one launch (start us, length us, event | category | flops | bytes accessed | tf_op | source)
XLA Modules:
  0.0 48.6 jit_solution(8089301785204090)
XLA Ops:
  0.6 1.8 %shard_map.67 = (f32[2,7,4,16,128]{4,3,2,1,0:T(8,128)S(1)}, f32[2,7,4,16,128]{4,3,2,1,0:T(8,128)S(1)}, f32[4,16,128]{2,1,0:T(8,128)S(1)}, f32[2,4,16,128]{3,2,1,...) custom-call(f32[2,7,4,16,128]{4,3,2,1,0:T(8,128)} %f_hbm.1, ...), custom_call_target="tpu_custom_call" | custom-call | tf_op jit(solution)/shard_map/pallas_call | solution.py:416
  2.4 0.0 collective-permute-start
  2.4 2.9 %collective-permute-start.1 = (f32[160,128]{1,0:T(8,128)S(1)}, f32[160,128]{1,0:T(8,128)S(1)}, u32[]{:S(2)}, u32[]{:S(2)}) collective-permute-start(f32[160,128]{1,0:T(8,128)S(1)} %get-tuple-element.30), channel_id=1, source_target_pairs={{64,0},{128,64},{192,128},{256,192},{320,256},{384,320},{448,384},... | collective-permute-start | bytes 245768 | tf_op jit(solution)/shard_map/ppermute | solution.py:482
  5.4 2.1 %collective-permute-done.below_ref = f32[160,128]{1,0:T(8,128)S(1)} collective-permute-done((f32[160,128]{1,0:T(8,128)S(1)}, f32[160,128]{1,0:T(8,128)S(1)}, u32[]{:S(2)}, u32[]{:S(2)}) %collective-permute-start) | collective-permute-done | bytes 81952 | tf_op jit(solution)/shard_map/ppermute | solution.py:481
  7.5 0.0 collective-permute-done.1.above_ref
  7.5 5.0 %collective-permute-start.3 = (f32[160,128]{1,0:T(8,128)S(1)}, f32[160,128]{1,0:T(8,128)S(1)}, u32[]{:S(2)}, u32[]{:S(2)}) collective-permute-start(f32[160,128]{1,0:T(8,128)S(1)} %get-tuple-element.34), channel_id=1, source_target_pairs={{0,56},{1,57},{2,58},{3,59},{4,60},{5,61},{6,62},{7,63},{8,16},{9,... | collective-permute-start | bytes 245768 | tf_op jit(solution)/shard_map/ppermute | solution.py:485
  12.6 1.9 %collective-permute-start.4 = (f32[40,128]{1,0:T(8,128)S(1)}, f32[40,128]{1,0:T(8,128)S(1)}, u32[]{:S(2)}, u32[]{:S(2)}) collective-permute-start(f32[40,128]{1,0:T(8,128)S(1)} %get-tuple-element.35), channel_id=1, source_target_pairs={{0,8},{1,9},{2,10},{3,11},{4,12},{5,13},{6,14},{7,15},{8,0},{9,1},... | collective-permute-start | bytes 61448 | tf_op jit(solution)/shard_map/ppermute | solution.py:487
  14.5 0.7 %collective-permute-start.2 = (f32[32,128]{1,0:T(8,128)S(1)}, f32[32,128]{1,0:T(8,128)S(1)}, u32[]{:S(2)}, u32[]{:S(2)}) collective-permute-start(f32[32,128]{1,0:T(8,128)S(1)} %get-tuple-element.33), channel_id=1, source_target_pairs={{64,71},{65,66},{66,65},{67,68},{68,67},{69,70},{70,69},{71,64},{7... | collective-permute-start | bytes 49160 | tf_op jit(solution)/shard_map/ppermute | solution.py:484
  15.2 5.6 %collective-permute-start.6 = (f32[136,128]{1,0:T(8,128)S(1)}, f32[136,128]{1,0:T(8,128)S(1)}, u32[]{:S(2)}, u32[]{:S(2)}) collective-permute-start(f32[136,128]{1,0:T(8,128)S(1)} %get-tuple-element.41), channel_id=1, source_target_pairs={{0,63},{3,60},{4,59},{7,56},{9,18},{10,17},{13,22},{14,21},{17,10}... | collective-permute-start | bytes 208904 | tf_op jit(solution)/shard_map/ppermute | solution.py:486
  20.8 0.0 collective-permute-done.2.z_ref
  20.8 0.0 collective-permute-done.4.near_ref
  20.8 0.0 collective-permute-done.3.y_ref
  20.9 1.9 %collective-permute-start.5 = (f32[96,128]{1,0:T(8,128)S(1)}, f32[96,128]{1,0:T(8,128)S(1)}, u32[]{:S(2)}, u32[]{:S(2)}) collective-permute-start(f32[96,128]{1,0:T(8,128)S(1)} %shard_map.69), channel_id=1, source_target_pairs={{0,64},{64,0},{128,192},{192,128},{256,320},{320,256},{384,448},{4... | collective-permute-start | bytes 147464 | tf_op jit(solution)/shard_map/ppermute | solution.py:489
  22.8 1.2 %collective-permute-done.5.back_ref = f32[96,128]{1,0:T(8,128)S(1)} collective-permute-done((f32[96,128]{1,0:T(8,128)S(1)}, f32[96,128]{1,0:T(8,128)S(1)}, u32[]{:S(2)}, u32[]{:S(2)}) %collective-permute-start.5) | collective-permute-done | bytes 49184 | tf_op jit(solution)/shard_map/ppermute | solution.py:489
  24.0 0.4 shard_map.70
  24.4 0.2 collective-permute-start.7
  24.6 2.8 %collective-permute-start.8 = (f32[48,128]{1,0:T(8,128)S(1)}, f32[48,128]{1,0:T(8,128)S(1)}, u32[]{:S(2)}, u32[]{:S(2)}) collective-permute-start(f32[48,128]{1,0:T(8,128)S(1)} %get-tuple-element.43), channel_id=1, source_target_pairs={{64,0},{128,64},{192,128},{256,192},{320,256},{384,320},{448,384},... | collective-permute-start | bytes 73736 | tf_op jit(solution)/shard_map/ppermute | solution.py:497
  27.3 0.7 %collective-permute-start.11 = (f32[48,128]{1,0:T(8,128)S(1)}, f32[48,128]{1,0:T(8,128)S(1)}, u32[]{:S(2)}, u32[]{:S(2)}) collective-permute-start(f32[48,128]{1,0:T(8,128)S(1)} %get-tuple-element.46), channel_id=1, source_target_pairs={{1,2},{2,1},{5,6},{6,5},{8,16},{11,19},{12,20},{15,23},{16,8},{19,... | collective-permute-start | bytes 73736 | tf_op jit(solution)/shard_map/ppermute | solution.py:500
  28.0 13.7 %collective-permute-start.10 = (f32[24,128]{1,0:T(8,128)S(1)}, f32[24,128]{1,0:T(8,128)S(1)}, u32[]{:S(2)}, u32[]{:S(2)}) collective-permute-start(f32[24,128]{1,0:T(8,128)S(1)} %get-tuple-element.45), channel_id=1, source_target_pairs={{0,1},{1,0},{2,3},{3,2},{4,5},{5,4},{6,7},{7,6},{8,9},{9,8},{10,11... | collective-permute-start | bytes 36872 | tf_op jit(solution)/shard_map/ppermute | solution.py:499
  41.8 0.0 collective-permute-done.6.diag_ref
  41.8 1.9 %collective-permute-start.9 = (f32[16,128]{1,0:T(8,128)S(1)}, f32[16,128]{1,0:T(8,128)S(1)}, u32[]{:S(2)}, u32[]{:S(2)}) collective-permute-start(f32[16,128]{1,0:T(8,128)S(1)} %get-tuple-element.44), channel_id=1, source_target_pairs={{0,8},{8,0},{16,24},{24,16},{32,40},{40,32},{48,56},{56,48},{1,9},... | collective-permute-start | bytes 24584 | tf_op jit(solution)/shard_map/ppermute | solution.py:498
  43.7 3.6 %collective-permute-done.9.y1_ref = f32[16,128]{1,0:T(8,128)S(1)} collective-permute-done((f32[16,128]{1,0:T(8,128)S(1)}, f32[16,128]{1,0:T(8,128)S(1)}, u32[]{:S(2)}, u32[]{:S(2)}) %collective-permute-start.9) | collective-permute-done | bytes 8224 | tf_op jit(solution)/shard_map/ppermute | solution.py:498
  47.3 0.0 collective-permute-done.10.z1_ref
  47.3 0.0 collective-permute-done.7.below_ref
  47.3 0.0 collective-permute-done.8.above_ref
  47.3 0.0 collective-permute-done.11.relay_ref
  47.3 1.2 %shard_map.71 = (f32[2,7,4,16,128]{4,3,2,1,0:T(8,128)}, f32[4,16,128]{2,1,0:T(8,128)}, f32[2,4,16,128]{3,2,1,0:T(8,128)}) custom-call(f32[2,7,4,16,128]{4,3,2,1,0:T(8,128)S(1)} %get-tuple-element.25.f_ref, f32[4,16,128]{2,1,0:T(8,128)S(1)} %get-tuple-element.26.r_ref, f32[2,4,16,128]{3,2,1,0:T(8,128)S(1)} %get-tuple-element.27.t_ref, ...), custom_call_target="tpu_custom_call" | custom-call | tf_op jit(solution)/shard_map/pallas_call | solution.py:416
  (2 shorter events, 0.0 us)
Async XLA Ops:
  2.4 5.1 %collective-permute-start = (f32[160,128]{1,0:T(8,128)S(1)}, f32[160,128]{1,0:T(8,128)S(1)}, u32[]{:S(2)}, u32[]{:S(2)}) collective-permute-start(f32[160,128]{1,0:T(8,128)S(1)} %get-tuple-element.29), channel_id=1, source_target_pairs={{0,64},{64,128},{128,192},{192,256},{256,320},{320,384},{384,448},... | collective-permute-start | bytes 245768 | tf_op jit(solution)/shard_map/ppermute | solution.py:481
  2.4 5.1 %collective-permute-start.1 = (f32[160,128]{1,0:T(8,128)S(1)}, f32[160,128]{1,0:T(8,128)S(1)}, u32[]{:S(2)}, u32[]{:S(2)}) collective-permute-start(f32[160,128]{1,0:T(8,128)S(1)} %get-tuple-element.30), channel_id=1, source_target_pairs={{64,0},{128,64},{192,128},{256,192},{320,256},{384,320},{448,384},... | collective-permute-start | bytes 245768 | tf_op jit(solution)/shard_map/ppermute | solution.py:482
  7.5 13.3 %collective-permute-start.3 = (f32[160,128]{1,0:T(8,128)S(1)}, f32[160,128]{1,0:T(8,128)S(1)}, u32[]{:S(2)}, u32[]{:S(2)}) collective-permute-start(f32[160,128]{1,0:T(8,128)S(1)} %get-tuple-element.34), channel_id=1, source_target_pairs={{0,56},{1,57},{2,58},{3,59},{4,60},{5,61},{6,62},{7,63},{8,16},{9,... | collective-permute-start | bytes 245768 | tf_op jit(solution)/shard_map/ppermute | solution.py:485
  12.6 8.2 %collective-permute-start.4 = (f32[40,128]{1,0:T(8,128)S(1)}, f32[40,128]{1,0:T(8,128)S(1)}, u32[]{:S(2)}, u32[]{:S(2)}) collective-permute-start(f32[40,128]{1,0:T(8,128)S(1)} %get-tuple-element.35), channel_id=1, source_target_pairs={{0,8},{1,9},{2,10},{3,11},{4,12},{5,13},{6,14},{7,15},{8,0},{9,1},... | collective-permute-start | bytes 61448 | tf_op jit(solution)/shard_map/ppermute | solution.py:487
  14.5 6.3 %collective-permute-start.2 = (f32[32,128]{1,0:T(8,128)S(1)}, f32[32,128]{1,0:T(8,128)S(1)}, u32[]{:S(2)}, u32[]{:S(2)}) collective-permute-start(f32[32,128]{1,0:T(8,128)S(1)} %get-tuple-element.33), channel_id=1, source_target_pairs={{64,71},{65,66},{66,65},{67,68},{68,67},{69,70},{70,69},{71,64},{7... | collective-permute-start | bytes 49160 | tf_op jit(solution)/shard_map/ppermute | solution.py:484
  15.2 26.6 %collective-permute-start.6 = (f32[136,128]{1,0:T(8,128)S(1)}, f32[136,128]{1,0:T(8,128)S(1)}, u32[]{:S(2)}, u32[]{:S(2)}) collective-permute-start(f32[136,128]{1,0:T(8,128)S(1)} %get-tuple-element.41), channel_id=1, source_target_pairs={{0,63},{3,60},{4,59},{7,56},{9,18},{10,17},{13,22},{14,21},{17,10}... | collective-permute-start | bytes 208904 | tf_op jit(solution)/shard_map/ppermute | solution.py:486
  20.9 3.1 %collective-permute-start.5 = (f32[96,128]{1,0:T(8,128)S(1)}, f32[96,128]{1,0:T(8,128)S(1)}, u32[]{:S(2)}, u32[]{:S(2)}) collective-permute-start(f32[96,128]{1,0:T(8,128)S(1)} %shard_map.69), channel_id=1, source_target_pairs={{0,64},{64,0},{128,192},{192,128},{256,320},{320,256},{384,448},{4... | collective-permute-start | bytes 147464 | tf_op jit(solution)/shard_map/ppermute | solution.py:489
  24.4 22.9 %collective-permute-start.7 = (f32[48,128]{1,0:T(8,128)S(1)}, f32[48,128]{1,0:T(8,128)S(1)}, u32[]{:S(2)}, u32[]{:S(2)}) collective-permute-start(f32[48,128]{1,0:T(8,128)S(1)} %get-tuple-element.42), channel_id=1, source_target_pairs={{0,64},{64,128},{128,192},{192,256},{256,320},{320,384},{384,448},... | collective-permute-start | bytes 73736 | tf_op jit(solution)/shard_map/ppermute | solution.py:496
  24.6 22.8 %collective-permute-start.8 = (f32[48,128]{1,0:T(8,128)S(1)}, f32[48,128]{1,0:T(8,128)S(1)}, u32[]{:S(2)}, u32[]{:S(2)}) collective-permute-start(f32[48,128]{1,0:T(8,128)S(1)} %get-tuple-element.43), channel_id=1, source_target_pairs={{64,0},{128,64},{192,128},{256,192},{320,256},{384,320},{448,384},... | collective-permute-start | bytes 73736 | tf_op jit(solution)/shard_map/ppermute | solution.py:497
  27.3 20.0 %collective-permute-start.11 = (f32[48,128]{1,0:T(8,128)S(1)}, f32[48,128]{1,0:T(8,128)S(1)}, u32[]{:S(2)}, u32[]{:S(2)}) collective-permute-start(f32[48,128]{1,0:T(8,128)S(1)} %get-tuple-element.46), channel_id=1, source_target_pairs={{1,2},{2,1},{5,6},{6,5},{8,16},{11,19},{12,20},{15,23},{16,8},{19,... | collective-permute-start | bytes 73736 | tf_op jit(solution)/shard_map/ppermute | solution.py:500
  28.0 19.3 %collective-permute-start.10 = (f32[24,128]{1,0:T(8,128)S(1)}, f32[24,128]{1,0:T(8,128)S(1)}, u32[]{:S(2)}, u32[]{:S(2)}) collective-permute-start(f32[24,128]{1,0:T(8,128)S(1)} %get-tuple-element.45), channel_id=1, source_target_pairs={{0,1},{1,0},{2,3},{3,2},{4,5},{5,4},{6,7},{7,6},{8,9},{9,8},{10,11... | collective-permute-start | bytes 36872 | tf_op jit(solution)/shard_map/ppermute | solution.py:499
  41.8 5.5 %collective-permute-start.9 = (f32[16,128]{1,0:T(8,128)S(1)}, f32[16,128]{1,0:T(8,128)S(1)}, u32[]{:S(2)}, u32[]{:S(2)}) collective-permute-start(f32[16,128]{1,0:T(8,128)S(1)} %get-tuple-element.44), channel_id=1, source_target_pairs={{0,8},{8,0},{16,24},{24,16},{32,40},{40,32},{48,56},{56,48},{1,9},... | collective-permute-start | bytes 24584 | tf_op jit(solution)/shard_map/ppermute | solution.py:498

commit v9 on v6

--- a/solution.py
+++ b/solution.py
@@ -137,10 +137,11 @@
     ]
     for copy in copies:
         copy.start()
-    for copy in copies:
-        copy.wait()
+    for i in (0, 2, 3):
+        copies[i].wait()
     even = parities()
     c, _, inverse, rate = collided(f_ref, r_ref, t_ref)
+    copies[1].wait()
     g = [[load(g_ref, s, q) for q in range(7)] for s in range(2)]
     up, down = [], []
     for axis in range(3):
@@ -368,7 +369,8 @@
 
 def third_kernel(
     f_ref, r_ref, t_ref, later_ref, rate_late_ref, relax_late_ref, deep_ref, raw_ref, diag_ref,
-    below_ref, above_ref, y1_ref, z1_ref, relay_ref, state_ref, rate_ref, relax_ref,
+    below_ref, above_ref, y1_ref, z1_ref, relay_ref, state_hbm, rate_hbm, relax_hbm,
+    state_ref, rate_ref, relax_ref, sems,
 ):
     even = parities()
     nx = r_ref.shape[0]
@@ -399,6 +401,7 @@
         for axis in range(3):
             upstream[s].append(moved(load(later_ref, s, 1 + 2 * axis), axis, 1, above[axis], s))
             upstream[s].append(moved(load(later_ref, s, 2 + 2 * axis), axis, -1, below[axis], s))
+    copies = []
     for x in range(nx):
         up = [[upstream[s][q][x] for q in range(7)] for s in range(2)]
         state = [[f_ref[s, q, x] for q in range(7)] for s in range(2)]
@@ -410,14 +413,23 @@
             relax_ref[s, x] = relax_late_ref[s, x] + relax_part[s]
             for q in range(7):
                 state_ref[s, q, x] = earlier[s][q]
-
-
-def call(kernel, shapes, *args, source=pltpu.VMEM, scratch=()):
+        copies += [
+            pltpu.make_async_copy(state_ref.at[:, :, x], state_hbm.at[:, :, x], sems.at[3 * x]),
+            pltpu.make_async_copy(rate_ref.at[x], rate_hbm.at[x], sems.at[3 * x + 1]),
+            pltpu.make_async_copy(relax_ref.at[:, x], relax_hbm.at[:, x], sems.at[3 * x + 2]),
+        ]
+        for copy in copies[-3:]:
+            copy.start()
+    for copy in copies:
+        copy.wait()
+
+
+def call(kernel, shapes, *args, source=pltpu.VMEM, target=pltpu.VMEM, scratch=()):
     return pl.pallas_call(
         kernel,
         out_shape=[jax.ShapeDtypeStruct(s, jnp.float32) for s in shapes],
         in_specs=[pl.BlockSpec(memory_space=source)] * len(args),
-        out_specs=[pl.BlockSpec(memory_space=pltpu.VMEM)] * len(shapes),
+        out_specs=[pl.BlockSpec(memory_space=target)] * len(shapes),
         scratch_shapes=list(scratch),
         compiler_params=pltpu.CompilerParams(vmem_limit_bytes=32 * 1024 * 1024),
     )(*args)
@@ -518,7 +530,8 @@
     return tuple(
         call(
             third_kernel, [f.shape, r.shape, t.shape],
-            f, r, t, later, rate_late, relax_late, deep, raw, diag_in, *received,
+            f, r, t, later, rate_late, relax_late, deep, raw, diag_in, *received, target=pltpu.HBM,
+            scratch=[pltpu.VMEM(a.shape, jnp.float32) for a in (f, r, t)] + [pltpu.SemaphoreType.DMA((3 * r.shape[0],))],
         )
     )
 

time: 48.7 us -> 48.7 us (level)
  no operation moved by 1% of the time
where the time goes in v9:
time: 48.7 us; the launch traced here: 48.3 us
  starting transfers between devices  36.4 us (75%)
  waiting for transfers between devices  7.64 us (16%)
  Pallas kernels  3.51 us (7%)
  between operations  0.75 us (2%)
    ppermute x1, starting transfers between devices, first_exchange(): y_in = lax.ppermute(y, AXES, grid_pairs(second_y_move))  13.2 us
    ppermute x1, starting transfers between devices, second_exchange(): lax.ppermute(y1, 'gy', axis_pairs('gy', 0))  4.92 us
    ppermute x1, starting transfers between devices, first_exchange(): back_in = lax.ppermute(back, 'gx', axis_pairs('gx', 0))  4.6 us
    pallas_call x5, Pallas kernels, call(): pl.pallas_call(kernel, out_shape=[jax.ShapeDtypeStruct(s, jnp.float32) fo...  3.51 us
    ppermute x1, waiting for transfers between devices, first_exchange(): near_in = lax.ppermute(near, AXES, grid_pairs(near_move))  3.03 us
    ppermute x1, starting transfers between devices, first_exchange(): above = lax.ppermute(down, 'gx', to_down)  2.94 us
    ppermute x1, starting transfers between devices, second_exchange(): lax.ppermute(z1, 'gz', axis_pairs('gz', 0))  2.66 us
    ppermute x1, starting transfers between devices, second_exchange(): lax.ppermute(down, 'gx', to_down)  2.61 us
  transfers between devices with their start and end apart: 12, of which 4 were waited for; matrix products, arithmetic and copies ran while one was open for 0% of the time, Pallas kernels for 1%

profile of v9, /device:TPU:8, one launch (start us, length us, event | category | flops | bytes accessed | tf_op | source)
XLA Modules:
  0.0 48.3 jit_solution(16266382806281634204)
XLA Ops:
  0.6 1.8 %shard_map.67 = (f32[2,7,4,16,128]{4,3,2,1,0:T(8,128)S(1)}, f32[2,7,4,16,128]{4,3,2,1,0:T(8,128)S(1)}, f32[4,16,128]{2,1,0:T(8,128)S(1)}, f32[2,4,16,128]{3,2,1,...) custom-call(f32[2,7,4,16,128]{4,3,2,1,0:T(8,128)} %f_hbm.1, ...), custom_call_target="tpu_custom_call" | custom-call | tf_op jit(solution)/shard_map/pallas_call | solution.py:428
  2.4 0.0 collective-permute-start
  2.4 2.9 %collective-permute-start.1 = (f32[160,128]{1,0:T(8,128)S(1)}, f32[160,128]{1,0:T(8,128)S(1)}, u32[]{:S(2)}, u32[]{:S(2)}) collective-permute-start(f32[160,128]{1,0:T(8,128)S(1)} %get-tuple-element.30), channel_id=1, source_target_pairs={{64,0},{128,64},{192,128},{256,192},{320,256},{384,320},{448,384},... | collective-permute-start | bytes 245768 | tf_op jit(solution)/shard_map/ppermute | solution.py:494
  5.4 2.1 %collective-permute-done.below_ref = f32[160,128]{1,0:T(8,128)S(1)} collective-permute-done((f32[160,128]{1,0:T(8,128)S(1)}, f32[160,128]{1,0:T(8,128)S(1)}, u32[]{:S(2)}, u32[]{:S(2)}) %collective-permute-start) | collective-permute-done | bytes 81952 | tf_op jit(solution)/shard_map/ppermute | solution.py:493
  7.5 0.0 collective-permute-done.1.above_ref
  7.5 13.2 %collective-permute-start.3 = (f32[160,128]{1,0:T(8,128)S(1)}, f32[160,128]{1,0:T(8,128)S(1)}, u32[]{:S(2)}, u32[]{:S(2)}) collective-permute-start(f32[160,128]{1,0:T(8,128)S(1)} %get-tuple-element.34), channel_id=1, source_target_pairs={{0,56},{1,57},{2,58},{3,59},{4,60},{5,61},{6,62},{7,63},{8,16},{9,... | collective-permute-start | bytes 245768 | tf_op jit(solution)/shard_map/ppermute | solution.py:497
  20.7 0.7 %collective-permute-start.2 = (f32[48,128]{1,0:T(8,128)S(1)}, f32[48,128]{1,0:T(8,128)S(1)}, u32[]{:S(2)}, u32[]{:S(2)}) collective-permute-start(f32[48,128]{1,0:T(8,128)S(1)} %get-tuple-element.33), channel_id=1, source_target_pairs={{64,71},{65,66},{66,65},{67,68},{68,67},{69,70},{70,69},{71,64},{7... | collective-permute-start | bytes 73736 | tf_op jit(solution)/shard_map/ppermute | solution.py:496
  21.4 1.9 %collective-permute-start.4 = (f32[32,128]{1,0:T(8,128)S(1)}, f32[32,128]{1,0:T(8,128)S(1)}, u32[]{:S(2)}, u32[]{:S(2)}) collective-permute-start(f32[32,128]{1,0:T(8,128)S(1)} %get-tuple-element.35), channel_id=1, source_target_pairs={{0,8},{1,9},{2,10},{3,11},{4,12},{5,13},{6,14},{7,15},{8,0},{9,1},... | collective-permute-start | bytes 49160 | tf_op jit(solution)/shard_map/ppermute | solution.py:499
  23.3 0.7 %collective-permute-start.6 = (f32[152,128]{1,0:T(8,128)S(1)}, f32[152,128]{1,0:T(8,128)S(1)}, u32[]{:S(2)}, u32[]{:S(2)}) collective-permute-start(f32[152,128]{1,0:T(8,128)S(1)} %get-tuple-element.41), channel_id=1, source_target_pairs={{0,63},{3,60},{4,59},{7,56},{9,18},{10,17},{13,22},{14,21},{17,10}... | collective-permute-start | bytes 233480 | tf_op jit(solution)/shard_map/ppermute | solution.py:498
  24.0 3.0 %collective-permute-done.4.near_ref = f32[32,128]{1,0:T(8,128)S(1)} collective-permute-done((f32[32,128]{1,0:T(8,128)S(1)}, f32[32,128]{1,0:T(8,128)S(1)}, u32[]{:S(2)}, u32[]{:S(2)}) %collective-permute-start.4) | collective-permute-done | bytes 16416 | tf_op jit(solution)/shard_map/ppermute | solution.py:499
  27.0 0.0 collective-permute-done.2.z_ref
  27.0 0.0 collective-permute-done.3.y_ref
  27.0 4.6 %collective-permute-start.5 = (f32[96,128]{1,0:T(8,128)S(1)}, f32[96,128]{1,0:T(8,128)S(1)}, u32[]{:S(2)}, u32[]{:S(2)}) collective-permute-start(f32[96,128]{1,0:T(8,128)S(1)} %shard_map.69), channel_id=1, source_target_pairs={{0,64},{64,0},{128,192},{192,128},{256,320},{320,256},{384,448},{4... | collective-permute-start | bytes 147464 | tf_op jit(solution)/shard_map/ppermute | solution.py:501
  31.6 0.9 %collective-permute-done.5.back_ref = f32[96,128]{1,0:T(8,128)S(1)} collective-permute-done((f32[96,128]{1,0:T(8,128)S(1)}, f32[96,128]{1,0:T(8,128)S(1)}, u32[]{:S(2)}, u32[]{:S(2)}) %collective-permute-start.5) | collective-permute-done | bytes 49184 | tf_op jit(solution)/shard_map/ppermute | solution.py:501
  32.5 0.4 shard_map.70
  32.9 0.4 collective-permute-start.7
  33.3 2.6 %collective-permute-start.8 = (f32[48,128]{1,0:T(8,128)S(1)}, f32[48,128]{1,0:T(8,128)S(1)}, u32[]{:S(2)}, u32[]{:S(2)}) collective-permute-start(f32[48,128]{1,0:T(8,128)S(1)} %get-tuple-element.43), channel_id=1, source_target_pairs={{64,0},{128,64},{192,128},{256,192},{320,256},{384,320},{448,384},... | collective-permute-start | bytes 73736 | tf_op jit(solution)/shard_map/ppermute | solution.py:509
  35.9 1.9 %collective-permute-start.11 = (f32[48,128]{1,0:T(8,128)S(1)}, f32[48,128]{1,0:T(8,128)S(1)}, u32[]{:S(2)}, u32[]{:S(2)}) collective-permute-start(f32[48,128]{1,0:T(8,128)S(1)} %get-tuple-element.46), channel_id=1, source_target_pairs={{1,2},{2,1},{5,6},{6,5},{8,16},{11,19},{12,20},{15,23},{16,8},{19,... | collective-permute-start | bytes 73736 | tf_op jit(solution)/shard_map/ppermute | solution.py:512
  37.8 2.7 %collective-permute-start.10 = (f32[24,128]{1,0:T(8,128)S(1)}, f32[24,128]{1,0:T(8,128)S(1)}, u32[]{:S(2)}, u32[]{:S(2)}) collective-permute-start(f32[24,128]{1,0:T(8,128)S(1)} %get-tuple-element.45), channel_id=1, source_target_pairs={{0,1},{1,0},{2,3},{3,2},{4,5},{5,4},{6,7},{7,6},{8,9},{9,8},{10,11... | collective-permute-start | bytes 36872 | tf_op jit(solution)/shard_map/ppermute | solution.py:511
  40.5 0.0 collective-permute-done.6.diag_ref
  40.5 4.9 %collective-permute-start.9 = (f32[16,128]{1,0:T(8,128)S(1)}, f32[16,128]{1,0:T(8,128)S(1)}, u32[]{:S(2)}, u32[]{:S(2)}) collective-permute-start(f32[16,128]{1,0:T(8,128)S(1)} %get-tuple-element.44), channel_id=1, source_target_pairs={{0,8},{8,0},{16,24},{24,16},{32,40},{40,32},{48,56},{56,48},{1,9},... | collective-permute-start | bytes 24584 | tf_op jit(solution)/shard_map/ppermute | solution.py:510
  45.4 1.6 %collective-permute-done.9.y1_ref = f32[16,128]{1,0:T(8,128)S(1)} collective-permute-done((f32[16,128]{1,0:T(8,128)S(1)}, f32[16,128]{1,0:T(8,128)S(1)}, u32[]{:S(2)}, u32[]{:S(2)}) %collective-permute-start.9) | collective-permute-done | bytes 8224 | tf_op jit(solution)/shard_map/ppermute | solution.py:510
  47.0 0.0 collective-permute-done.10.z1_ref
  47.0 0.0 collective-permute-done.7.below_ref
  47.0 0.0 collective-permute-done.8.above_ref
  47.0 0.0 collective-permute-done.11.relay_ref
  47.0 1.3 %shard_map.71 = (f32[2,7,4,16,128]{4,3,2,1,0:T(8,128)}, f32[4,16,128]{2,1,0:T(8,128)}, f32[2,4,16,128]{3,2,1,0:T(8,128)}) custom-call(f32[2,7,4,16,128]{4,3,2,1,0:T(8,128)S(1)} %get-tuple-element.25.f_ref, f32[4,16,128]{2,1,0:T(8,128)S(1)} %get-tuple-element.26.r_ref, f32[2,4,16,128]{3,2,1,0:T(8,128)S(1)} %get-tuple-element.27.t_ref, ...), custom_call_target="tpu_custom_call" | custom-call | tf_op jit(solution)/shard_map/pallas_call | solution.py:428
  (2 shorter events, 0.0 us)
Async XLA Ops:
  2.4 5.1 %collective-permute-start = (f32[160,128]{1,0:T(8,128)S(1)}, f32[160,128]{1,0:T(8,128)S(1)}, u32[]{:S(2)}, u32[]{:S(2)}) collective-permute-start(f32[160,128]{1,0:T(8,128)S(1)} %get-tuple-element.29), channel_id=1, source_target_pairs={{0,64},{64,128},{128,192},{192,256},{256,320},{320,384},{384,448},... | collective-permute-start | bytes 245768 | tf_op jit(solution)/shard_map/ppermute | solution.py:493
  2.4 5.1 %collective-permute-start.1 = (f32[160,128]{1,0:T(8,128)S(1)}, f32[160,128]{1,0:T(8,128)S(1)}, u32[]{:S(2)}, u32[]{:S(2)}) collective-permute-start(f32[160,128]{1,0:T(8,128)S(1)} %get-tuple-element.30), channel_id=1, source_target_pairs={{64,0},{128,64},{192,128},{256,192},{320,256},{384,320},{448,384},... | collective-permute-start | bytes 245768 | tf_op jit(solution)/shard_map/ppermute | solution.py:494
  7.5 19.5 %collective-permute-start.3 = (f32[160,128]{1,0:T(8,128)S(1)}, f32[160,128]{1,0:T(8,128)S(1)}, u32[]{:S(2)}, u32[]{:S(2)}) collective-permute-start(f32[160,128]{1,0:T(8,128)S(1)} %get-tuple-element.34), channel_id=1, source_target_pairs={{0,56},{1,57},{2,58},{3,59},{4,60},{5,61},{6,62},{7,63},{8,16},{9,... | collective-permute-start | bytes 245768 | tf_op jit(solution)/shard_map/ppermute | solution.py:497
  20.7 6.3 %collective-permute-start.2 = (f32[48,128]{1,0:T(8,128)S(1)}, f32[48,128]{1,0:T(8,128)S(1)}, u32[]{:S(2)}, u32[]{:S(2)}) collective-permute-start(f32[48,128]{1,0:T(8,128)S(1)} %get-tuple-element.33), channel_id=1, source_target_pairs={{64,71},{65,66},{66,65},{67,68},{68,67},{69,70},{70,69},{71,64},{7... | collective-permute-start | bytes 73736 | tf_op jit(solution)/shard_map/ppermute | solution.py:496
  21.4 5.6 %collective-permute-start.4 = (f32[32,128]{1,0:T(8,128)S(1)}, f32[32,128]{1,0:T(8,128)S(1)}, u32[]{:S(2)}, u32[]{:S(2)}) collective-permute-start(f32[32,128]{1,0:T(8,128)S(1)} %get-tuple-element.35), channel_id=1, source_target_pairs={{0,8},{1,9},{2,10},{3,11},{4,12},{5,13},{6,14},{7,15},{8,0},{9,1},... | collective-permute-start | bytes 49160 | tf_op jit(solution)/shard_map/ppermute | solution.py:499
  23.3 17.2 %collective-permute-start.6 = (f32[152,128]{1,0:T(8,128)S(1)}, f32[152,128]{1,0:T(8,128)S(1)}, u32[]{:S(2)}, u32[]{:S(2)}) collective-permute-start(f32[152,128]{1,0:T(8,128)S(1)} %get-tuple-element.41), channel_id=1, source_target_pairs={{0,63},{3,60},{4,59},{7,56},{9,18},{10,17},{13,22},{14,21},{17,10}... | collective-permute-start | bytes 233480 | tf_op jit(solution)/shard_map/ppermute | solution.py:498
  27.0 5.5 %collective-permute-start.5 = (f32[96,128]{1,0:T(8,128)S(1)}, f32[96,128]{1,0:T(8,128)S(1)}, u32[]{:S(2)}, u32[]{:S(2)}) collective-permute-start(f32[96,128]{1,0:T(8,128)S(1)} %shard_map.69), channel_id=1, source_target_pairs={{0,64},{64,0},{128,192},{192,128},{256,320},{320,256},{384,448},{4... | collective-permute-start | bytes 147464 | tf_op jit(solution)/shard_map/ppermute | solution.py:501
  32.9 14.1 %collective-permute-start.7 = (f32[48,128]{1,0:T(8,128)S(1)}, f32[48,128]{1,0:T(8,128)S(1)}, u32[]{:S(2)}, u32[]{:S(2)}) collective-permute-start(f32[48,128]{1,0:T(8,128)S(1)} %get-tuple-element.42), channel_id=1, source_target_pairs={{0,64},{64,128},{128,192},{192,256},{256,320},{320,384},{384,448},... | collective-permute-start | bytes 73736 | tf_op jit(solution)/shard_map/ppermute | solution.py:508
  33.3 13.7 %collective-permute-start.8 = (f32[48,128]{1,0:T(8,128)S(1)}, f32[48,128]{1,0:T(8,128)S(1)}, u32[]{:S(2)}, u32[]{:S(2)}) collective-permute-start(f32[48,128]{1,0:T(8,128)S(1)} %get-tuple-element.43), channel_id=1, source_target_pairs={{64,0},{128,64},{192,128},{256,192},{320,256},{384,320},{448,384},... | collective-permute-start | bytes 73736 | tf_op jit(solution)/shard_map/ppermute | solution.py:509
  35.9 11.1 %collective-permute-start.11 = (f32[48,128]{1,0:T(8,128)S(1)}, f32[48,128]{1,0:T(8,128)S(1)}, u32[]{:S(2)}, u32[]{:S(2)}) collective-permute-start(f32[48,128]{1,0:T(8,128)S(1)} %get-tuple-element.46), channel_id=1, source_target_pairs={{1,2},{2,1},{5,6},{6,5},{8,16},{11,19},{12,20},{15,23},{16,8},{19,... | collective-permute-start | bytes 73736 | tf_op jit(solution)/shard_map/ppermute | solution.py:512
  37.8 9.2 %collective-permute-start.10 = (f32[24,128]{1,0:T(8,128)S(1)}, f32[24,128]{1,0:T(8,128)S(1)}, u32[]{:S(2)}, u32[]{:S(2)}) collective-permute-start(f32[24,128]{1,0:T(8,128)S(1)} %get-tuple-element.45), channel_id=1, source_target_pairs={{0,1},{1,0},{2,3},{3,2},{4,5},{5,4},{6,7},{7,6},{8,9},{9,8},{10,11... | collective-permute-start | bytes 36872 | tf_op jit(solution)/shard_map/ppermute | solution.py:511
  40.5 6.5 %collective-permute-start.9 = (f32[16,128]{1,0:T(8,128)S(1)}, f32[16,128]{1,0:T(8,128)S(1)}, u32[]{:S(2)}, u32[]{:S(2)}) collective-permute-start(f32[16,128]{1,0:T(8,128)S(1)} %get-tuple-element.44), channel_id=1, source_target_pairs={{0,8},{8,0},{16,24},{24,16},{32,40},{40,32},{48,56},{56,48},{1,9},... | collective-permute-start | bytes 24584 | tf_op jit(solution)/shard_map/ppermute | solution.py:510

commit v10 on v9

--- a/solution.py
+++ b/solution.py
@@ -79,6 +79,22 @@
                 out = jnp.where(lane == j, part, out)
                 j += 1
     return out
+
+
+def pack_z_shifted(fields, shift, start=0, out=None):
+    lane = lax.broadcasted_iota(jnp.int32, (8, 128), 1)
+    out = jnp.zeros((8, 128), jnp.float32) if out is None else out
+    j = start
+    for v in fields:
+        for plane in v:
+            for h in range(plane.shape[0] // 8):
+                out = jnp.where(lane == j, pltpu.roll(plane[8 * h : 8 * h + 8], shift + j, axis=1), out)
+                j += 1
+    return out
+
+
+def choose(flag, a, b):
+    return [[jnp.where(flag, x, y) for x, y in zip(u, v)] for u, v in zip(a, b)]
 
 
 def cut(v, axis, sign):
@@ -165,17 +181,17 @@
         x_lines.append(jnp.zeros((28 - 4 * len(rate) - len(x_lines), 128), jnp.float32))
         z_lines = [jnp.where(lane < 64, rows_of(a, i), rows_of(b, i)) for a, b in z_edge]
         y_faces.append((raw, jnp.concatenate([raw, deep, *x_lines], axis=0), jnp.concatenate(z_lines, axis=0)))
-        raw = pack_z((up if last else down)[2], last)
-        deep = pack_z(face_fields(g, c, *z_sums, inverse, rate, 2, last), last, 32, raw)
-        y_lines = [[jnp.where(row < 8, u, v) for u, v in zip(a, b)] for a, b in y_edge]
-        x_lines = [a[:-1] + b[-1:] for a, b in x_edge]
-        z_faces.append((raw, deep, pack_z(y_lines + x_lines, last)))
+        z_faces.append(face_fields(g, c, *z_sums, inverse, rate, 2, last))
+    odd = jnp.where(even[2], 0, 1)
+    y_lines = [[jnp.where(row < 8, u, v) for u, v in zip(a, b)] for a, b in y_edge]
+    x_lines = [a[:-1] + b[-1:] for a, b in x_edge]
+    z1 = pack_z_shifted(choose(even[2], up[2], down[2]), 1 - odd)
+    z2 = pack_z_shifted(choose(even[2], down[2], up[2]), odd)
+    z_deep = pack_z_shifted(choose(even[2], *z_faces), odd, 32, z2)
+    z_lines = pack_z_shifted(y_lines + x_lines, odd)
     y1, y2 = jnp.where(even[1], y_faces[1][0], y_faces[0][0]), jnp.where(even[1], y_faces[0][0], y_faces[1][0])
-    z1, z2 = jnp.where(even[2], z_faces[1][0], z_faces[0][0]), jnp.where(even[2], z_faces[0][0], z_faces[1][0])
     y_deep = jnp.where(even[1], y_faces[0][1], y_faces[1][1])
     y_lines = jnp.where(even[1], y_faces[0][2], y_faces[1][2])
-    z_deep = jnp.where(even[2], z_faces[0][1], z_faces[1][1])
-    z_lines = jnp.where(even[2], z_faces[0][2], z_faces[1][2])
     raw_ref[0:16] = y2
     raw_ref[16:24] = z2
     diag_ref[0:16] = y_lines

time: 48.7 us -> 48.6 us (level)
  the two profiles are of different devices: /device:TPU:8 before, /device:TPU:40 now
where the time goes in v10:
time: 48.6 us; the launch traced here: 48.3 us
  starting transfers between devices  37.5 us (77%)
  waiting for transfers between devices  6.62 us (14%)
  Pallas kernels  3.39 us (7%)
  between operations  0.77 us (2%)
    ppermute x1, starting transfers between devices, first_exchange(): near_in = lax.ppermute(near, AXES, grid_pairs(near_move))  11.3 us
    ppermute x1, starting transfers between devices, first_exchange(): back_in = lax.ppermute(back, 'gx', axis_pairs('gx', 0))  6.2 us
    ppermute x1, starting transfers between devices, second_exchange(): lax.ppermute(z1, 'gz', axis_pairs('gz', 0))  5.06 us
    ppermute x1, starting transfers between devices, first_exchange(): y_in = lax.ppermute(y, AXES, grid_pairs(second_y_move))  3.83 us
    ppermute x1, waiting for transfers between devices, second_exchange(): lax.ppermute(y1, 'gy', axis_pairs('gy', 0))  3.62 us
    pallas_call x5, Pallas kernels, call(): pl.pallas_call(kernel, out_shape=[jax.ShapeDtypeStruct(s, jnp.float32) fo...  3.39 us
    ppermute x1, starting transfers between devices, first_exchange(): above = lax.ppermute(down, 'gx', to_down)  2.94 us
    ppermute x1, starting transfers between devices, second_exchange(): lax.ppermute(down, 'gx', to_down)  2.61 us
  transfers between devices with their start and end apart: 12, of which 3 were waited for; matrix products, arithmetic and copies ran while one was open for 0% of the time, Pallas kernels for 1%

profile of v10, /device:TPU:40, one launch (start us, length us, event | category | flops | bytes accessed | tf_op | source)
XLA Modules:
  0.0 48.3 jit_solution(9540361403892306925)
XLA Ops:
  0.6 1.7 %shard_map.67 = (f32[2,7,4,16,128]{4,3,2,1,0:T(8,128)S(1)}, f32[2,7,4,16,128]{4,3,2,1,0:T(8,128)S(1)}, f32[4,16,128]{2,1,0:T(8,128)S(1)}, f32[2,4,16,128]{3,2,1,...) custom-call(f32[2,7,4,16,128]{4,3,2,1,0:T(8,128)} %f_hbm.1, ...), custom_call_target="tpu_custom_call" | custom-call | tf_op jit(solution)/shard_map/pallas_call | solution.py:444
  2.3 0.0 collective-permute-start
  2.3 2.9 %collective-permute-start.1 = (f32[160,128]{1,0:T(8,128)S(1)}, f32[160,128]{1,0:T(8,128)S(1)}, u32[]{:S(2)}, u32[]{:S(2)}) collective-permute-start(f32[160,128]{1,0:T(8,128)S(1)} %get-tuple-element.30), channel_id=1, source_target_pairs={{64,0},{128,64},{192,128},{256,192},{320,256},{384,320},{448,384},... | collective-permute-start | bytes 245768 | tf_op jit(solution)/shard_map/ppermute | solution.py:510
  5.3 2.1 %collective-permute-done.below_ref = f32[160,128]{1,0:T(8,128)S(1)} collective-permute-done((f32[160,128]{1,0:T(8,128)S(1)}, f32[160,128]{1,0:T(8,128)S(1)}, u32[]{:S(2)}, u32[]{:S(2)}) %collective-permute-start) | collective-permute-done | bytes 81952 | tf_op jit(solution)/shard_map/ppermute | solution.py:509
  7.4 0.0 collective-permute-done.1.above_ref
  7.4 3.8 %collective-permute-start.3 = (f32[160,128]{1,0:T(8,128)S(1)}, f32[160,128]{1,0:T(8,128)S(1)}, u32[]{:S(2)}, u32[]{:S(2)}) collective-permute-start(f32[160,128]{1,0:T(8,128)S(1)} %get-tuple-element.34), channel_id=1, source_target_pairs={{0,56},{1,57},{2,58},{3,59},{4,60},{5,61},{6,62},{7,63},{8,16},{9,... | collective-permute-start | bytes 245768 | tf_op jit(solution)/shard_map/ppermute | solution.py:513
  11.2 0.7 %collective-permute-start.2 = (f32[48,128]{1,0:T(8,128)S(1)}, f32[48,128]{1,0:T(8,128)S(1)}, u32[]{:S(2)}, u32[]{:S(2)}) collective-permute-start(f32[48,128]{1,0:T(8,128)S(1)} %get-tuple-element.33), channel_id=1, source_target_pairs={{64,71},{65,66},{66,65},{67,68},{68,67},{69,70},{70,69},{71,64},{7... | collective-permute-start | bytes 73736 | tf_op jit(solution)/shard_map/ppermute | solution.py:512
  11.9 11.3 %collective-permute-start.4 = (f32[32,128]{1,0:T(8,128)S(1)}, f32[32,128]{1,0:T(8,128)S(1)}, u32[]{:S(2)}, u32[]{:S(2)}) collective-permute-start(f32[32,128]{1,0:T(8,128)S(1)} %get-tuple-element.35), channel_id=1, source_target_pairs={{0,8},{1,9},{2,10},{3,11},{4,12},{5,13},{6,14},{7,15},{8,0},{9,1},... | collective-permute-start | bytes 49160 | tf_op jit(solution)/shard_map/ppermute | solution.py:515
  23.3 1.9 %collective-permute-start.6 = (f32[152,128]{1,0:T(8,128)S(1)}, f32[152,128]{1,0:T(8,128)S(1)}, u32[]{:S(2)}, u32[]{:S(2)}) collective-permute-start(f32[152,128]{1,0:T(8,128)S(1)} %get-tuple-element.41), channel_id=1, source_target_pairs={{0,63},{3,60},{4,59},{7,56},{9,18},{10,17},{13,22},{14,21},{17,10}... | collective-permute-start | bytes 233480 | tf_op jit(solution)/shard_map/ppermute | solution.py:514
  25.2 0.0 collective-permute-done.4.near_ref
  25.2 0.0 collective-permute-done.2.z_ref
  25.2 0.0 collective-permute-done.3.y_ref
  25.3 6.2 %collective-permute-start.5 = (f32[96,128]{1,0:T(8,128)S(1)}, f32[96,128]{1,0:T(8,128)S(1)}, u32[]{:S(2)}, u32[]{:S(2)}) collective-permute-start(f32[96,128]{1,0:T(8,128)S(1)} %shard_map.69), channel_id=1, source_target_pairs={{0,64},{64,0},{128,192},{192,128},{256,320},{320,256},{384,448},{4... | collective-permute-start | bytes 147464 | tf_op jit(solution)/shard_map/ppermute | solution.py:517
  31.5 0.9 %collective-permute-done.5.back_ref = f32[96,128]{1,0:T(8,128)S(1)} collective-permute-done((f32[96,128]{1,0:T(8,128)S(1)}, f32[96,128]{1,0:T(8,128)S(1)}, u32[]{:S(2)}, u32[]{:S(2)}) %collective-permute-start.5) | collective-permute-done | bytes 49184 | tf_op jit(solution)/shard_map/ppermute | solution.py:517
  32.3 0.4 shard_map.70
  32.7 0.4 collective-permute-start.7
  33.1 2.6 %collective-permute-start.8 = (f32[48,128]{1,0:T(8,128)S(1)}, f32[48,128]{1,0:T(8,128)S(1)}, u32[]{:S(2)}, u32[]{:S(2)}) collective-permute-start(f32[48,128]{1,0:T(8,128)S(1)} %get-tuple-element.43), channel_id=1, source_target_pairs={{64,0},{128,64},{192,128},{256,192},{320,256},{384,320},{448,384},... | collective-permute-start | bytes 73736 | tf_op jit(solution)/shard_map/ppermute | solution.py:525
  35.7 0.7 %collective-permute-start.11 = (f32[48,128]{1,0:T(8,128)S(1)}, f32[48,128]{1,0:T(8,128)S(1)}, u32[]{:S(2)}, u32[]{:S(2)}) collective-permute-start(f32[48,128]{1,0:T(8,128)S(1)} %get-tuple-element.46), channel_id=1, source_target_pairs={{1,2},{2,1},{5,6},{6,5},{8,16},{11,19},{12,20},{15,23},{16,8},{19,... | collective-permute-start | bytes 73736 | tf_op jit(solution)/shard_map/ppermute | solution.py:528
  36.4 5.1 %collective-permute-start.10 = (f32[24,128]{1,0:T(8,128)S(1)}, f32[24,128]{1,0:T(8,128)S(1)}, u32[]{:S(2)}, u32[]{:S(2)}) collective-permute-start(f32[24,128]{1,0:T(8,128)S(1)} %get-tuple-element.45), channel_id=1, source_target_pairs={{0,1},{1,0},{2,3},{3,2},{4,5},{5,4},{6,7},{7,6},{8,9},{9,8},{10,11... | collective-permute-start | bytes 36872 | tf_op jit(solution)/shard_map/ppermute | solution.py:527
  41.4 0.0 collective-permute-done.6.diag_ref
  41.4 1.9 %collective-permute-start.9 = (f32[16,128]{1,0:T(8,128)S(1)}, f32[16,128]{1,0:T(8,128)S(1)}, u32[]{:S(2)}, u32[]{:S(2)}) collective-permute-start(f32[16,128]{1,0:T(8,128)S(1)} %get-tuple-element.44), channel_id=1, source_target_pairs={{0,8},{8,0},{16,24},{24,16},{32,40},{40,32},{48,56},{56,48},{1,9},... | collective-permute-start | bytes 24584 | tf_op jit(solution)/shard_map/ppermute | solution.py:526
  43.4 3.6 %collective-permute-done.9.y1_ref = f32[16,128]{1,0:T(8,128)S(1)} collective-permute-done((f32[16,128]{1,0:T(8,128)S(1)}, f32[16,128]{1,0:T(8,128)S(1)}, u32[]{:S(2)}, u32[]{:S(2)}) %collective-permute-start.9) | collective-permute-done | bytes 8224 | tf_op jit(solution)/shard_map/ppermute | solution.py:526
  47.0 0.0 collective-permute-done.10.z1_ref
  47.0 0.0 collective-permute-done.7.below_ref
  47.0 0.0 collective-permute-done.8.above_ref
  47.0 0.0 collective-permute-done.11.relay_ref
  47.0 1.3 %shard_map.71 = (f32[2,7,4,16,128]{4,3,2,1,0:T(8,128)}, f32[4,16,128]{2,1,0:T(8,128)}, f32[2,4,16,128]{3,2,1,0:T(8,128)}) custom-call(f32[2,7,4,16,128]{4,3,2,1,0:T(8,128)S(1)} %get-tuple-element.25.f_ref, f32[4,16,128]{2,1,0:T(8,128)S(1)} %get-tuple-element.26.r_ref, f32[2,4,16,128]{3,2,1,0:T(8,128)S(1)} %get-tuple-element.27.t_ref, ...), custom_call_target="tpu_custom_call" | custom-call | tf_op jit(solution)/shard_map/pallas_call | solution.py:444
  (2 shorter events, 0.0 us)
Async XLA Ops:
  2.3 5.1 %collective-permute-start = (f32[160,128]{1,0:T(8,128)S(1)}, f32[160,128]{1,0:T(8,128)S(1)}, u32[]{:S(2)}, u32[]{:S(2)}) collective-permute-start(f32[160,128]{1,0:T(8,128)S(1)} %get-tuple-element.29), channel_id=1, source_target_pairs={{0,64},{64,128},{128,192},{192,256},{256,320},{320,384},{384,448},... | collective-permute-start | bytes 245768 | tf_op jit(solution)/shard_map/ppermute | solution.py:509
  2.3 5.1 %collective-permute-start.1 = (f32[160,128]{1,0:T(8,128)S(1)}, f32[160,128]{1,0:T(8,128)S(1)}, u32[]{:S(2)}, u32[]{:S(2)}) collective-permute-start(f32[160,128]{1,0:T(8,128)S(1)} %get-tuple-element.30), channel_id=1, source_target_pairs={{64,0},{128,64},{192,128},{256,192},{320,256},{384,320},{448,384},... | collective-permute-start | bytes 245768 | tf_op jit(solution)/shard_map/ppermute | solution.py:510
  7.4 17.8 %collective-permute-start.3 = (f32[160,128]{1,0:T(8,128)S(1)}, f32[160,128]{1,0:T(8,128)S(1)}, u32[]{:S(2)}, u32[]{:S(2)}) collective-permute-start(f32[160,128]{1,0:T(8,128)S(1)} %get-tuple-element.34), channel_id=1, source_target_pairs={{0,56},{1,57},{2,58},{3,59},{4,60},{5,61},{6,62},{7,63},{8,16},{9,... | collective-permute-start | bytes 245768 | tf_op jit(solution)/shard_map/ppermute | solution.py:513
  11.2 14.0 %collective-permute-start.2 = (f32[48,128]{1,0:T(8,128)S(1)}, f32[48,128]{1,0:T(8,128)S(1)}, u32[]{:S(2)}, u32[]{:S(2)}) collective-permute-start(f32[48,128]{1,0:T(8,128)S(1)} %get-tuple-element.33), channel_id=1, source_target_pairs={{64,71},{65,66},{66,65},{67,68},{68,67},{69,70},{70,69},{71,64},{7... | collective-permute-start | bytes 73736 | tf_op jit(solution)/shard_map/ppermute | solution.py:512
  11.9 13.3 %collective-permute-start.4 = (f32[32,128]{1,0:T(8,128)S(1)}, f32[32,128]{1,0:T(8,128)S(1)}, u32[]{:S(2)}, u32[]{:S(2)}) collective-permute-start(f32[32,128]{1,0:T(8,128)S(1)} %get-tuple-element.35), channel_id=1, source_target_pairs={{0,8},{1,9},{2,10},{3,11},{4,12},{5,13},{6,14},{7,15},{8,0},{9,1},... | collective-permute-start | bytes 49160 | tf_op jit(solution)/shard_map/ppermute | solution.py:515
  23.3 18.2 %collective-permute-start.6 = (f32[152,128]{1,0:T(8,128)S(1)}, f32[152,128]{1,0:T(8,128)S(1)}, u32[]{:S(2)}, u32[]{:S(2)}) collective-permute-start(f32[152,128]{1,0:T(8,128)S(1)} %get-tuple-element.41), channel_id=1, source_target_pairs={{0,63},{3,60},{4,59},{7,56},{9,18},{10,17},{13,22},{14,21},{17,10}... | collective-permute-start | bytes 233480 | tf_op jit(solution)/shard_map/ppermute | solution.py:514
  25.3 7.1 %collective-permute-start.5 = (f32[96,128]{1,0:T(8,128)S(1)}, f32[96,128]{1,0:T(8,128)S(1)}, u32[]{:S(2)}, u32[]{:S(2)}) collective-permute-start(f32[96,128]{1,0:T(8,128)S(1)} %shard_map.69), channel_id=1, source_target_pairs={{0,64},{64,0},{128,192},{192,128},{256,320},{320,256},{384,448},{4... | collective-permute-start | bytes 147464 | tf_op jit(solution)/shard_map/ppermute | solution.py:517
  32.7 14.3 %collective-permute-start.7 = (f32[48,128]{1,0:T(8,128)S(1)}, f32[48,128]{1,0:T(8,128)S(1)}, u32[]{:S(2)}, u32[]{:S(2)}) collective-permute-start(f32[48,128]{1,0:T(8,128)S(1)} %get-tuple-element.42), channel_id=1, source_target_pairs={{0,64},{64,128},{128,192},{192,256},{256,320},{320,384},{384,448},... | collective-permute-start | bytes 73736 | tf_op jit(solution)/shard_map/ppermute | solution.py:524
  33.1 13.9 %collective-permute-start.8 = (f32[48,128]{1,0:T(8,128)S(1)}, f32[48,128]{1,0:T(8,128)S(1)}, u32[]{:S(2)}, u32[]{:S(2)}) collective-permute-start(f32[48,128]{1,0:T(8,128)S(1)} %get-tuple-element.43), channel_id=1, source_target_pairs={{64,0},{128,64},{192,128},{256,192},{320,256},{384,320},{448,384},... | collective-permute-start | bytes 73736 | tf_op jit(solution)/shard_map/ppermute | solution.py:525
  35.7 11.3 %collective-permute-start.11 = (f32[48,128]{1,0:T(8,128)S(1)}, f32[48,128]{1,0:T(8,128)S(1)}, u32[]{:S(2)}, u32[]{:S(2)}) collective-permute-start(f32[48,128]{1,0:T(8,128)S(1)} %get-tuple-element.46), channel_id=1, source_target_pairs={{1,2},{2,1},{5,6},{6,5},{8,16},{11,19},{12,20},{15,23},{16,8},{19,... | collective-permute-start | bytes 73736 | tf_op jit(solution)/shard_map/ppermute | solution.py:528
  36.4 10.6 %collective-permute-start.10 = (f32[24,128]{1,0:T(8,128)S(1)}, f32[24,128]{1,0:T(8,128)S(1)}, u32[]{:S(2)}, u32[]{:S(2)}) collective-permute-start(f32[24,128]{1,0:T(8,128)S(1)} %get-tuple-element.45), channel_id=1, source_target_pairs={{0,1},{1,0},{2,3},{3,2},{4,5},{5,4},{6,7},{7,6},{8,9},{9,8},{10,11... | collective-permute-start | bytes 36872 | tf_op jit(solution)/shard_map/ppermute | solution.py:527
  41.4 5.5 %collective-permute-start.9 = (f32[16,128]{1,0:T(8,128)S(1)}, f32[16,128]{1,0:T(8,128)S(1)}, u32[]{:S(2)}, u32[]{:S(2)}) collective-permute-start(f32[16,128]{1,0:T(8,128)S(1)} %get-tuple-element.44), channel_id=1, source_target_pairs={{0,8},{8,0},{16,24},{24,16},{32,40},{40,32},{48,56},{56,48},{1,9},... | collective-permute-start | bytes 24584 | tf_op jit(solution)/shard_map/ppermute | solution.py:526
